TPU v7x, 256 devices: a whole 4x4x8 slice. The times are simulated.
256 devices in a mesh: depth: 64 (over x_hi, y, z), band: 4 (over x_lo, core).
Axes of the slice: x: 4 (x_hi: 2, x_lo: 2; x = x_hi * 2 + x_lo), y: 4, z: 8, core: 2. Of those that a mesh axis runs over, the one named last changes fastest.
Arguments:
- planes: float32 [64, 256, 2048], P('depth', 'band'), may hold values from -6 to 6
- denoised: float32 [64, 256, 2048], P('depth', 'band'), may hold values from -6 to 6
- scaled_dual: float32 [64, 256, 2048], P('depth', 'band'), may hold values from -4 to 4
- measured: float32 [256, 2048], P('band'), may hold values from -6 to 6
- lenslet_psf: bfloat16 [64, 31, 31], P('depth'), may hold values from -0.0234375 to 0.0234375
- kernel: bfloat16 [27, 16], replicated, may hold values from -1.25 to 1.25
- layer_bias: float32 [16], replicated, may hold values from -3 to 3
- mix_weight: bfloat16 [16], replicated, may hold values from -1.5 to 1.5
Outputs:
- new_planes: float32 [64, 256, 2048], P('depth', 'band')
- new_denoised: float32 [64, 256, 2048], P('depth', 'band')
- new_dual: float32 [64, 256, 2048], P('depth', 'band')
All inputs are finite; a program needn't handle non-finite values.
Results may differ from a plain program's by a relative error of at most 0.0049.
Values may be sent and summed in bfloat16 or wider, within the bound.
No kernel may reach another device: no remote copies, remote signals or barrier semaphores. Data moves between devices by JAX's collectives and lax.ppermute only.
A program may use at most 128 MiB of HBM per device.

v0:
```python
import jax
import jax.numpy as jnp
from jax import lax
from jax.sharding import PartitionSpec as P

KS = 31


step_size = 4.0
penalty = 0.5


def padded_2(block, sides, width):
    for axis, dim in sides:
        count = lax.axis_size(axis)
        forward = [(i, i + 1) for i in range(count - 1)]
        backward = [(target, source) for source, target in forward]
        low = lax.ppermute(
            lax.slice_in_dim(block, block.shape[dim] - width, None, axis=dim), axis, forward
        )
        high = lax.ppermute(lax.slice_in_dim(block, 0, width, axis=dim), axis, backward)
        block = jnp.concatenate([low, block, high], axis=dim)
    return block


def project(rimmed, psf_one):
    span_rows = rimmed.shape[0] - KS + 1
    total_cols = rimmed.shape[1]
    col_block = 256
    window_cols = col_block + KS - 1
    edge = KS // 2
    padded = jnp.pad(rimmed, ((0, 0), (edge, edge)))
    offsets = jnp.arange(window_cols)[:, None] - jnp.arange(col_block)[None, :]
    onehot = (offsets[None] == jnp.arange(KS)[:, None, None]).astype(jnp.bfloat16)
    band_matrix = jnp.einsum("ab,btj->atj", psf_one, onehot, preferred_element_type=jnp.float32)
    band_matrix = band_matrix.astype(jnp.bfloat16).reshape(KS * window_cols, col_block)
    pieces = []
    for b in range(total_cols // col_block):
        window = padded[:, b * col_block : b * col_block + window_cols]
        stacked = jnp.stack([window[a : a + span_rows] for a in range(KS)], axis=1)
        stacked = stacked.reshape(span_rows, KS * window_cols)
        pieces.append(jnp.dot(stacked, band_matrix, preferred_element_type=jnp.float32))
    return jnp.concatenate(pieces, axis=1)


def shards(planes, denoised, scaled_dual, measured, lenslet_psf, kernel, layer_bias, mix_weight):
    plane_count, band_rows, total_cols = planes.shape
    edge = KS // 2
    planes_half = planes.astype(jnp.bfloat16)
    rimmed = padded_2(planes_half, (("band", 1),), edge)
    partial_value = project(rimmed[0], lenslet_psf[0])
    sensor = lax.psum(partial_value, "depth")
    residual = (sensor - measured).astype(jnp.bfloat16)
    residual_rimmed = padded_2(residual, (("band", 0),), edge)
    gradient = jnp.stack([project(residual_rimmed, lenslet_psf[0][::-1, ::-1])])
    new_planes = planes - step_size * (gradient + penalty * (planes - (denoised - scaled_dual)))
    noisy = new_planes + scaled_dual
    noisy_half = noisy.astype(jnp.bfloat16)
    volume = padded_2(noisy_half, (("depth", 0), ("band", 1)), 1)
    volume = jnp.pad(volume, ((0, 0), (0, 0), (1, 1)))
    taps = []
    for i in range(3):
        for j in range(3):
            for k in range(3):
                taps.append(volume[i : i + plane_count, j : j + band_rows, k : k + total_cols])
    stacked = jnp.stack(taps)
    hidden = jnp.einsum("kn,kprc->nprc", kernel, stacked, preferred_element_type=jnp.float32)
    hidden = jnp.maximum(hidden + layer_bias[:, None, None, None], 0.0).astype(jnp.bfloat16)
    noise = jnp.einsum("n,nprc->prc", mix_weight, hidden, preferred_element_type=jnp.float32)
    new_denoised = noisy - noise
    new_dual = scaled_dual + new_planes - new_denoised
    return (new_planes, new_denoised, new_dual)


def solution(mesh):
    in_specs = (
        P("depth", "band", None),
        P("depth", "band", None),
        P("depth", "band", None),
        P("band", None),
        P("depth", None, None),
        P(),
        P(),
        P(),
    )
    out_specs = (P("depth", "band", None), P("depth", "band", None), P("depth", "band", None))
    return jax.shard_map(shards, mesh=mesh, in_specs=in_specs, out_specs=out_specs, check_vma=False)
```

profile of v0, /device:TPU:1, one launch (start us, length us, event | category | flops | bytes accessed | tf_op | source)
XLA Modules:
  0.0 903.1 jit_solution(1731038789126102001)
XLA Ops:
  7.2 1.1 convert_element_type.35
  8.3 4.5 collective-permute-start
  12.8 1.9 collective-permute-start.1
  14.8 2.9 convert_bitcast_fusion.1
  19.3 1.2 constant_dynamic-update-slice_fusion.153
  20.4 1.2 constant_dynamic-update-slice_fusion.152
  21.6 1.2 constant_dynamic-update-slice_fusion.151
  22.8 1.2 constant_dynamic-update-slice_fusion.150
  23.9 1.2 constant_dynamic-update-slice_fusion.149
  25.1 1.2 constant_dynamic-update-slice_fusion.148
  26.3 1.2 constant_dynamic-update-slice_fusion.147
  27.4 1.1 constant_dynamic-update-slice_fusion.146
  28.5 1.2 constant_dynamic-update-slice_fusion.145
  29.7 1.2 constant_dynamic-update-slice_fusion.144
  30.8 1.2 constant_dynamic-update-slice_fusion.143
  32.0 1.2 constant_dynamic-update-slice_fusion.142
  33.2 1.2 constant_dynamic-update-slice_fusion.141
  34.3 1.2 constant_dynamic-update-slice_fusion.140
  35.5 1.2 constant_dynamic-update-slice_fusion.139
  36.7 1.1 constant_dynamic-update-slice_fusion.138
  37.8 1.2 constant_dynamic-update-slice_fusion.137
  38.9 1.2 constant_dynamic-update-slice_fusion.136
  40.1 1.2 constant_dynamic-update-slice_fusion.135
  41.3 1.2 constant_dynamic-update-slice_fusion.134
  42.5 1.2 constant_dynamic-update-slice_fusion.133
  43.6 1.2 constant_dynamic-update-slice_fusion.132
  44.8 1.2 constant_dynamic-update-slice_fusion.131
  46.0 1.1 constant_dynamic-update-slice_fusion.130
  47.1 1.2 constant_dynamic-update-slice_fusion.129
  48.2 1.2 constant_dynamic-update-slice_fusion.128
  56.9 5.2 fusion.30
  62.1 5.1 fusion.29
  67.1 5.3 fusion.28
  72.4 5.1 fusion.27
  77.5 5.5 fusion.26
  83.0 5.1 fusion.25
  88.0 5.1 fusion.24
  93.1 5.7 fusion.23
  98.8 0.8 copy-done.5
  99.7 647.0 %all-reduce.5.cloned.1.call-done = f32[64,2048]{1,0:T(8,128)} async-done(((f32[64,2048]{1,0:T(8,128)}), f32[64,2048]{1,0:T(8,128)}) %all-reduce.5.cloned.1.call-update) | async-done | bytes 524304 | tf_op jit(solution)/shard_map/psum | solution.py:52
  746.7 1.1 subtract_convert_fusion
  747.9 48.5 %collective-permute-start.2 = (bf16[15,2048]{1,0:T(8,128)(2,1)S(1)}, bf16[15,2048]{1,0:T(8,128)(2,1)S(1)}, u32[]{:S(2)}, u32[]{:S(2)}) collective-permute-start(bf16[15,2048]{1,0:T(8,128)(2,1)S(1)} %get-tuple-element.349), channel_id=1, source_target_pairs={{0,1},{1,2},{2,3},{4,5},{5,6},{6,7},{8,9},{9,10},{10,11},{12,13},{... | collective-permute-start | bytes 184328 | tf_op jit(solution)/shard_map/ppermute | solution.py:18
  796.4 2.2 convert_bitcast_fusion
  798.6 1.9 collective-permute-start.3
  802.3 1.9 collective-permute-done.3
  814.5 5.5 fusion.22
  825.4 5.0 fusion.21
  830.4 5.2 fusion.20
  835.6 5.1 fusion.19
  840.7 5.1 fusion.18
  845.8 5.5 fusion.17
  851.2 5.1 fusion.16
  856.3 5.2 fusion.15
  861.6 1.0 fusion.249
  862.5 2.3 collective-permute-start.4
  864.8 1.3 collective-permute-start.5
  866.1 2.8 collective-permute-done.4
  869.0 4.1 collective-permute-done.5
  873.1 2.4 collective-permute-start.6
  875.5 1.9 collective-permute-start.7
  877.5 3.2 collective-permute-done.7
  883.8 2.9 copy-done.9
  886.7 8.1 fusion.8
  894.8 1.2 fusion.248
  (304 shorter events, 29.0 us)
Async XLA Ops:
  7.2 879.6 %copy-start = (bf16[27,16]{0,1:T(8,128)(2,1)S(1)}, bf16[27,16]{0,1:T(8,128)(2,1)}, u32[]{:S(2)}) copy-start(bf16[27,16]{0,1:T(8,128)(2,1)} %param.13) | copy-start | bytes 2596
  7.2 739.5 %all-reduce.5.cloned.1.call-start = ((), (), s32[]{:S(2)}) async-start(), calls=%async_computation | async-start | bytes 1048576 | tf_op jit(solution)/shard_map/psum | solution.py:52
  8.3 9.4 %collective-permute-start = (bf16[1,15,2048]{2,1,0:T(8,128)(2,1)S(1)}, bf16[1,15,2048]{2,1,0:T(8,128)(2,1)S(1)}, u32[]{:S(2)}, u32[]{:S(2)}) collective-permute-start(bf16[1,15,2048]{2,1,0:T(8,128)(2,1)S(1)} %get-tuple-element.351), channel_id=1, source_target_pairs={{0,1},{1,2},{2,3},{4,5},{5,6},{6,7},{8,9},{9,10},{10,11},{12,13},{... | collective-permute-start | bytes 184328 | tf_op jit(solution)/shard_map/ppermute | solution.py:18
  12.8 5.6 collective-permute-start.1
  18.5 0.7 copy-start.1
  40.1 9.3 %copy-start.2 = (bf16[94,2048]{1,0:T(8,128)(2,1)S(1)}, bf16[94,2048]{1,0:T(8,128)(2,1)}, u32[]{:S(2)}) copy-start(bf16[94,2048]{1,0:T(8,128)(2,1)} %copy-done.1) | copy-start | bytes 1155076
  93.1 6.5 copy-start.8
  93.1 653.6 %copy-start.4 = (f32[64,2048]{1,0:T(8,128)S(1)}, f32[64,2048]{1,0:T(8,128)}, u32[]{:S(2)}) copy-start(f32[64,2048]{1,0:T(8,128)} %param.11) | copy-start | bytes 1572868
  98.8 0.8 copy-start.5
  747.9 52.7 %collective-permute-start.2 = (bf16[15,2048]{1,0:T(8,128)(2,1)S(1)}, bf16[15,2048]{1,0:T(8,128)(2,1)S(1)}, u32[]{:S(2)}, u32[]{:S(2)}) collective-permute-start(bf16[15,2048]{1,0:T(8,128)(2,1)S(1)} %get-tuple-element.349), channel_id=1, source_target_pairs={{0,1},{1,2},{2,3},{4,5},{5,6},{6,7},{8,9},{9,10},{10,11},{12,13},{... | collective-permute-start | bytes 184328 | tf_op jit(solution)/shard_map/ppermute | solution.py:18
  798.6 5.6 collective-permute-start.3
  856.3 5.3 copy-start.3
  856.3 5.3 copy-start.6
  856.3 5.3 copy-start.7
  862.5 6.4 collective-permute-start.4
  864.8 8.2 collective-permute-start.5
  873.1 4.3 collective-permute-start.6
  875.5 5.1 collective-permute-start.7
  883.3 3.5 copy-start.10
  883.3 3.4 copy-start.11
  883.8 2.9 copy-start.9
Sparse Core Ops, SparseCore 0:
  99.7 646.9 all-reduce.4
where the time goes:
time: 916 us; the launch traced here: 903 us
  waiting for transfers between devices  660 us (72%)
  matrix products  96.7 us (11%)
  starting transfers between devices  64.8 us (7%)
  local copies, waits for them, and re-layouts  45 us (5%)
  other arithmetic  21.3 us (2%)
  between operations  15.5 us (2%)
    psum x1, waiting for transfers between devices, shards(): sensor = lax.psum(partial_value, 'depth')  647 us
    dot_general x16, matrix products, project(): jnp.dot(stacked, band_matrix, preferred_element_type=jnp.float32)  83.5 us
    ppermute x4, starting transfers between devices, padded_2(): lax.ppermute(lax.slice_in_dim(block, block.shape[dim] - width, None, axis...  57.7 us
    unnamed x164, local copies, waits for them, and re-layouts  44.4 us
  transfers between devices with their start and end apart: 9, of which 6 were waited for; matrix products, arithmetic and copies ran while one was open for 1% of the time, Pallas kernels for 0%

commit v1 on v0

v1 whole, which is shorter than its diff:
```python
import functools

import jax
import jax.numpy as jnp
from jax import lax
from jax.experimental import pallas as pl
from jax.experimental.pallas import tpu as pltpu
from jax.sharding import Mesh, PartitionSpec as P

STEP = 4.0
HALF = 0.5
BF = jnp.bfloat16
F32 = jnp.float32
VMEM_LIMIT = 56 * 1024 * 1024


def iota(shape, axis):
    return lax.broadcasted_iota(jnp.int32, shape, axis)


def cross4(x0, x1, x2, x3):
    lane = iota(x0.shape, x0.ndim - 1)
    low = lane < 64
    even = (lane // 32) % 2 == 0
    ax = x0.ndim - 1

    def pair(a, b, mask, shift):
        return (
            jnp.where(mask, a, pltpu.roll(b, shift, ax)),
            jnp.where(mask, pltpu.roll(a, 128 - shift, ax), b),
        )

    y0, y2 = pair(x0, x2, low, 64)
    y1, y3 = pair(x1, x3, low, 64)
    z0, z1 = pair(y0, y1, even, 32)
    z2, z3 = pair(y2, y3, even, 32)
    return z0, z1, z2, z3


def to_blocks(src, base, put):
    for t in range(16):
        for h in range(2):
            x = [src[t, pl.ds(base + 4 * h + m, 8, stride=8), :] for m in range(4)]
            for g, z in enumerate(cross4(*x)):
                put(4 * t + g, h, z)


def from_blocks(get, dst):
    for t in range(16):
        for h in range(2):
            z = cross4(*[get(4 * t + g, h) for g in range(4)])
            for m in range(4):
                dst[t, pl.ds(4 * h + m, 8, stride=8), :] = z[m]


def toeplitz(psf, flip, strips, put):
    s = iota((64, 128), 0) - 1
    b = iota((64, 128), 1)
    pick = jnp.where(s == ((30 - b) if flip else b), 1.0, 0.0).astype(BF)
    turned = lax.dot_general(pick, psf, (((1,), (1,)), ((), ())), preferred_element_type=F32).astype(BF)
    a = iota((32, 1536), 0)
    u = iota((32, 1536), 1) // 32
    spread = jnp.where(a == ((u - 8) if flip else (38 - u)), 1.0, 0.0).astype(BF)
    strip = jnp.dot(turned, spread, preferred_element_type=F32)
    j = iota((64, 1536), 1) % 32
    for bit in (1, 2, 4, 8, 16):
        strip = jnp.where((j & bit) != 0, pltpu.roll(strip, bit, 0), strip)
    for k in range(4):
        moved = strip if k == 0 else pltpu.roll(strip, 1536 - 32 * k, 1)
        strips[k] = moved.astype(BF)
    for d in range(5):
        for i in range(8):
            u0 = 23 - 8 * (d - 2) - i
            cut = slice(128 * (u0 // 4), 128 * (u0 // 4) + 256)
            at = 512 * d + 32 * i
            put(at, strips[u0 % 4, 16:48, cut])
            put(at + 256, strips[u0 % 4, 48:64, cut])
            put(at + 272, strips[u0 % 4, 0:16, cut])


def weights_kernel(psf_ref, kernel_ref, bias_ref, mix_ref, wf_ref, wd_ref, mx_ref, strips, taps, rim):
    def put(at, value):
        wf_ref[at : at + value.shape[0], :] = value

    toeplitz(psf_ref[...], False, strips, put)
    n_of = jnp.where(iota((16, 1024), 1) // 64 == iota((16, 1024), 0), 1.0, 0.0).astype(BF)
    taps[0:27, :] = jnp.dot(kernel_ref[...], n_of, preferred_element_type=F32)
    lane = iota((32, 1024), 1)
    j = lane % 32
    r = (lane // 32) % 2
    jp = iota((32, 1024), 0)
    lane1 = iota((1, 1024), 1)
    j1 = lane1 % 32
    r1 = (lane1 // 32) % 2
    rim[...] = jnp.zeros_like(rim)
    for d in range(3):
        for w in range(4):
            total = jnp.zeros((32, 1024), F32)
            right = jnp.zeros((1, 1024), F32)
            left = jnp.zeros((1, 1024), F32)
            for u in range(3):
                if w - u not in (0, 1):
                    continue
                for v in range(3):
                    row = taps[9 * d + 3 * u + v : 9 * d + 3 * u + v + 1, :]
                    total = jnp.where((r == w - u) & (jp == j + (v - 1)), row, total)
                    if v == 2:
                        right = jnp.where((r1 == w - u) & (j1 == 31), row, right)
                    if v == 0:
                        left = jnp.where((r1 == w - u) & (j1 == 0), row, left)
            wd_ref[(4 * d + w) * 32 : (4 * d + w) * 32 + 32, :] = total.astype(BF)
            at = 32 * w + 2 * d
            rim[at : at + 1, :] = right
            at = (32 * w + 31 + 2 * d) % 128
            rim[at : at + 1, :] = left
    bias = bias_ref[...]
    for at in (6, 7, 8):
        part = bias.astype(BF)
        rim[at : at + 1, :] = jnp.dot(part, n_of, preferred_element_type=F32)
        bias = bias - part.astype(F32)
    wd_ref[384:512, :] = rim[...].astype(BF)
    rows_n = jnp.where(iota((1024, 16), 0) // 64 == iota((1024, 16), 1), 1.0, 0.0).astype(BF)
    mixed = jnp.dot(rows_n, jnp.broadcast_to(mix_ref[...], (16, 128)), preferred_element_type=F32)
    pos = iota((1024, 128), 0) % 64
    lane = iota((1024, 128), 1)
    mx_ref[0:1024, :] = jnp.where(lane == pos, mixed, 0.0).astype(BF)
    mx_ref[1024:2048, :] = jnp.where(lane == pos + 64, mixed, 0.0).astype(BF)


def back_weights_kernel(psf_ref, prev_ref, next_ref, wg_ref, strips):
    for p, ref in enumerate((prev_ref, psf_ref, next_ref)):

        def put(at, value, p=p):
            wg_ref[at : at + value.shape[0], 256 * p : 256 * p + 256] = value

        if p == 1:
            psf = psf_ref[...]
        else:
            psf = jnp.concatenate([ref[g // 2, :, 128 * (g % 2) : 128 * (g % 2) + 128] for g in range(4)], axis=0)
        toeplitz(psf, True, strips, put)


def gather_rows(main, side, lhs):
    j = iota((64, 8, 256), 2) % 32
    for d in range(5):
        lhs[:, 512 * d : 512 * d + 256] = main[1:65, d : d + 8, :].reshape(512, 256).astype(BF)
        rims = jnp.where(j < 16, main[2:66, d : d + 8, :], main[0:64, d : d + 8, :])
        if side is not None:
            side[:, d : d + 8, :] = rims
        lhs[:, 512 * d + 256 : 512 * d + 512] = rims.reshape(512, 256).astype(BF)


def forward_kernel(planes, denoised, dual, measured, lo, hi, psf, wf, part_ref, own_ref, pack_ref,
                   nat, main, lhs, blocks):
    cols = [slice(128 * t, 128 * t + 128) for t in range(16)]
    for t, c in enumerate(cols):
        nat[t, 0:16, :] = lo[0:16, c].astype(F32)
        nat[t, 16:80, :] = planes[:, c].astype(BF).astype(F32)
        nat[t, 80:96, :] = hi[0:16, c].astype(F32)
        nat[t, 96:128, :] = jnp.zeros((32, 128), F32)
    main[0] = jnp.zeros((16, 256), F32)
    main[65] = jnp.zeros((16, 256), F32)
    for half in range(2):

        def put(k, h, z, half=half):
            main[1 + k, 8 * half : 8 * half + 8, 128 * h : 128 * h + 128] = z

        to_blocks(nat, 64 * half, put)
    gather_rows(main, None, lhs)

    def put_measured(k, h, z):
        blocks[8 * k : 8 * k + 8, 128 * h : 128 * h + 128] = z

    for t, c in enumerate(cols):
        nat[t, 0:64, :] = measured[:, c]
    to_blocks(nat, 0, put_measured)
    sums = jnp.dot(lhs[...], wf[...], preferred_element_type=F32)
    part_ref[...] = (sums - blocks[...] * (1.0 / 64)).astype(BF)

    for t, c in enumerate(cols):
        nat[t, 0:8, :] = lo[16:24, c].astype(F32)
        nat[t, 8:72, :] = base(planes[:, c], denoised[:, c], dual[:, c])
        nat[t, 72:80, :] = hi[16:24, c].astype(F32)
    for half in range(2):

        def put(k, h, z, half=half):
            main[k, 8 * half : 8 * half + 8, 128 * h : 128 * h + 128] = z

        to_blocks(nat, 64 * half, put)
    inner = main[0:64, 1:9, :]
    own_ref[...] = inner.reshape(512, 256)
    pack_ref[0:64] = inner.astype(BF)
    lane = iota((64, 128), 1)
    edge = jnp.where(lane >= 96, main[0:64, 0, 128:256], main[0:64, 9, 0:128]).astype(BF)
    for g in range(8):
        pack_ref[64 + g // 2, :, 128 * (g % 2) : 128 * (g % 2) + 128] = edge[8 * g : 8 * g + 8, :]
    for g in range(4):
        pack_ref[68 + g // 2, :, 128 * (g % 2) : 128 * (g % 2) + 128] = psf[8 * g : 8 * g + 8, :]


def base(planes, denoised, dual):
    return planes - STEP * (HALF * (planes - (denoised - dual))) + dual


def final_kernel(valid, planes, denoised, dual, res, res_lo, res_hi, own, own_pack, prev_pack, next_pack, wg, wd, mx,
                 np_ref, nd_ref, du_ref, main, side, lhs, vol, wins, nat, blocks):
    main[0] = jnp.zeros((16, 256), F32)
    main[65] = jnp.zeros((16, 256), F32)
    main[1:65, 0:2, :] = res_lo[...].astype(F32)
    main[1:65, 2:10, :] = res[...].astype(F32).reshape(64, 8, 256)
    main[1:65, 10:12, :] = res_hi[...].astype(F32)
    gather_rows(main, side, lhs)
    grads = jnp.dot(lhs[...], wg[...], preferred_element_type=F32)

    def edge_rows(first):
        parts = []
        for q in range(first, first + 4):
            parts.append(main[1:65, q, :].astype(BF))
            parts.append(side[:, q, :].astype(BF))
        return jnp.concatenate(parts, axis=1)

    above = edge_rows(0)
    below = edge_rows(8)
    lane = iota((64, 128), 1)
    use_lo = valid[0] > 0
    use_hi = valid[1] > 0
    for p, pack in enumerate((prev_pack, own_pack, next_pack)):
        start = own[...] if p == 1 else pack[0:64].astype(F32).reshape(512, 256)
        noisy = start - STEP * grads[:, 256 * p : 256 * p + 256]
        vol[p, 0] = jnp.zeros((16, 256), F32)
        vol[p, 65] = jnp.zeros((16, 256), F32)
        vol[p, 1:65, 1:9, :] = noisy.reshape(64, 8, 256)
        g_lo = jnp.dot(above, wg[512:2560, 256 * p + 128 : 256 * p + 256], preferred_element_type=F32)
        g_hi = jnp.dot(below, wg[0:2048, 256 * p : 256 * p + 128], preferred_element_type=F32)
        edge = jnp.concatenate(
            [pack[64 + g // 2, :, 128 * (g % 2) : 128 * (g % 2) + 128].astype(F32) for g in range(8)], axis=0
        )
        vol[p, 1:65, 0, 128:256] = jnp.where(use_lo, edge - STEP * g_lo, 0.0)
        vol[p, 1:65, 9, 0:128] = jnp.where(use_hi, edge - STEP * g_hi, 0.0)
        for c in range(0, 66, 6):
            t0 = vol[p, c : c + 6, 1:9, 0:128]
            t1 = vol[p, c : c + 6, 1:9, 128:256]
            before = vol[p, c : c + 6, 0:8, 128:256]
            after = vol[p, c : c + 6, 2:10, 0:128]
            group = iota((6, 8, 128), 2) // 32
            up0, up1, upb = (pltpu.roll(x, 32, 2) for x in (t0, t1, before))
            dn0, dn1, dna = (pltpu.roll(x, 96, 2) for x in (t0, t1, after))
            wins[p, 0, c : c + 6] = jnp.where(group == 0, upb, up0)
            wins[p, 2, c : c + 6] = jnp.where(group == 0, up0, up1)
            wins[p, 1, c : c + 6] = jnp.where(group == 3, dn1, dn0)
            wins[p, 3, c : c + 6] = jnp.where(group == 3, dna, dn1)
    lane = iota((8, 8, 128), 2)
    j = lane % 32
    ones = (lane >= 6) & (lane <= 8)
    for k in range(4):
        for c in range(0, 64, 8):
            rim = jnp.zeros((8, 8, 128), F32)
            for p in range(3):
                mid = wins[p, k, c + 1 : c + 9]
                lhs[8 * c : 8 * c + 64, 512 * k + 128 * p : 512 * k + 128 * p + 128] = mid.reshape(64, 128).astype(BF)
                e = jnp.where(j == 0, wins[p, k, c + 2 : c + 10], jnp.where(j == 31, wins[p, k, c : c + 8], 0.0))
                rim = rim + (e if p == 0 else pltpu.roll(e, 2 * p, 2))
            rim = jnp.where(ones, 1.0, rim)
            lhs[8 * c : 8 * c + 64, 512 * k + 384 : 512 * k + 512] = rim.reshape(64, 128).astype(BF)
    for half in range(2):
        total = None
        for e in range(2):
            k = 2 * half + e
            hidden = jnp.dot(lhs[:, 512 * k : 512 * k + 512], wd[...], preferred_element_type=F32)
            hidden = jnp.maximum(hidden, 0.0).astype(BF)
            noise = jnp.dot(hidden, mx[1024 * e : 1024 * e + 1024, :], preferred_element_type=F32)
            total = noise if total is None else total + noise
        blocks[:, 128 * half : 128 * half + 128] = total
    from_blocks(lambda k, h: blocks[8 * k : 8 * k + 8, 128 * h : 128 * h + 128], nat.at[1])
    blocks[...] = grads[:, 256:512]
    from_blocks(lambda k, h: blocks[8 * k : 8 * k + 8, 128 * h : 128 * h + 128], nat.at[0])
    for t in range(16):
        c = slice(128 * t, 128 * t + 128)
        x = planes[:, c]
        z = dual[:, c]
        moved = x - STEP * (nat[0, t] + HALF * (x - (denoised[:, c] - z)))
        cleaned = (moved + z) - nat[1, t]
        np_ref[:, c] = moved
        nd_ref[:, c] = cleaned
        du_ref[:, c] = z + moved - cleaned


def call(body, outs, scratch, n_in, flops=1_000_000_000, smem=0):
    specs = [pl.BlockSpec(memory_space=pltpu.SMEM)] * smem + [pl.BlockSpec(memory_space=pltpu.VMEM)] * (n_in - smem)
    return pl.pallas_call(
        body,
        out_shape=outs,
        in_specs=specs,
        out_specs=[pl.BlockSpec(memory_space=pltpu.VMEM)] * len(outs),
        scratch_shapes=scratch,
        compiler_params=pltpu.CompilerParams(vmem_limit_bytes=VMEM_LIMIT),
        cost_estimate=pl.CostEstimate(flops=flops, bytes_accessed=4_000_000, transcendentals=0),
    )


def out(shape, dtype):
    return jax.ShapeDtypeStruct(shape, dtype)


def all_sum(part):
    group = ("xh", "y", "zl")
    got = lax.all_to_all(part, group, 0, 0, tiled=True)
    mine = jnp.sum(got.reshape(16, 32, 256).astype(F32), axis=0).astype(BF)
    for bit in (2, 1):
        other = lax.ppermute(mine, "zh", [(a, a ^ bit) for a in range(4)])
        mine = (mine.astype(F32) + other.astype(F32)).astype(BF)
    wide = jnp.broadcast_to(mine[None], (16, 32, 256)).reshape(512, 256)
    return lax.all_to_all(wide, group, 0, 0, tiled=True)


def shards(planes, denoised, dual, measured, psf, kernel, bias, mix):
    depth = ("xh", "y", "zh", "zl")
    x, d, z = planes[0], denoised[0], dual[0]
    psf_pad = jnp.pad(psf[0], ((0, 1), (0, 97)))

    def pack(rows, octet):
        edge = base(x[octet], d[octet], z[octet])
        return jnp.concatenate([x[rows].astype(BF), edge.astype(BF)], axis=0)

    down = [(i, i + 1) for i in range(3)]
    up = [(i + 1, i) for i in range(3)]
    lo = lax.ppermute(pack(slice(48, 64), slice(56, 64)), "band", down)
    hi = lax.ppermute(pack(slice(0, 16), slice(0, 8)), "band", up)
    wf, wd, mx = call(
        weights_kernel,
        [out((2560, 256), BF), out((512, 1024), BF), out((2048, 128), BF)],
        [pltpu.VMEM((4, 64, 1536), BF), pltpu.VMEM((32, 1024), F32), pltpu.VMEM((128, 1024), F32)],
        4,
    )(psf_pad, kernel, bias.reshape(1, 16), mix.reshape(16, 1))
    part, own, packed = call(
        forward_kernel,
        [out((512, 256), BF), out((512, 256), F32), out((70, 8, 256), BF)],
        [
            pltpu.VMEM((16, 128, 128), F32),
            pltpu.VMEM((66, 16, 256), F32),
            pltpu.VMEM((512, 2560), BF),
            pltpu.VMEM((512, 256), F32),
        ],
        8,
    )(x, d, z, measured, lo, hi, psf_pad, wf)
    later = [(i, i + 1) for i in range(63)]
    earlier = [(i + 1, i) for i in range(63)]
    prev_pack = lax.ppermute(packed, depth, later)
    next_pack = lax.ppermute(packed, depth, earlier)
    res = all_sum(part)
    res3 = res.reshape(64, 8, 256)
    res_lo = lax.ppermute(res3[:, 6:8], "band", down)
    res_hi = lax.ppermute(res3[:, 0:2], "band", up)
    (wg,) = call(back_weights_kernel, [out((2560, 768), BF)], [pltpu.VMEM((4, 64, 1536), BF)], 3)(
        psf_pad, prev_pack[68:70], next_pack[68:70]
    )
    band = lax.axis_index("band")
    valid = jnp.stack([(band > 0).astype(jnp.int32), (band < 3).astype(jnp.int32)])
    outs = call(
        final_kernel,
        [out((64, 2048), F32)] * 3,
        [
            pltpu.VMEM((66, 16, 256), F32),
            pltpu.VMEM((64, 16, 256), F32),
            pltpu.VMEM((512, 2560), BF),
            pltpu.VMEM((3, 66, 16, 256), F32),
            pltpu.VMEM((3, 4, 66, 8, 128), F32),
            pltpu.VMEM((2, 16, 64, 128), F32),
            pltpu.VMEM((512, 256), F32),
        ],
        14,
        flops=10_000_000_000,
        smem=1,
    )(valid, x, d, z, res, res_lo, res_hi, own, packed, prev_pack, next_pack, wg, wd, mx)
    return tuple(o[None] for o in outs)


def solution(mesh):
    fine = Mesh(mesh.devices.reshape(2, 4, 4, 2, 4), ("xh", "y", "zh", "zl", "band"))
    depth = ("xh", "y", "zh", "zl")
    volume = P(depth, "band", None)
    in_specs = (volume, volume, volume, P("band", None), P(depth, None, None), P(), P(), P())
    return jax.shard_map(shards, mesh=fine, in_specs=in_specs, out_specs=(volume,) * 3, check_vma=False)
```

time: 916 us -> 114 us (0.12)
  the two profiles are of different devices: /device:TPU:1 before, /device:TPU:5 now
where the time goes in v1:
time: 114 us; the launch traced here: 113 us
  starting transfers between devices  39.9 us (35%)
  Pallas kernels  35 us (31%)
  blocking collectives  14.6 us (13%)
  waiting for transfers between devices  13 us (11%)
  local copies, waits for them, and re-layouts  7.38 us (6%)
  other arithmetic  2.77 us (2%)
    all_to_all x1, blocking collectives, all_sum(): got = lax.all_to_all(part, group, 0, 0, tiled=True)  14.6 us
    pallas_call x1, Pallas kernels, shards(): call(forward_kernel, [out((512, 256), BF), out((512, 256), F32), out((70,...  14 us
    pallas_call x1, Pallas kernels, shards(): call(final_kernel, [out((64, 2048), F32)] * 3, [pltpu.VMEM((66, 16, 256),...  12.9 us
    ppermute x1, waiting for transfers between devices, shards(): prev_pack = lax.ppermute(packed, depth, later)  8.82 us
    ppermute x2, starting transfers between devices, all_sum(): other = lax.ppermute(mine, 'zh', [(a, a ^ bit) for a in range(4)])  8.72 us
    ppermute x1, starting transfers between devices, shards(): next_pack = lax.ppermute(packed, depth, earlier)  8.49 us
    all_to_all x1, starting transfers between devices, all_sum(): return lax.all_to_all(wide, group, 0, 0, tiled=True)  5.38 us
    ppermute x1, starting transfers between devices, shards(): res_hi = lax.ppermute(res3[:, 0:2], 'band', up)  5.32 us
  transfers between devices with their start and end apart: 9, of which 4 were waited for; matrix products, arithmetic and copies ran while one was open for 5% of the time, Pallas kernels for 7%

profile of v1, /device:TPU:5, one launch (start us, length us, event | category | flops | bytes accessed | tf_op | source)
XLA Modules:
  0.0 113.5 jit_solution(2039225499612431348)
XLA Ops:
  0.6 1.1 convert.8
  1.7 1.0 fusion.3
  2.8 3.4 %collective-permute-start = (bf16[24,2048]{1,0:T(8,128)(2,1)S(1)}, bf16[24,2048]{1,0:T(8,128)(2,1)S(1)}, u32[]{:S(2)}, u32[]{:S(2)}) collective-permute-start(bf16[24,2048]{1,0:T(8,128)(2,1)S(1)} %pad_maximum_fusion), channel_id=1, source_target_pairs={{0,1},{1,2},{2,3},{4,5},{5,6},{6,7},{8,9},{9,10},{10,11},{12,13},{... | collective-permute-start | bytes 294920 | tf_op jit(solution)/shard_map/ppermute | solution.py:327
  6.2 1.9 %collective-permute-start.1 = (bf16[24,2048]{1,0:T(8,128)(2,1)S(1)}, bf16[24,2048]{1,0:T(8,128)(2,1)S(1)}, u32[]{:S(2)}, u32[]{:S(2)}) collective-permute-start(bf16[24,2048]{1,0:T(8,128)(2,1)S(1)} %pad_maximum_fusion.1), channel_id=1, source_target_pairs={{1,0},{2,1},{3,2},{5,4},{6,5},{7,6},{9,8},{10,9},{11,10},{13,12},{... | collective-permute-start | bytes 294920 | tf_op jit(solution)/shard_map/ppermute | solution.py:328
  8.1 1.3 %copy.12.mix_ref = bf16[16,1]{1,0:T(8,128)(2,1)} copy(bf16[16,1]{0,1:T(2,128)(2,1)} %bitcast.62) | data formatting | bytes 64 | tf_op jit(solution)/shard_map/reshape | solution.py:334
  9.5 1.4 %copy.11.kernel_ref = bf16[27,16]{1,0:T(8,128)(2,1)} copy(bf16[27,16]{0,1:T(8,128)(2,1)} %param.13) | data formatting | bytes 1728 | tf_op args[5]
  10.8 1.3 %pad.4.psf_ref.psf = bf16[32,128]{1,0:T(8,128)(2,1)} pad(bf16[31,31]{1,0:T(8,128)(2,1)} %bitcast.61, bf16[]{:T(256)} %constant.16.clone.1), padding=0_1x0_97 | pad | bytes 10116 | tf_op jit(solution)/shard_map/jit(_pad)/pad | solution.py:319
  12.1 3.9 %shard_map.103 = (bf16[2560,256]{1,0:T(8,128)(2,1)}, bf16[512,1024]{1,0:T(8,128)(2,1)}, bf16[2048,128]{1,0:T(8,128)(2,1)}) custom-call(bf16[32,128]{1,0:T(8,128)(2,1)} %pad.4.psf_ref.psf, bf16[27,16]{1,0:T(8,128)(2,1)} %copy.11.kernel_ref, f32[1,16]{1,0:T(1,128)} %bitcast.63, bf16[16,1]{1,0:T(8,128)(2,1)} %copy.12.mix_ref), custom_call_target="tpu_custom_call" | custom-call | flops 1000000000 | bytes 4000000 | tf_op jit(solution)/shard_map/pallas_call | solution.py:329
  16.1 0.0 collective-permute-done.lo
  16.1 0.0 copy-start.3
  16.1 0.0 collective-permute-done.1.hi
  16.1 0.0 copy-start.4
  16.1 0.6 copy-done.3
  16.7 0.0 copy-done.4
  16.7 14.0 %shard_map.104 = (bf16[512,256]{1,0:T(8,128)(2,1)}, f32[512,256]{1,0:T(8,128)}, bf16[70,8,256]{2,1,0:T(8,128)(2,1)}) custom-call(f32[64,2048]{1,0:T(8,128)} %bitcast.52, f32[64,2048]{1,0:T(8,128)} %bitcast.57, f32[64,2048]{1,0:T(8,128)} %bitcast.59, f32[64,2048]{1,0:T(8,128)} %measured.1, bf16[24,2048]{1,0:T(8,128)(2,1)} %copy-done.3, ...), custom_call_target="tpu_custom_call" | custom-call | flops 1000000000 | bytes 4000000 | tf_op jit(solution)/shard_map/pallas_call | solution.py:335
  30.7 14.6 %all_to_all.17 = bf16[16,32,256]{2,1,0:T(8,128)(2,1)S(1)} all-to-all(bf16[16,32,256]{2,1,0:T(8,128)(2,1)} %bitcast.56), channel_id=1, replica_groups=mesh['xh'=2,'y'=4,'zh'=4,'zl'=2,'band'=4] {'xh','y','zl'}, dimensions={0} | all-to-all | bytes 524288 | tf_op jit(solution)/shard_map/all_to_all | solution.py:307
  45.4 6.1 %collective-permute-start.2 = (bf16[32,256]{1,0:T(8,128)(2,1)S(1)}, bf16[32,256]{1,0:T(8,128)(2,1)S(1)}, u32[]{:S(2)}, u32[]{:S(2)}) collective-permute-start(bf16[32,256]{1,0:T(8,128)(2,1)S(1)} %reduce_sum.12), channel_id=1, source_target_pairs={{0,16},{8,24},{16,0},{24,8},{1,17},{9,25},{17,1},{25,9},{2,18},{10... | collective-permute-start | bytes 49160 | tf_op jit(solution)/shard_map/ppermute | solution.py:310
  51.5 1.3 %collective-permute-done.2 = bf16[32,256]{1,0:T(8,128)(2,1)S(1)} collective-permute-done((bf16[32,256]{1,0:T(8,128)(2,1)S(1)}, bf16[32,256]{1,0:T(8,128)(2,1)S(1)}, u32[]{:S(2)}, u32[]{:S(2)}) %collective-permute-start.2) | collective-permute-done | bytes 16416 | tf_op jit(solution)/shard_map/ppermute | solution.py:310
  52.8 2.6 %collective-permute-start.3 = (bf16[32,256]{1,0:T(8,128)(2,1)S(1)}, bf16[32,256]{1,0:T(8,128)(2,1)S(1)}, u32[]{:S(2)}, u32[]{:S(2)}) collective-permute-start(bf16[32,256]{1,0:T(8,128)(2,1)S(1)} %add_convert_fusion.1), channel_id=1, source_target_pairs={{0,8},{8,0},{16,24},{24,16},{1,9},{9,1},{17,25},{25,17},{2,10},{10... | collective-permute-start | bytes 49160 | tf_op jit(solution)/shard_map/ppermute | solution.py:310
  55.4 1.2 %collective-permute-done.3 = bf16[32,256]{1,0:T(8,128)(2,1)S(1)} collective-permute-done((bf16[32,256]{1,0:T(8,128)(2,1)S(1)}, bf16[32,256]{1,0:T(8,128)(2,1)S(1)}, u32[]{:S(2)}, u32[]{:S(2)}) %collective-permute-start.3) | collective-permute-done | bytes 16416 | tf_op jit(solution)/shard_map/ppermute | solution.py:310
  56.6 0.7 broadcast_in_dim.15
  57.4 5.4 %all-to-all-start.1 = ((bf16[16,32,256]{2,1,0:T(8,128)(2,1)}), bf16[16,32,256]{2,1,0:T(8,128)(2,1)S(1)}, u32[]{:S(2)}, u32[]{:S(2)}) async-start(bf16[16,32,256]{2,1,0:T(8,128)(2,1)} %broadcast_in_dim.15), calls=%async_computation.1 | async-start | bytes 524288 | tf_op jit(solution)/shard_map/all_to_all | solution.py:313
  62.8 8.5 %collective-permute-start.7 = (bf16[70,8,256]{2,1,0:T(8,128)(2,1)}, bf16[70,8,256]{2,1,0:T(8,128)(2,1)S(1)}, u32[]{:S(2)}, u32[]{:S(2)}) collective-permute-start(bf16[70,8,256]{2,1,0:T(8,128)(2,1)} %get-tuple-element.15.own_pack), channel_id=1, source_target_pairs={{4,0},{8,4},{12,8},{16,12},{20,16},{24,20},{28,24},{32,28},{36,32}... | collective-permute-start | bytes 860168 | tf_op jit(solution)/shard_map/ppermute | solution.py:349
  71.3 1.9 %collective-permute-start.6 = (bf16[70,8,256]{2,1,0:T(8,128)(2,1)}, bf16[70,8,256]{2,1,0:T(8,128)(2,1)S(1)}, u32[]{:S(2)}, u32[]{:S(2)}) collective-permute-start(bf16[70,8,256]{2,1,0:T(8,128)(2,1)} %get-tuple-element.15.own_pack), channel_id=1, source_target_pairs={{0,4},{4,8},{8,12},{12,16},{16,20},{20,24},{24,28},{28,32},{32,36}... | collective-permute-start | bytes 860168 | tf_op jit(solution)/shard_map/ppermute | solution.py:348
  73.2 0.6 add_convert_fusion.2.valid
  73.8 1.7 %collective-permute-done.7.next_pack = bf16[70,8,256]{2,1,0:T(8,128)(2,1)S(1)} collective-permute-done((bf16[70,8,256]{2,1,0:T(8,128)(2,1)}, bf16[70,8,256]{2,1,0:T(8,128)(2,1)S(1)}, u32[]{:S(2)}, u32[]{:S(2)}) %collective-permute-start.7) | collective-permute-done | bytes 286752 | tf_op jit(solution)/shard_map/ppermute | solution.py:349
  75.5 0.0 copy-start.1
  75.5 0.6 slice.81.next_ref
  76.1 8.8 %collective-permute-done.6.prev_pack = bf16[70,8,256]{2,1,0:T(8,128)(2,1)S(1)} collective-permute-done((bf16[70,8,256]{2,1,0:T(8,128)(2,1)}, bf16[70,8,256]{2,1,0:T(8,128)(2,1)S(1)}, u32[]{:S(2)}, u32[]{:S(2)}) %collective-permute-start.6) | collective-permute-done | bytes 286752 | tf_op jit(solution)/shard_map/ppermute | solution.py:348
  84.9 0.0 copy-start.2
  84.9 0.6 slice.80.prev_ref
  85.6 0.0 all-to-all-done.1
  85.6 0.0 copy-start
  85.6 0.1 fusion.8
  85.7 5.3 %collective-permute-start.5 = (bf16[64,2,256]{2,1,0:T(2,128)(2,1)S(1)}, bf16[64,2,256]{2,1,0:T(2,128)(2,1)S(1)}, u32[]{:S(2)}, u32[]{:S(2)}) collective-permute-start(bf16[64,2,256]{2,1,0:T(2,128)(2,1)S(1)} %get-tuple-element.23), channel_id=1, source_target_pairs={{1,0},{2,1},{3,2},{5,4},{6,5},{7,6},{9,8},{10,9},{11,10},{13,12},{... | collective-permute-start | bytes 196616 | tf_op jit(solution)/shard_map/ppermute | solution.py:353
  91.0 4.8 %collective-permute-start.4 = (bf16[64,2,256]{2,1,0:T(2,128)(2,1)S(1)}, bf16[64,2,256]{2,1,0:T(2,128)(2,1)S(1)}, u32[]{:S(2)}, u32[]{:S(2)}) collective-permute-start(bf16[64,2,256]{2,1,0:T(2,128)(2,1)S(1)} %get-tuple-element.24), channel_id=1, source_target_pairs={{0,1},{1,2},{2,3},{4,5},{5,6},{6,7},{8,9},{9,10},{10,11},{12,13},{... | collective-permute-start | bytes 196616 | tf_op jit(solution)/shard_map/ppermute | solution.py:352
  95.8 4.1 %shard_map.105.wg = bf16[2560,768]{1,0:T(8,128)(2,1)} custom-call(bf16[32,128]{1,0:T(8,128)(2,1)} %pad.4.psf_ref.psf, bf16[2,8,256]{2,1,0:T(8,128)(2,1)} %slice.80.prev_ref, bf16[2,8,256]{2,1,0:T(8,128)(2,1)} %slice.81.next_ref), custom_call_target="tpu_custom_call" | custom-call | flops 1000000000 | bytes 4000000 | tf_op jit(solution)/shard_map/pallas_call | solution.py:354
  99.9 0.0 collective-permute-done.5.res_hi
  99.9 0.0 copy-start.5
  99.9 0.0 collective-permute-done.4.res_lo
  99.9 0.0 copy-start.6
  99.9 0.0 copy-done.1
  99.9 0.0 copy-done.2
  99.9 0.0 copy-done
  99.9 0.6 copy-done.5
  100.5 0.0 copy-done.6
  100.5 12.9 %shard_map.106 = (f32[64,2048]{1,0:T(8,128)}, f32[64,2048]{1,0:T(8,128)}, f32[64,2048]{1,0:T(8,128)}) custom-call(s32[2]{0:T(128)} %add_convert_fusion.2.valid, f32[64,2048]{1,0:T(8,128)} %bitcast.53, f32[64,2048]{1,0:T(8,128)} %bitcast.58, f32[64,2048]{1,0:T(8,128)} %bitcast.60, bf16[512,256]{1,0:T(8,128)(2,1)} %bitcast.55, bf16[64,2,256]{2,1,0:T(2,128)(2,1)} %copy-done.6, ...), custom_call_target="tpu_custom_call" | custom-call | flops 10000000000 | bytes 4000000 | tf_op jit(solution)/shard_map/pallas_call | solution.py:359
  (6 shorter events, 0.1 us)
Async XLA Ops:
  2.8 13.3 %collective-permute-start = (bf16[24,2048]{1,0:T(8,128)(2,1)S(1)}, bf16[24,2048]{1,0:T(8,128)(2,1)S(1)}, u32[]{:S(2)}, u32[]{:S(2)}) collective-permute-start(bf16[24,2048]{1,0:T(8,128)(2,1)S(1)} %pad_maximum_fusion), channel_id=1, source_target_pairs={{0,1},{1,2},{2,3},{4,5},{5,6},{6,7},{8,9},{9,10},{10,11},{12,13},{... | collective-permute-start | bytes 294920 | tf_op jit(solution)/shard_map/ppermute | solution.py:327
  6.2 9.9 %collective-permute-start.1 = (bf16[24,2048]{1,0:T(8,128)(2,1)S(1)}, bf16[24,2048]{1,0:T(8,128)(2,1)S(1)}, u32[]{:S(2)}, u32[]{:S(2)}) collective-permute-start(bf16[24,2048]{1,0:T(8,128)(2,1)S(1)} %pad_maximum_fusion.1), channel_id=1, source_target_pairs={{1,0},{2,1},{3,2},{5,4},{6,5},{7,6},{9,8},{10,9},{11,10},{13,12},{... | collective-permute-start | bytes 294920 | tf_op jit(solution)/shard_map/ppermute | solution.py:328
  16.1 0.6 copy-start.3
  16.1 0.7 copy-start.4
  45.4 7.4 %collective-permute-start.2 = (bf16[32,256]{1,0:T(8,128)(2,1)S(1)}, bf16[32,256]{1,0:T(8,128)(2,1)S(1)}, u32[]{:S(2)}, u32[]{:S(2)}) collective-permute-start(bf16[32,256]{1,0:T(8,128)(2,1)S(1)} %reduce_sum.12), channel_id=1, source_target_pairs={{0,16},{8,24},{16,0},{24,8},{1,17},{9,25},{17,1},{25,9},{2,18},{10... | collective-permute-start | bytes 49160 | tf_op jit(solution)/shard_map/ppermute | solution.py:310
  52.8 3.9 %collective-permute-start.3 = (bf16[32,256]{1,0:T(8,128)(2,1)S(1)}, bf16[32,256]{1,0:T(8,128)(2,1)S(1)}, u32[]{:S(2)}, u32[]{:S(2)}) collective-permute-start(bf16[32,256]{1,0:T(8,128)(2,1)S(1)} %add_convert_fusion.1), channel_id=1, source_target_pairs={{0,8},{8,0},{16,24},{24,16},{1,9},{9,1},{17,25},{25,17},{2,10},{10... | collective-permute-start | bytes 49160 | tf_op jit(solution)/shard_map/ppermute | solution.py:310
  57.4 28.2 %all-to-all-start.1 = ((bf16[16,32,256]{2,1,0:T(8,128)(2,1)}), bf16[16,32,256]{2,1,0:T(8,128)(2,1)S(1)}, u32[]{:S(2)}, u32[]{:S(2)}) async-start(bf16[16,32,256]{2,1,0:T(8,128)(2,1)} %broadcast_in_dim.15), calls=%async_computation.1 | async-start | bytes 524288 | tf_op jit(solution)/shard_map/all_to_all | solution.py:313
  62.8 12.7 %collective-permute-start.7 = (bf16[70,8,256]{2,1,0:T(8,128)(2,1)}, bf16[70,8,256]{2,1,0:T(8,128)(2,1)S(1)}, u32[]{:S(2)}, u32[]{:S(2)}) collective-permute-start(bf16[70,8,256]{2,1,0:T(8,128)(2,1)} %get-tuple-element.15.own_pack), channel_id=1, source_target_pairs={{4,0},{8,4},{12,8},{16,12},{20,16},{24,20},{28,24},{32,28},{36,32}... | collective-permute-start | bytes 860168 | tf_op jit(solution)/shard_map/ppermute | solution.py:349
  71.3 13.7 %collective-permute-start.6 = (bf16[70,8,256]{2,1,0:T(8,128)(2,1)}, bf16[70,8,256]{2,1,0:T(8,128)(2,1)S(1)}, u32[]{:S(2)}, u32[]{:S(2)}) collective-permute-start(bf16[70,8,256]{2,1,0:T(8,128)(2,1)} %get-tuple-element.15.own_pack), channel_id=1, source_target_pairs={{0,4},{4,8},{8,12},{12,16},{16,20},{20,24},{24,28},{28,32},{32,36}... | collective-permute-start | bytes 860168 | tf_op jit(solution)/shard_map/ppermute | solution.py:348
  75.5 24.4 %copy-start.1 = (bf16[70,8,256]{2,1,0:T(8,128)(2,1)}, bf16[70,8,256]{2,1,0:T(8,128)(2,1)S(1)}, u32[]{:S(2)}) copy-start(bf16[70,8,256]{2,1,0:T(8,128)(2,1)S(1)} %collective-permute-done.7.next_pack) | copy-start | bytes 860164
  84.9 15.0 %copy-start.2 = (bf16[70,8,256]{2,1,0:T(8,128)(2,1)}, bf16[70,8,256]{2,1,0:T(8,128)(2,1)S(1)}, u32[]{:S(2)}) copy-start(bf16[70,8,256]{2,1,0:T(8,128)(2,1)S(1)} %collective-permute-done.6.prev_pack) | copy-start | bytes 860164
  85.6 14.4 %copy-start = (bf16[16,32,256]{2,1,0:T(8,128)(2,1)}, bf16[16,32,256]{2,1,0:T(8,128)(2,1)S(1)}, u32[]{:S(2)}) copy-start(bf16[16,32,256]{2,1,0:T(8,128)(2,1)S(1)} %all-to-all-done.1) | copy-start | bytes 786436
  85.7 14.2 %collective-permute-start.5 = (bf16[64,2,256]{2,1,0:T(2,128)(2,1)S(1)}, bf16[64,2,256]{2,1,0:T(2,128)(2,1)S(1)}, u32[]{:S(2)}, u32[]{:S(2)}) collective-permute-start(bf16[64,2,256]{2,1,0:T(2,128)(2,1)S(1)} %get-tuple-element.23), channel_id=1, source_target_pairs={{1,0},{2,1},{3,2},{5,4},{6,5},{7,6},{9,8},{10,9},{11,10},{13,12},{... | collective-permute-start | bytes 196616 | tf_op jit(solution)/shard_map/ppermute | solution.py:353
  91.0 8.9 %collective-permute-start.4 = (bf16[64,2,256]{2,1,0:T(2,128)(2,1)S(1)}, bf16[64,2,256]{2,1,0:T(2,128)(2,1)S(1)}, u32[]{:S(2)}, u32[]{:S(2)}) collective-permute-start(bf16[64,2,256]{2,1,0:T(2,128)(2,1)S(1)} %get-tuple-element.24), channel_id=1, source_target_pairs={{0,1},{1,2},{2,3},{4,5},{5,6},{6,7},{8,9},{9,10},{10,11},{12,13},{... | collective-permute-start | bytes 196616 | tf_op jit(solution)/shard_map/ppermute | solution.py:352
  99.9 0.6 copy-start.5
  99.9 0.6 copy-start.6

commit v2 on v1

v2 whole, which is shorter than its diff:
```python
import jax
import jax.numpy as jnp
from jax import lax
from jax.experimental import pallas as pl
from jax.experimental.pallas import tpu as pltpu
from jax.sharding import Mesh, PartitionSpec as P

STEP = 4.0
HALF = 0.5
BF = jnp.bfloat16
F32 = jnp.float32
MIB = 1024 * 1024


def iota(shape, axis):
    return lax.broadcasted_iota(jnp.int32, shape, axis)


def swap_matrix():
    k = iota((512, 512), 0)
    n = iota((512, 512), 1)
    return jnp.where(n == 128 * ((k // 32) % 4) + 32 * (k // 128) + k % 32, 1.0, 0.0).astype(BF)


def split(x):
    high = x.astype(BF)
    return high, (x - high.astype(F32)).astype(BF)


def toeplitz(psf, flip, strips, put, scale=1.0, turn=0):
    s = iota((64, 128), 0) - 1
    b = iota((64, 128), 1)
    pick = jnp.where(s == ((30 - b) if flip else b), 1.0, 0.0).astype(BF)
    turned = lax.dot_general(pick, psf, (((1,), (1,)), ((), ())), preferred_element_type=F32).astype(BF)
    a = iota((32, 1536), 0)
    u = iota((32, 1536), 1) // 32
    spread = jnp.where(a == ((u - 8) if flip else (38 - u)), scale, 0.0).astype(BF)
    strip = jnp.dot(turned, spread, preferred_element_type=F32)
    j = (iota((64, 1536), 1) - turn + 32) % 32
    for bit in (1, 2, 4, 8, 16):
        strip = jnp.where((j & bit) != 0, pltpu.roll(strip, bit, 0), strip)
    for k in range(4):
        moved = strip if k == 0 else pltpu.roll(strip, 1536 - 32 * k, 1)
        strips[k] = moved.astype(BF)
    for d in range(5):
        for i in range(8):
            u0 = 23 - 8 * (d - 2) - i
            cut = slice(128 * (u0 // 4), 128 * (u0 // 4) + 256)
            at = 512 * d + 32 * i
            put(at, strips[u0 % 4, 16:48, cut])
            put(at + 256, strips[u0 % 4, 48:64, cut])
            put(at + 272, strips[u0 % 4, 0:16, cut])


TURN = (2, 0, 4)


def forward_weights_kernel(psf_ref, wf_ref, strips):
    def put(at, value):
        wf_ref[at : at + value.shape[0], :] = value

    toeplitz(unpack_psf(psf_ref), False, strips, put)


def denoiser_weights_kernel(kernel_ref, bias_ref, mix_ref, even_ref, odd_ref, mx_ref, taps, rims):
    n_of = jnp.where(iota((16, 1024), 1) // 64 == iota((16, 1024), 0), 1.0, 0.0).astype(BF)
    taps[0:27, :] = jnp.dot(kernel_ref[...], n_of, preferred_element_type=F32)
    lane = iota((32, 1024), 1)
    j = lane % 32
    r = (lane // 32) % 2
    lane1 = iota((1, 1024), 1)
    j1 = lane1 % 32
    r1 = (lane1 // 32) % 2
    rims[...] = jnp.zeros_like(rims)
    for d in range(3):
        jp = (iota((32, 1024), 0) - TURN[d] + 32) % 32
        for w in range(4):
            total = jnp.zeros((32, 1024), F32)
            right = jnp.zeros((1, 1024), F32)
            left = jnp.zeros((1, 1024), F32)
            for u in range(3):
                if w - u not in (0, 1):
                    continue
                for v in range(3):
                    row = taps[9 * d + 3 * u + v : 9 * d + 3 * u + v + 1, :]
                    total = jnp.where((r == w - u) & (jp == j + (v - 1)), row, total)
                    if v == 2:
                        right = jnp.where((r1 == w - u) & (j1 == 31), row, right)
                    if v == 0:
                        left = jnp.where((r1 == w - u) & (j1 == 0), row, left)
            for odd, ref in enumerate((even_ref, odd_ref)):
                group = (w + (1 if odd else 3)) % 4
                ref[(4 * d + group) * 32 : (4 * d + group) * 32 + 32, :] = total.astype(BF)
                at = 32 * group + TURN[d]
                rims[odd, at : at + 1, :] = right
                at = 32 * group + (31 + TURN[d]) % 32
                rims[odd, at : at + 1, :] = left
    bias = bias_ref[...]
    for at in (6, 7, 8):
        part = bias.astype(BF)
        row = jnp.dot(part, n_of, preferred_element_type=F32)
        rims[0, at : at + 1, :] = row
        rims[1, at : at + 1, :] = row
        bias = bias - part.astype(F32)
    even_ref[384:512, :] = rims[0].astype(BF)
    odd_ref[384:512, :] = rims[1].astype(BF)
    rows_n = jnp.where(iota((1024, 16), 0) // 64 == iota((1024, 16), 1), 1.0, 0.0).astype(BF)
    mixed = jnp.dot(rows_n, jnp.broadcast_to(mix_ref[...], (16, 128)), preferred_element_type=F32)
    pos = iota((1024, 128), 0) % 64
    lane = iota((1024, 128), 1)
    mx_ref[0:1024, :] = jnp.where(lane == pos, mixed, 0.0).astype(BF)
    mx_ref[1024:2048, :] = jnp.where(lane == pos + 64, mixed, 0.0).astype(BF)


def unpack_psf(ref):
    return jnp.concatenate([ref[64 + g // 2, :, 128 * (g % 2) : 128 * (g % 2) + 128] for g in range(4)], axis=0)


def back_weights_kernel(prev_pack, own_pack, next_pack, wg_ref, down_ref, up_ref, strips, wide):
    down_ref[64:128, 128:256] = jnp.ones((64, 128), BF)
    up_ref[64:128, 128:256] = jnp.ones((64, 128), BF)
    for p, pack in enumerate((prev_pack, own_pack, next_pack)):

        def put(at, value, p=p):
            wg_ref[at : at + value.shape[0], 256 * p : 256 * p + 256] = value

        toeplitz(unpack_psf(pack), True, strips, put, -STEP, TURN[p])
        wide[...] = pack[0:64].astype(F32)
        at = slice(64 * (p // 2), 64 * (p // 2) + 64)
        lanes = slice(128 * (p % 2), 128 * (p % 2) + 128)
        down_ref[at, lanes] = wide[:, 7, 128:256].astype(BF)
        up_ref[at, lanes] = wide[:, 0, 0:128].astype(BF)


def gather_rows(main, lhs):
    j = iota((64, 8, 256), 2) % 32
    for d in range(5):
        lhs[:, 512 * d : 512 * d + 256] = main[1:65, d : d + 8, :].reshape(512, 256).astype(BF)
        rims = jnp.where(j < 16, main[2:66, d : d + 8, :], main[0:64, d : d + 8, :])
        lhs[:, 512 * d + 256 : 512 * d + 512] = rims.reshape(512, 256).astype(BF)


def base(planes, denoised, dual):
    return planes - STEP * (HALF * (planes - (denoised - dual))) + dual


def octets(nat, t, h, at):
    return jnp.concatenate([nat[t, pl.ds(at + 4 * h + m, 8, stride=8), :] for m in range(4)], axis=1)


def start_kernel(planes, denoised, dual, psf_ref, down_ref, up_ref, pack_ref, low_ref, swap_ref, nat, lhs):
    psf = jnp.pad(psf_ref[...].astype(F32), ((0, 1), (0, 97))).astype(BF)
    down_ref[...] = planes[48:64, :].astype(BF)
    up_ref[...] = planes[0:16, :].astype(BF)
    swap = swap_matrix()
    swap_ref[...] = swap
    for t in range(16):
        c = slice(128 * t, 128 * t + 128)
        nat[t] = base(planes[:, c], denoised[:, c], dual[:, c])
    for t in range(16):
        rows = jnp.concatenate([octets(nat, t, 0, 0), octets(nat, t, 1, 0)], axis=0)
        lhs[0, 16 * t : 16 * t + 16, :], lhs[1, 16 * t : 16 * t + 16, :] = split(rows)
    for part, ref in enumerate((pack_ref, low_ref)):
        moved = jnp.dot(lhs[part], swap, preferred_element_type=F32)
        for t in range(16):
            for g in range(4):
                for h in range(2):
                    at = 16 * t + 8 * h
                    ref[4 * t + g, :, 128 * h : 128 * h + 128] = moved[at : at + 8, 128 * g : 128 * g + 128].astype(BF)
    for g in range(4):
        pack_ref[64 + g // 2, :, 128 * (g % 2) : 128 * (g % 2) + 128] = psf[8 * g : 8 * g + 8, :]


def forward_kernel(planes, measured, lo, hi, wf, swap, part_ref, nat, main, lhs, turn):
    for t in range(16):
        c = slice(128 * t, 128 * t + 128)
        nat[0, t, 0:16, :] = lo[:, c].astype(F32)
        nat[0, t, 16:80, :] = planes[:, c].astype(BF).astype(F32)
        nat[0, t, 80:96, :] = hi[:, c].astype(F32)
        nat[0, t, 96:128, :] = jnp.zeros((32, 128), F32)
        nat[1, t, 0:64, :] = measured[:, c]
    for t in range(16):
        for h in range(2):
            rows = jnp.concatenate([octets(nat.at[0], t, h, 0), octets(nat.at[0], t, h, 64)], axis=0)
            turn[32 * t + 16 * h : 32 * t + 16 * h + 16, :] = rows.astype(BF)
        rows = jnp.concatenate([octets(nat.at[1], t, 0, 0), octets(nat.at[1], t, 1, 0)], axis=0)
        turn[512 + 16 * t : 528 + 16 * t, :], turn[768 + 16 * t : 784 + 16 * t, :] = split(rows)
    moved = jnp.dot(turn[...], swap[...], preferred_element_type=F32)
    main[0] = jnp.zeros((16, 256), F32)
    main[65] = jnp.zeros((16, 256), F32)
    for t in range(16):
        for h in range(2):
            for g in range(4):
                at = 32 * t + 16 * h
                main[1 + 4 * t + g, :, 128 * h : 128 * h + 128] = moved[at : at + 16, 128 * g : 128 * g + 128]
    gather_rows(main, lhs)
    sums = jnp.dot(lhs[...], wf[...], preferred_element_type=F32)
    seen = moved[512:768, :] + moved[768:1024, :]
    for t in range(16):
        for g in range(4):
            k = 4 * t + g
            mine = jnp.concatenate(
                [seen[16 * t + 8 * h : 16 * t + 8 * h + 8, 128 * g : 128 * g + 128] for h in range(2)], axis=1
            )
            part_ref[8 * k : 8 * k + 8, :] = (sums[8 * k : 8 * k + 8, :] - mine * (1.0 / 64)).astype(BF)


def rims_kernel(res, edge_down, edge_up, down_ref, up_ref, wide):
    wide[...] = res[...].astype(F32).reshape(64, 8, 256)
    for at, q in enumerate((6, 7)):
        down_ref[64 * at : 64 * at + 64, :] = wide[:, q, :].astype(BF)
    for at, q in enumerate((0, 1)):
        up_ref[64 * at : 64 * at + 64, :] = wide[:, q, :].astype(BF)
    down_ref[128:256, :] = edge_down[...]
    up_ref[128:256, :] = edge_up[...]


def back_kernel(res, wg, moves_ref, main, lhs):
    main[0] = jnp.zeros((16, 256), F32)
    main[65] = jnp.zeros((16, 256), F32)
    main[1:65, 0:2, :] = jnp.zeros((64, 2, 256), F32)
    main[1:65, 2:10, :] = res[...].astype(F32).reshape(64, 8, 256)
    main[1:65, 10:12, :] = jnp.zeros((64, 2, 256), F32)
    gather_rows(main, lhs)
    moves_ref[...] = jnp.dot(lhs[...], wg[...], preferred_element_type=F32)


def final_kernel(planes, denoised, dual, res, moves, lo, hi, own_low, own_pack, prev_pack, next_pack, wg, even, odd, mx,
                 swap, np_ref, nd_ref, du_ref, main, lhs, vol, wins, nat, turn, mine):
    main[0] = jnp.zeros((16, 256), F32)
    main[65] = jnp.zeros((16, 256), F32)
    main[1:65, 2:10, :] = res[...].astype(F32).reshape(64, 8, 256)
    for at in range(2):
        main[1:65, at, :] = lo[64 * at : 64 * at + 64, :].astype(F32)
        main[1:65, 10 + at, :] = hi[64 * at : 64 * at + 64, :].astype(F32)
    j = iota((64, 256), 1) % 32

    def octet(q):
        rim = jnp.where(j < 16, main[2:66, q, :], main[0:64, q, :])
        return [main[1:65, q, :].astype(BF), rim.astype(BF)]

    rows = {q: octet(q) for q in (0, 1, 2, 3, 8, 9, 10, 11)}
    above = jnp.concatenate(rows[0] + rows[1] + rows[2] + rows[3], axis=1)
    below = jnp.concatenate(rows[8] + rows[9] + rows[10] + rows[11], axis=1)
    none = [jnp.zeros((64, 512), BF)]
    first = jnp.concatenate(
        [jnp.concatenate(rows[0] + rows[1], axis=1), jnp.concatenate(rows[1] + none, axis=1)], axis=0
    )
    last = jnp.concatenate(
        [jnp.concatenate(none + rows[10], axis=1), jnp.concatenate(rows[10] + rows[11], axis=1)], axis=0
    )
    first = jnp.dot(first, wg[0:1024, :], preferred_element_type=F32)
    last = jnp.dot(last, wg[1536:2560, :], preferred_element_type=F32)
    use_lo = lo[192:256, 128:256] > 0
    use_hi = hi[192:256, 128:256] > 0
    row = iota((256, 256), 0)
    col = iota((256, 256), 1)
    for p, pack in enumerate((prev_pack, own_pack, next_pack)):
        start = pack[0:64].reshape(512, 256)
        at = slice(128 + 64 * (p // 2), 192 + 64 * (p // 2))
        lanes = slice(128 * (p % 2), 128 * (p % 2) + 128)
        edge_lo = lo[at, lanes]
        edge_hi = hi[at, lanes]
        if p == 1:
            start = start.astype(F32) + own_low[...].astype(F32).reshape(512, 256)
            edge_lo = edge_lo.astype(F32)
            edge_hi = edge_hi.astype(F32)
        else:
            same = (col // 32 == row // 32) & (col % 32 == (row % 32 + TURN[p]) % 32)
            shift = jnp.where(same, 1.0, 0.0).astype(BF)
            start = jnp.dot(start, shift, preferred_element_type=F32)
            edge_lo = jnp.dot(edge_lo, shift[0:128, 0:128], preferred_element_type=F32)
            edge_hi = jnp.dot(edge_hi, shift[0:128, 0:128], preferred_element_type=F32)
        vol[p, 0] = jnp.zeros((16, 256), F32)
        vol[p, 65] = jnp.zeros((16, 256), F32)
        cut = slice(256 * p, 256 * p + 256)
        vol[p, 1:65, 1:9, :] = (start + moves[:, cut]).reshape(64, 8, 256)
        for at in range(2):
            vol[p, 1:65, 1 + at, :] += first[64 * at : 64 * at + 64, cut]
            vol[p, 1:65, 7 + at, :] += last[64 * at : 64 * at + 64, cut]
        if p == 1:
            mine[...] = moves[:, cut].reshape(64, 8, 256)
            for at in range(2):
                mine[:, at, :] += first[64 * at : 64 * at + 64, cut]
                mine[:, 6 + at, :] += last[64 * at : 64 * at + 64, cut]
        g_lo = jnp.dot(above, wg[512:2560, 256 * p + 128 : 256 * p + 256], preferred_element_type=F32)
        g_hi = jnp.dot(below, wg[0:2048, 256 * p : 256 * p + 128], preferred_element_type=F32)
        vol[p, 1:65, 0, 128:256] = jnp.where(use_lo, edge_lo + g_lo, 0.0)
        vol[p, 1:65, 9, 0:128] = jnp.where(use_hi, edge_hi + g_hi, 0.0)
        group = iota((66, 8, 128), 2) // 32
        t0 = vol[p, :, 1:9, 0:128]
        t1 = vol[p, :, 1:9, 128:256]
        wins[p, 0] = jnp.where(group == 3, vol[p, :, 0:8, 128:256], t0)
        wins[p, 1] = jnp.where(group == 0, t1, t0)
        wins[p, 2] = jnp.where(group == 3, t0, t1)
        wins[p, 3] = jnp.where(group == 0, vol[p, :, 2:10, 0:128], t1)
    lane = iota((64, 8, 128), 2)
    j = lane % 32
    ones = jnp.where((lane >= 6) & (lane <= 8), 1.0, 0.0)
    for k in range(4):
        rim = ones
        for p in range(3):
            at = 512 * k + 128 * p
            lhs[:, at : at + 128] = wins[p, k, 1:65].reshape(512, 128).astype(BF)
            rim = jnp.where(j == TURN[p], wins[p, k, 2:66], rim)
            rim = jnp.where(j == (31 + TURN[p]) % 32, wins[p, k, 0:64], rim)
        lhs[:, 512 * k + 384 : 512 * k + 512] = rim.reshape(512, 128).astype(BF)
    noise = []
    for half in range(2):
        total = None
        for e, wd in enumerate((even, odd)):
            k = 2 * half + e
            hidden = jnp.dot(lhs[:, 512 * k : 512 * k + 512], wd[...], preferred_element_type=F32)
            hidden = jnp.maximum(hidden, 0.0).astype(BF)
            part = jnp.dot(hidden, mx[1024 * e : 1024 * e + 1024, :], preferred_element_type=F32)
            total = part if total is None else total + part
        noise.append(total)
    for f in range(2):
        for t in range(16):
            for h in range(2):
                rows = jnp.concatenate(
                    [
                        noise[h][8 * k : 8 * k + 8, :] if f else mine[k, :, 128 * h : 128 * h + 128]
                        for k in range(4 * t, 4 * t + 4)
                    ],
                    axis=1,
                )
                if h == 0:
                    first = rows
            turn[f, 0, 16 * t : 16 * t + 16, :], turn[f, 1, 16 * t : 16 * t + 16, :] = split(
                jnp.concatenate([first, rows], axis=0)
            )
        moved = jnp.dot(turn[f, 0], swap[...], preferred_element_type=F32)
        moved = moved + jnp.dot(turn[f, 1], swap[...], preferred_element_type=F32)
        for t in range(16):
            for h in range(2):
                for m in range(4):
                    at = 16 * t + 8 * h
                    nat[f, t, pl.ds(4 * h + m, 8, stride=8), :] = moved[at : at + 8, 128 * m : 128 * m + 128]
    for t in range(16):
        c = slice(128 * t, 128 * t + 128)
        x = planes[:, c]
        z = dual[:, c]
        moved = (x - STEP * (HALF * (x - (denoised[:, c] - z)))) + nat[0, t]
        cleaned = (moved + z) - nat[1, t]
        np_ref[:, c] = moved
        nd_ref[:, c] = cleaned
        du_ref[:, c] = z + moved - cleaned


def call(body, outs, scratch, n_in, flops=1_000_000_000, vmem=20, specs=None):
    whole = pl.BlockSpec(memory_space=pltpu.VMEM)
    return pl.pallas_call(
        body,
        out_shape=outs,
        in_specs=specs or [whole] * n_in,
        out_specs=[whole] * len(outs),
        scratch_shapes=scratch,
        compiler_params=pltpu.CompilerParams(vmem_limit_bytes=vmem * MIB),
        cost_estimate=pl.CostEstimate(flops=flops, bytes_accessed=4_000_000, transcendentals=0),
    )


def out(shape, dtype):
    return jax.ShapeDtypeStruct(shape, dtype)


def shards(planes, denoised, dual, measured, psf, kernel, bias, mix):
    depth = ("xh", "y", "zh", "zl")
    group = ("xh", "y", "zl")
    x, d, z = planes[0], denoised[0], dual[0]
    down = [(i, i + 1) for i in range(3)]
    up = [(i + 1, i) for i in range(3)]
    later = [(i, i + 1) for i in range(63)]
    earlier = [(i + 1, i) for i in range(63)]

    to_down, to_up, packed, low, swap = call(
        start_kernel,
        [out((16, 2048), BF), out((16, 2048), BF), out((66, 8, 256), BF), out((64, 8, 256), BF), out((512, 512), BF)],
        [pltpu.VMEM((16, 64, 128), F32), pltpu.VMEM((2, 256, 512), BF)],
        4,
    )(x, d, z, psf[0])
    lo = lax.ppermute(to_down, "band", down)
    hi = lax.ppermute(to_up, "band", up)
    prev_pack = lax.ppermute(packed, depth, later)
    next_pack = lax.ppermute(packed, depth, earlier)
    strips = pltpu.VMEM((4, 64, 1536), BF)
    (wf,) = call(forward_weights_kernel, [out((2560, 256), BF)], [strips], 1)(packed)
    (part,) = call(
        forward_kernel,
        [out((512, 256), BF)],
        [
            pltpu.VMEM((2, 16, 128, 128), F32),
            pltpu.VMEM((66, 16, 256), F32),
            pltpu.VMEM((512, 2560), BF),
            pltpu.VMEM((1024, 512), BF),
        ],
        6,
    )(x, measured, lo, hi, wf, swap)
    part, prev_pack, next_pack = lax.optimization_barrier((part, prev_pack, next_pack))
    got = lax.all_to_all(part, group, 0, 0, tiled=True)
    got, prev_pack, own_pack, next_pack, kernel, bias, mix = lax.optimization_barrier(
        (got, prev_pack, packed, next_pack, kernel, bias.reshape(1, 16), mix.reshape(16, 1))
    )
    mine = jnp.sum(got.reshape(16, 32, 256).astype(F32), axis=0)
    other = lax.ppermute(mine, "zh", [(a, a ^ 2) for a in range(4)])
    wg, edge_down, edge_up = call(
        back_weights_kernel,
        [out((2560, 768), BF), out((128, 256), BF), out((128, 256), BF)],
        [strips, pltpu.VMEM((64, 8, 256), F32)],
        3,
    )(prev_pack, own_pack, next_pack)
    mine, wg = lax.optimization_barrier((mine + other, wg))
    other = lax.ppermute(mine, "zh", [(a, a ^ 1) for a in range(4)])
    even, odd, mx = call(
        denoiser_weights_kernel,
        [out((512, 1024), BF), out((512, 1024), BF), out((2048, 128), BF)],
        [pltpu.VMEM((32, 1024), F32), pltpu.VMEM((2, 128, 1024), F32)],
        3,
    )(kernel, bias, mix)
    mine, even = lax.optimization_barrier((mine + other, even))
    wide = jnp.broadcast_to(mine.astype(BF)[None], (16, 32, 256)).reshape(512, 256)
    res = lax.all_to_all(wide, group, 0, 0, tiled=True)
    rim_down, rim_up = call(
        rims_kernel, [out((256, 256), BF), out((256, 256), BF)], [pltpu.VMEM((64, 8, 256), F32)], 3
    )(res, edge_down, edge_up)
    rim_lo = lax.ppermute(rim_down, "band", down)
    rim_hi = lax.ppermute(rim_up, "band", up)
    (moves,) = call(
        back_kernel,
        [out((512, 768), F32)],
        [pltpu.VMEM((66, 16, 256), F32), pltpu.VMEM((512, 2560), BF)],
        2,
    )(res, wg)
    outs = call(
        final_kernel,
        [out((64, 2048), F32)] * 3,
        [
            pltpu.VMEM((66, 16, 256), F32),
            pltpu.VMEM((512, 2048), BF),
            pltpu.VMEM((3, 66, 16, 256), F32),
            pltpu.VMEM((3, 4, 66, 8, 128), F32),
            pltpu.VMEM((2, 16, 64, 128), F32),
            pltpu.VMEM((2, 2, 256, 512), BF),
            pltpu.VMEM((64, 8, 256), F32),
        ],
        16,
        flops=10_000_000_000,
        vmem=36,
    )(x, d, z, res, moves, rim_lo, rim_hi, low, packed, prev_pack, next_pack, wg, even, odd, mx, swap)
    return tuple(o[None] for o in outs)


def solution(mesh):
    fine = Mesh(mesh.devices.reshape(2, 4, 4, 2, 4), ("xh", "y", "zh", "zl", "band"))
    depth = ("xh", "y", "zh", "zl")
    volume = P(depth, "band", None)
    in_specs = (volume, volume, volume, P("band", None), P(depth, None, None), P(), P(), P())
    return jax.shard_map(shards, mesh=fine, in_specs=in_specs, out_specs=(volume,) * 3, check_vma=False)
```

time: 114 us -> 91.4 us (0.80)
  the two profiles are of different devices: /device:TPU:5 before, /device:TPU:1 now
where the time goes in v2:
time: 91.4 us; the launch traced here: 90.9 us
  blocking collectives  33.9 us (37%)
  starting transfers between devices  21.5 us (24%)
  Pallas kernels  19.7 us (22%)
  waiting for transfers between devices  8.95 us (10%)
  local copies, waits for them, and re-layouts  5.93 us (6%)
    all_to_all x1, blocking collectives, shards(): got = lax.all_to_all(part, group, 0, 0, tiled=True)  22.4 us
    all_to_all x1, blocking collectives, shards(): res = lax.all_to_all(wide, group, 0, 0, tiled=True)  11.4 us
    pallas_call x1, Pallas kernels, shards(): call(final_kernel, [out((64, 2048), F32)] * 3, [pltpu.VMEM((66, 16, 256),...  9.76 us
    ppermute x1, starting transfers between devices, shards(): rim_lo = lax.ppermute(rim_down, 'band', down)  6.09 us
    unnamed x26, local copies, waits for them, and re-layouts  5.72 us
    ppermute x1, starting transfers between devices, shards(): prev_pack = lax.ppermute(packed, depth, later)  5.02 us
    ppermute x1, starting transfers between devices, shards(): lo = lax.ppermute(to_down, 'band', down)  4.06 us
    ppermute x1, waiting for transfers between devices, shards(): hi = lax.ppermute(to_up, 'band', up)  2.94 us
  transfers between devices with their start and end apart: 8, of which 4 were waited for; matrix products, arithmetic and copies ran while one was open for 0% of the time, Pallas kernels for 10%

profile of v2, /device:TPU:1, one launch (start us, length us, event | category | flops | bytes accessed | tf_op | source)
XLA Modules:
  0.0 90.9 jit_solution(9509485620949498675)
XLA Ops:
  0.6 0.0 copy-start.3
  0.6 1.0 %copy-done.3 = f32[1,64,2048]{2,1,0:T(8,128)S(1)} copy-done((f32[1,64,2048]{2,1,0:T(8,128)S(1)}, f32[1,64,2048]{2,1,0:T(8,128)}, u32[]{:S(2)}) %copy-start.3) | copy-done | bytes 524312
  1.7 0.0 copy-start.5
  1.7 1.0 %copy-done.5 = f32[1,64,2048]{2,1,0:T(8,128)S(1)} copy-done((f32[1,64,2048]{2,1,0:T(8,128)S(1)}, f32[1,64,2048]{2,1,0:T(8,128)}, u32[]{:S(2)}) %copy-start.5) | copy-done | bytes 524312
  2.7 0.0 copy-start.7
  2.7 1.0 %copy-done.7 = f32[1,64,2048]{2,1,0:T(8,128)S(1)} copy-done((f32[1,64,2048]{2,1,0:T(8,128)S(1)}, f32[1,64,2048]{2,1,0:T(8,128)}, u32[]{:S(2)}) %copy-start.7) | copy-done | bytes 524312
  3.8 0.0 copy-start.9
  3.8 0.7 copy-done.9
  4.5 0.8 shard_map.103
  5.3 1.3 %collective-permute-start.3 = (bf16[66,8,256]{2,1,0:T(8,128)(2,1)S(1)}, bf16[66,8,256]{2,1,0:T(8,128)(2,1)S(1)}, u32[]{:S(2)}, u32[]{:S(2)}) collective-permute-start(bf16[66,8,256]{2,1,0:T(8,128)(2,1)S(1)} %get-tuple-element.42.psf_ref.own_pack), channel_id=1, source_target_pairs={{4,0},{8,4},{12,8},{16,12},{20,16},{24,20},{28,24},{32,28},{36,32}... | collective-permute-start | bytes 811016 | tf_op jit(solution)/shard_map/ppermute | solution.py:386
  6.6 5.0 %collective-permute-start.2 = (bf16[66,8,256]{2,1,0:T(8,128)(2,1)S(1)}, bf16[66,8,256]{2,1,0:T(8,128)(2,1)S(1)}, u32[]{:S(2)}, u32[]{:S(2)}) collective-permute-start(bf16[66,8,256]{2,1,0:T(8,128)(2,1)S(1)} %get-tuple-element.42.psf_ref.own_pack), channel_id=1, source_target_pairs={{0,4},{4,8},{8,12},{12,16},{16,20},{20,24},{24,28},{28,32},{32,36}... | collective-permute-start | bytes 811016 | tf_op jit(solution)/shard_map/ppermute | solution.py:385
  11.6 4.1 %collective-permute-start = (bf16[16,2048]{1,0:T(8,128)(2,1)S(1)}, bf16[16,2048]{1,0:T(8,128)(2,1)S(1)}, u32[]{:S(2)}, u32[]{:S(2)}) collective-permute-start(bf16[16,2048]{1,0:T(8,128)(2,1)S(1)} %get-tuple-element.33), channel_id=1, source_target_pairs={{0,1},{1,2},{2,3},{4,5},{5,6},{6,7},{8,9},{9,10},{10,11},{12,13},{... | collective-permute-start | bytes 196616 | tf_op jit(solution)/shard_map/ppermute | solution.py:383
  15.6 0.0 copy-start.2
  15.7 0.0 copy-start.4
  15.7 2.1 %collective-permute-start.1 = (bf16[16,2048]{1,0:T(8,128)(2,1)S(1)}, bf16[16,2048]{1,0:T(8,128)(2,1)S(1)}, u32[]{:S(2)}, u32[]{:S(2)}) collective-permute-start(bf16[16,2048]{1,0:T(8,128)(2,1)S(1)} %get-tuple-element.34), channel_id=1, source_target_pairs={{1,0},{2,1},{3,2},{5,4},{6,5},{7,6},{9,8},{10,9},{11,10},{13,12},{... | collective-permute-start | bytes 196616 | tf_op jit(solution)/shard_map/ppermute | solution.py:384
  17.7 0.7 shard_map.104.wf
  18.4 0.0 collective-permute-done.lo
  18.4 2.9 %collective-permute-done.1.hi = bf16[16,2048]{1,0:T(8,128)(2,1)S(1)} collective-permute-done((bf16[16,2048]{1,0:T(8,128)(2,1)S(1)}, bf16[16,2048]{1,0:T(8,128)(2,1)S(1)}, u32[]{:S(2)}, u32[]{:S(2)}) %collective-permute-start.1) | collective-permute-done | bytes 65568 | tf_op jit(solution)/shard_map/ppermute | solution.py:384
  21.4 0.0 copy-done.2
  21.4 0.0 copy-done.4
  21.4 2.3 %shard_map.105 = bf16[512,256]{1,0:T(8,128)(2,1)S(1)} custom-call(f32[64,2048]{1,0:T(8,128)S(1)} %bitcast.19, f32[64,2048]{1,0:T(8,128)S(1)} %copy-done.2, bf16[16,2048]{1,0:T(8,128)(2,1)S(1)} %collective-permute-done.lo, bf16[16,2048]{1,0:T(8,128)(2,1)S(1)} %collective-permute-done.1.hi, bf16[2560,256]{1,0:T(8,128)(2,1)S(1)} %shard_map.104.wf, ...), custom_call_target="tpu_custom_call" | custom-call | flops 1000000000 | bytes 4000000 | tf_op jit(solution)/shard_map/pallas_call | solution.py:389
  23.7 0.0 collective-permute-done.3.next_pack
  23.8 0.0 collective-permute-done.2.prev_pack
  23.8 22.4 %all_to_all.20 = bf16[16,32,256]{2,1,0:T(8,128)(2,1)S(1)} all-to-all(bf16[16,32,256]{2,1,0:T(8,128)(2,1)S(1)} %bitcast.17), channel_id=1, replica_groups=mesh['xh'=2,'y'=4,'zh'=4,'zl'=2,'band'=4] {'xh','y','zl'}, dimensions={0} | all-to-all | bytes 524288 | tf_op jit(solution)/shard_map/all_to_all | solution.py:401
  46.2 0.0 copy-start.12
  46.3 0.0 copy-start.11
  46.3 0.0 copy-start.10
  46.3 0.1 collective-permute-start.4
  46.4 1.7 %shard_map.106 = (bf16[2560,768]{1,0:T(8,128)(2,1)S(1)}, bf16[128,256]{1,0:T(8,128)(2,1)S(1)}, bf16[128,256]{1,0:T(8,128)(2,1)S(1)}) custom-call(bf16[66,8,256]{2,1,0:T(8,128)(2,1)S(1)} %collective-permute-done.2.prev_pack, bf16[66,8,256]{2,1,0:T(8,128)(2,1)S(1)} %get-tuple-element.42.psf_ref.own_pack, bf16[66,8,256]{2,1,0:T(8,128)(2,1)S(1)} %collective-permute-done.3.next_pack), custom_call_target="tpu_custom_call" | custom-call | flops 1000000000 | bytes 4000000 | tf_op jit(solution)/shard_map/pallas_call | solution.py:407
  48.1 0.0 copy-start
  48.1 1.9 %copy-done = bf16[2560,768]{1,0:T(8,128)(2,1)} copy-done((bf16[2560,768]{1,0:T(8,128)(2,1)}, bf16[2560,768]{1,0:T(8,128)(2,1)S(1)}, u32[]{:S(2)}) %copy-start) | copy-done | bytes 3932184
  50.0 0.0 copy-done.12
  50.0 0.1 copy.12.mix_ref
  50.1 0.0 copy-done.11
  50.1 0.1 copy.11.kernel_ref
  50.2 2.9 %collective-permute-done.4 = f32[32,256]{1,0:T(8,128)S(1)} collective-permute-done((f32[32,256]{1,0:T(8,128)S(1)}, f32[32,256]{1,0:T(8,128)S(1)}, u32[]{:S(2)}, u32[]{:S(2)}) %collective-permute-start.4) | collective-permute-done | bytes 32800 | tf_op jit(solution)/shard_map/ppermute | solution.py:406
  53.0 0.6 collective-permute-start.5
  53.7 0.0 copy-done.10
  53.7 1.3 %shard_map.107 = (bf16[512,1024]{1,0:T(8,128)(2,1)S(1)}, bf16[512,1024]{1,0:T(8,128)(2,1)S(1)}, bf16[2048,128]{1,0:T(8,128)(2,1)S(1)}) custom-call(bf16[27,16]{1,0:T(8,128)(2,1)S(1)} %copy.11.kernel_ref, f32[1,16]{1,0:T(1,128)S(1)} %bitcast.26, bf16[16,1]{1,0:T(8,128)(2,1)S(1)} %copy.12.mix_ref), custom_call_target="tpu_custom_call" | custom-call | flops 1000000000 | bytes 4000000 | tf_op jit(solution)/shard_map/pallas_call | solution.py:415
  55.0 1.7 %collective-permute-done.5 = f32[32,256]{1,0:T(8,128)S(1)} collective-permute-done((f32[32,256]{1,0:T(8,128)S(1)}, f32[32,256]{1,0:T(8,128)S(1)}, u32[]{:S(2)}, u32[]{:S(2)}) %collective-permute-start.5) | collective-permute-done | bytes 32800 | tf_op jit(solution)/shard_map/ppermute | solution.py:414
  56.7 0.0 copy-start.1
  56.8 11.4 %all_to_all.21 = bf16[16,32,256]{2,1,0:T(8,128)(2,1)S(1)} all-to-all(bf16[16,32,256]{2,1,0:T(8,128)(2,1)S(1)} %broadcast_in_dim.15), channel_id=1, replica_groups=mesh['xh'=2,'y'=4,'zh'=4,'zl'=2,'band'=4] {'xh','y','zl'}, dimensions={0} | all-to-all | bytes 524288 | tf_op jit(solution)/shard_map/all_to_all | solution.py:423
  68.2 0.4 shard_map.109
  68.6 6.1 %collective-permute-start.6 = (bf16[256,256]{1,0:T(8,128)(2,1)S(1)}, bf16[256,256]{1,0:T(8,128)(2,1)S(1)}, u32[]{:S(2)}, u32[]{:S(2)}) collective-permute-start(bf16[256,256]{1,0:T(8,128)(2,1)S(1)} %get-tuple-element.54), channel_id=1, source_target_pairs={{0,1},{1,2},{2,3},{4,5},{5,6},{6,7},{8,9},{9,10},{10,11},{12,13},{... | collective-permute-start | bytes 393224 | tf_op jit(solution)/shard_map/ppermute | solution.py:427
  74.7 0.0 copy-start.6
  74.7 0.0 copy-start.8
  74.7 2.2 %collective-permute-start.7 = (bf16[256,256]{1,0:T(8,128)(2,1)S(1)}, bf16[256,256]{1,0:T(8,128)(2,1)S(1)}, u32[]{:S(2)}, u32[]{:S(2)}) collective-permute-start(bf16[256,256]{1,0:T(8,128)(2,1)S(1)} %get-tuple-element.55), channel_id=1, source_target_pairs={{1,0},{2,1},{3,2},{5,4},{6,5},{7,6},{9,8},{10,9},{11,10},{13,12},{... | collective-permute-start | bytes 393224 | tf_op jit(solution)/shard_map/ppermute | solution.py:428
  76.9 0.0 copy-done.1
  76.9 2.7 %shard_map.108.moves = f32[512,768]{1,0:T(8,128)S(1)} custom-call(bf16[512,256]{1,0:T(8,128)(2,1)S(1)} %bitcast.15, bf16[2560,768]{1,0:T(8,128)(2,1)S(1)} %copy-done.1), custom_call_target="tpu_custom_call" | custom-call | flops 1000000000 | bytes 4000000 | tf_op jit(solution)/shard_map/pallas_call | solution.py:429
  79.7 0.0 collective-permute-done.6.lo
  79.7 1.4 %collective-permute-done.7.hi = bf16[256,256]{1,0:T(8,128)(2,1)S(1)} collective-permute-done((bf16[256,256]{1,0:T(8,128)(2,1)S(1)}, bf16[256,256]{1,0:T(8,128)(2,1)S(1)}, u32[]{:S(2)}, u32[]{:S(2)}) %collective-permute-start.7) | collective-permute-done | bytes 131104 | tf_op jit(solution)/shard_map/ppermute | solution.py:428
  81.1 0.0 copy-done.6
  81.1 0.0 copy-done.8
  81.1 9.8 %shard_map.110 = (f32[64,2048]{1,0:T(8,128)}, f32[64,2048]{1,0:T(8,128)}, f32[64,2048]{1,0:T(8,128)}) custom-call(f32[64,2048]{1,0:T(8,128)S(1)} %bitcast.20, f32[64,2048]{1,0:T(8,128)S(1)} %bitcast.22, f32[64,2048]{1,0:T(8,128)S(1)} %bitcast.24, bf16[512,256]{1,0:T(8,128)(2,1)S(1)} %bitcast.16, f32[512,768]{1,0:T(8,128)S(1)} %shard_map.108.moves, ...), custom_call_target="tpu_custom_call" | custom-call | flops 10000000000 | bytes 4000000 | tf_op jit(solution)/shard_map/pallas_call | solution.py:435
  (4 shorter events, 0.1 us)
Async XLA Ops:
  0.6 1.0 %copy-start.3 = (f32[1,64,2048]{2,1,0:T(8,128)S(1)}, f32[1,64,2048]{2,1,0:T(8,128)}, u32[]{:S(2)}) copy-start(f32[1,64,2048]{2,1,0:T(8,128)} %param.8) | copy-start | bytes 1572868
  1.7 1.0 %copy-start.5 = (f32[1,64,2048]{2,1,0:T(8,128)S(1)}, f32[1,64,2048]{2,1,0:T(8,128)}, u32[]{:S(2)}) copy-start(f32[1,64,2048]{2,1,0:T(8,128)} %param.9) | copy-start | bytes 1572868
  2.7 1.0 %copy-start.7 = (f32[1,64,2048]{2,1,0:T(8,128)S(1)}, f32[1,64,2048]{2,1,0:T(8,128)}, u32[]{:S(2)}) copy-start(f32[1,64,2048]{2,1,0:T(8,128)} %param.10) | copy-start | bytes 1572868
  3.8 0.7 copy-start.9
  5.3 18.5 %collective-permute-start.3 = (bf16[66,8,256]{2,1,0:T(8,128)(2,1)S(1)}, bf16[66,8,256]{2,1,0:T(8,128)(2,1)S(1)}, u32[]{:S(2)}, u32[]{:S(2)}) collective-permute-start(bf16[66,8,256]{2,1,0:T(8,128)(2,1)S(1)} %get-tuple-element.42.psf_ref.own_pack), channel_id=1, source_target_pairs={{4,0},{8,4},{12,8},{16,12},{20,16},{24,20},{28,24},{32,28},{36,32}... | collective-permute-start | bytes 811016 | tf_op jit(solution)/shard_map/ppermute | solution.py:386
  6.6 17.2 %collective-permute-start.2 = (bf16[66,8,256]{2,1,0:T(8,128)(2,1)S(1)}, bf16[66,8,256]{2,1,0:T(8,128)(2,1)S(1)}, u32[]{:S(2)}, u32[]{:S(2)}) collective-permute-start(bf16[66,8,256]{2,1,0:T(8,128)(2,1)S(1)} %get-tuple-element.42.psf_ref.own_pack), channel_id=1, source_target_pairs={{0,4},{4,8},{8,12},{12,16},{16,20},{20,24},{24,28},{28,32},{32,36}... | collective-permute-start | bytes 811016 | tf_op jit(solution)/shard_map/ppermute | solution.py:385
  11.6 6.9 %collective-permute-start = (bf16[16,2048]{1,0:T(8,128)(2,1)S(1)}, bf16[16,2048]{1,0:T(8,128)(2,1)S(1)}, u32[]{:S(2)}, u32[]{:S(2)}) collective-permute-start(bf16[16,2048]{1,0:T(8,128)(2,1)S(1)} %get-tuple-element.33), channel_id=1, source_target_pairs={{0,1},{1,2},{2,3},{4,5},{5,6},{6,7},{8,9},{9,10},{10,11},{12,13},{... | collective-permute-start | bytes 196616 | tf_op jit(solution)/shard_map/ppermute | solution.py:383
  15.6 5.7 %copy-start.2 = (f32[64,2048]{1,0:T(8,128)S(1)}, f32[64,2048]{1,0:T(8,128)}, u32[]{:S(2)}) copy-start(f32[64,2048]{1,0:T(8,128)} %measured.1) | copy-start | bytes 1572868
  15.7 5.7 %copy-start.4 = (f32[1,64,2048]{2,1,0:T(8,128)S(1)}, f32[1,64,2048]{2,1,0:T(8,128)}, u32[]{:S(2)}) copy-start(f32[1,64,2048]{2,1,0:T(8,128)} %param.8) | copy-start | bytes 1572868
  15.7 5.7 %collective-permute-start.1 = (bf16[16,2048]{1,0:T(8,128)(2,1)S(1)}, bf16[16,2048]{1,0:T(8,128)(2,1)S(1)}, u32[]{:S(2)}, u32[]{:S(2)}) collective-permute-start(bf16[16,2048]{1,0:T(8,128)(2,1)S(1)} %get-tuple-element.34), channel_id=1, source_target_pairs={{1,0},{2,1},{3,2},{5,4},{6,5},{7,6},{9,8},{10,9},{11,10},{13,12},{... | collective-permute-start | bytes 196616 | tf_op jit(solution)/shard_map/ppermute | solution.py:384
  46.2 3.7 %copy-start.12 = (bf16[16]{0:T(256)(128)(2,1)S(1)}, bf16[16]{0:T(256)(128)(2,1)}, u32[]{:S(2)}) copy-start(bf16[16]{0:T(256)(128)(2,1)} %param.15) | copy-start | bytes 100
  46.3 3.8 %copy-start.11 = (bf16[27,16]{0,1:T(8,128)(2,1)S(1)}, bf16[27,16]{0,1:T(8,128)(2,1)}, u32[]{:S(2)}) copy-start(bf16[27,16]{0,1:T(8,128)(2,1)} %param.13) | copy-start | bytes 2596
  46.3 7.4 %copy-start.10 = (f32[16]{0:T(128)S(1)}, f32[16]{0:T(128)}, u32[]{:S(2)}) copy-start(f32[16]{0:T(128)} %param.14) | copy-start | bytes 196
  46.3 6.8 %collective-permute-start.4 = (f32[32,256]{1,0:T(8,128)S(1)}, f32[32,256]{1,0:T(8,128)S(1)}, u32[]{:S(2)}, u32[]{:S(2)}) collective-permute-start(f32[32,256]{1,0:T(8,128)S(1)} %convert_reduce_fusion), channel_id=1, source_target_pairs={{0,16},{8,24},{16,0},{24,8},{1,17},{9,25},{17,1},{25,9},{2,18},{10... | collective-permute-start | bytes 98312 | tf_op jit(solution)/shard_map/ppermute | solution.py:406
  48.1 1.9 %copy-start = (bf16[2560,768]{1,0:T(8,128)(2,1)}, bf16[2560,768]{1,0:T(8,128)(2,1)S(1)}, u32[]{:S(2)}) copy-start(bf16[2560,768]{1,0:T(8,128)(2,1)S(1)} %get-tuple-element.51.wg) | copy-start | bytes 11796484
  53.0 3.7 %collective-permute-start.5 = (f32[32,256]{1,0:T(8,128)S(1)}, f32[32,256]{1,0:T(8,128)S(1)}, u32[]{:S(2)}, u32[]{:S(2)}) collective-permute-start(f32[32,256]{1,0:T(8,128)S(1)} %add.6), channel_id=1, source_target_pairs={{0,8},{8,0},{16,24},{24,16},{1,9},{9,1},{17,25},{25,17},{2,10},{10... | collective-permute-start | bytes 98312 | tf_op jit(solution)/shard_map/ppermute | solution.py:414
  56.7 20.2 %copy-start.1 = (bf16[2560,768]{1,0:T(8,128)(2,1)S(1)}, bf16[2560,768]{1,0:T(8,128)(2,1)}, u32[]{:S(2)}) copy-start(bf16[2560,768]{1,0:T(8,128)(2,1)} %copy-done) | copy-start | bytes 11796484
  68.6 11.1 %collective-permute-start.6 = (bf16[256,256]{1,0:T(8,128)(2,1)S(1)}, bf16[256,256]{1,0:T(8,128)(2,1)S(1)}, u32[]{:S(2)}, u32[]{:S(2)}) collective-permute-start(bf16[256,256]{1,0:T(8,128)(2,1)S(1)} %get-tuple-element.54), channel_id=1, source_target_pairs={{0,1},{1,2},{2,3},{4,5},{5,6},{6,7},{8,9},{9,10},{10,11},{12,13},{... | collective-permute-start | bytes 393224 | tf_op jit(solution)/shard_map/ppermute | solution.py:427
  74.7 6.4 %copy-start.6 = (f32[1,64,2048]{2,1,0:T(8,128)S(1)}, f32[1,64,2048]{2,1,0:T(8,128)}, u32[]{:S(2)}) copy-start(f32[1,64,2048]{2,1,0:T(8,128)} %param.9) | copy-start | bytes 1572868
  74.7 6.4 %copy-start.8 = (f32[1,64,2048]{2,1,0:T(8,128)S(1)}, f32[1,64,2048]{2,1,0:T(8,128)}, u32[]{:S(2)}) copy-start(f32[1,64,2048]{2,1,0:T(8,128)} %param.10) | copy-start | bytes 1572868
  74.7 6.4 %collective-permute-start.7 = (bf16[256,256]{1,0:T(8,128)(2,1)S(1)}, bf16[256,256]{1,0:T(8,128)(2,1)S(1)}, u32[]{:S(2)}, u32[]{:S(2)}) collective-permute-start(bf16[256,256]{1,0:T(8,128)(2,1)S(1)} %get-tuple-element.55), channel_id=1, source_target_pairs={{1,0},{2,1},{3,2},{5,4},{6,5},{7,6},{9,8},{10,9},{11,10},{13,12},{... | collective-permute-start | bytes 393224 | tf_op jit(solution)/shard_map/ppermute | solution.py:428

commit v3 on v2

--- a/solution.py
+++ b/solution.py
@@ -55,7 +55,7 @@
 TURN = (2, 0, 4)
 
 
-def forward_weights_kernel(psf_ref, wf_ref, strips):
+def forward_weights_kernel(psf_ref, wf_ref, same_ref, strips):
     def put(at, value):
         wf_ref[at : at + value.shape[0], :] = value
 
@@ -148,15 +148,12 @@
     return jnp.concatenate([nat[t, pl.ds(at + 4 * h + m, 8, stride=8), :] for m in range(4)], axis=1)
 
 
-def start_kernel(planes, denoised, dual, psf_ref, down_ref, up_ref, pack_ref, low_ref, swap_ref, nat, lhs):
+def start_kernel(start, psf_ref, pack_ref, low_ref, swap_ref, nat, lhs):
     psf = jnp.pad(psf_ref[...].astype(F32), ((0, 1), (0, 97))).astype(BF)
-    down_ref[...] = planes[48:64, :].astype(BF)
-    up_ref[...] = planes[0:16, :].astype(BF)
     swap = swap_matrix()
     swap_ref[...] = swap
     for t in range(16):
-        c = slice(128 * t, 128 * t + 128)
-        nat[t] = base(planes[:, c], denoised[:, c], dual[:, c])
+        nat[t] = start[:, 128 * t : 128 * t + 128]
     for t in range(16):
         rows = jnp.concatenate([octets(nat, t, 0, 0), octets(nat, t, 1, 0)], axis=0)
         lhs[0, 16 * t : 16 * t + 16, :], lhs[1, 16 * t : 16 * t + 16, :] = split(rows)
@@ -226,7 +223,7 @@
 
 
 def final_kernel(planes, denoised, dual, res, moves, lo, hi, own_low, own_pack, prev_pack, next_pack, wg, even, odd, mx,
-                 swap, np_ref, nd_ref, du_ref, main, lhs, vol, wins, nat, turn, mine):
+                 swap, np_ref, nd_ref, du_ref, main, lhs, vol, wins, nat, turn, mine, held, sems):
     main[0] = jnp.zeros((16, 256), F32)
     main[65] = jnp.zeros((16, 256), F32)
     main[1:65, 2:10, :] = res[...].astype(F32).reshape(64, 8, 256)
@@ -337,25 +334,40 @@
                 for m in range(4):
                     at = 16 * t + 8 * h
                     nat[f, t, pl.ds(4 * h + m, 8, stride=8), :] = moved[at : at + 8, 128 * m : 128 * m + 128]
-    for t in range(16):
-        c = slice(128 * t, 128 * t + 128)
-        x = planes[:, c]
-        z = dual[:, c]
-        moved = (x - STEP * (HALF * (x - (denoised[:, c] - z)))) + nat[0, t]
-        cleaned = (moved + z) - nat[1, t]
-        np_ref[:, c] = moved
-        nd_ref[:, c] = cleaned
-        du_ref[:, c] = z + moved - cleaned
-
-
-def call(body, outs, scratch, n_in, flops=1_000_000_000, vmem=20, specs=None):
+    copies = []
+
+    def send(a, ref, c):
+        copy = pltpu.make_async_copy(held.at[a, c], ref.at[:, pl.ds(512 * c, 512)], sems.at[a, c])
+        copy.start()
+        copies.append(copy)
+
+    for c in range(4):
+        for t in range(4):
+            cut = slice(512 * c + 128 * t, 512 * c + 128 * t + 128)
+            at = slice(128 * t, 128 * t + 128)
+            x = planes[:, cut]
+            z = dual[:, cut]
+            moved = (x - STEP * (HALF * (x - (denoised[:, cut] - z)))) + nat[0, 4 * c + t]
+            cleaned = (moved + z) - nat[1, 4 * c + t]
+            held[0, c, :, at] = moved
+            held[1, c, :, at] = cleaned
+            held[2, c, :, at] = z + moved - cleaned
+        for a, ref in enumerate((np_ref, nd_ref, du_ref)):
+            send(a, ref, c)
+    for copy in copies:
+        copy.wait()
+
+
+def call(body, outs, scratch, n_in, flops=1_000_000_000, vmem=20, far_out=False, aliases=None):
     whole = pl.BlockSpec(memory_space=pltpu.VMEM)
+    distant = pl.BlockSpec(memory_space=pltpu.HBM)
     return pl.pallas_call(
         body,
         out_shape=outs,
-        in_specs=specs or [whole] * n_in,
-        out_specs=[whole] * len(outs),
+        in_specs=[whole] * n_in,
+        out_specs=[distant if far_out else whole] * len(outs),
         scratch_shapes=scratch,
+        input_output_aliases=aliases or {},
         compiler_params=pltpu.CompilerParams(vmem_limit_bytes=vmem * MIB),
         cost_estimate=pl.CostEstimate(flops=flops, bytes_accessed=4_000_000, transcendentals=0),
     )
@@ -374,18 +386,26 @@
     later = [(i, i + 1) for i in range(63)]
     earlier = [(i + 1, i) for i in range(63)]
 
-    to_down, to_up, packed, low, swap = call(
+    lo = lax.ppermute(x[48:64].astype(BF), "band", down)
+    hi = lax.ppermute(x[0:16].astype(BF), "band", up)
+    packed, low, swap = call(
         start_kernel,
-        [out((16, 2048), BF), out((16, 2048), BF), out((66, 8, 256), BF), out((64, 8, 256), BF), out((512, 512), BF)],
+        [out((66, 8, 256), BF), out((64, 8, 256), BF), out((512, 512), BF)],
         [pltpu.VMEM((16, 64, 128), F32), pltpu.VMEM((2, 256, 512), BF)],
-        4,
-    )(x, d, z, psf[0])
-    lo = lax.ppermute(to_down, "band", down)
-    hi = lax.ppermute(to_up, "band", up)
+        2,
+        vmem=12,
+    )(base(x, d, z), psf[0])
+    strips = pltpu.VMEM((4, 64, 1536), BF)
+    wf, packed = call(
+        forward_weights_kernel,
+        [out((2560, 256), BF), out((66, 8, 256), BF)],
+        [strips],
+        1,
+        vmem=8,
+        aliases={0: 1},
+    )(packed)
     prev_pack = lax.ppermute(packed, depth, later)
     next_pack = lax.ppermute(packed, depth, earlier)
-    strips = pltpu.VMEM((4, 64, 1536), BF)
-    (wf,) = call(forward_weights_kernel, [out((2560, 256), BF)], [strips], 1)(packed)
     (part,) = call(
         forward_kernel,
         [out((512, 256), BF)],
@@ -399,30 +419,27 @@
     )(x, measured, lo, hi, wf, swap)
     part, prev_pack, next_pack = lax.optimization_barrier((part, prev_pack, next_pack))
     got = lax.all_to_all(part, group, 0, 0, tiled=True)
-    got, prev_pack, own_pack, next_pack, kernel, bias, mix = lax.optimization_barrier(
-        (got, prev_pack, packed, next_pack, kernel, bias.reshape(1, 16), mix.reshape(16, 1))
-    )
     mine = jnp.sum(got.reshape(16, 32, 256).astype(F32), axis=0)
-    other = lax.ppermute(mine, "zh", [(a, a ^ 2) for a in range(4)])
+    others = [lax.ppermute(mine, "zh", [(a, a ^ bits) for a in range(4)]) for bits in (2, 1, 3)]
     wg, edge_down, edge_up = call(
         back_weights_kernel,
         [out((2560, 768), BF), out((128, 256), BF), out((128, 256), BF)],
         [strips, pltpu.VMEM((64, 8, 256), F32)],
         3,
-    )(prev_pack, own_pack, next_pack)
-    mine, wg = lax.optimization_barrier((mine + other, wg))
-    other = lax.ppermute(mine, "zh", [(a, a ^ 1) for a in range(4)])
+        vmem=10,
+    )(prev_pack, packed, next_pack)
     even, odd, mx = call(
         denoiser_weights_kernel,
         [out((512, 1024), BF), out((512, 1024), BF), out((2048, 128), BF)],
         [pltpu.VMEM((32, 1024), F32), pltpu.VMEM((2, 128, 1024), F32)],
         3,
-    )(kernel, bias, mix)
-    mine, even = lax.optimization_barrier((mine + other, even))
+        vmem=8,
+    )(kernel, bias.reshape(1, 16), mix.reshape(16, 1))
+    mine = (mine + others[0]) + (others[1] + others[2])
     wide = jnp.broadcast_to(mine.astype(BF)[None], (16, 32, 256)).reshape(512, 256)
     res = lax.all_to_all(wide, group, 0, 0, tiled=True)
     rim_down, rim_up = call(
-        rims_kernel, [out((256, 256), BF), out((256, 256), BF)], [pltpu.VMEM((64, 8, 256), F32)], 3
+        rims_kernel, [out((256, 256), BF), out((256, 256), BF)], [pltpu.VMEM((64, 8, 256), F32)], 3, vmem=4
     )(res, edge_down, edge_up)
     rim_lo = lax.ppermute(rim_down, "band", down)
     rim_hi = lax.ppermute(rim_up, "band", up)
@@ -431,6 +448,7 @@
         [out((512, 768), F32)],
         [pltpu.VMEM((66, 16, 256), F32), pltpu.VMEM((512, 2560), BF)],
         2,
+        vmem=14,
     )(res, wg)
     outs = call(
         final_kernel,
@@ -443,10 +461,13 @@
             pltpu.VMEM((2, 16, 64, 128), F32),
             pltpu.VMEM((2, 2, 256, 512), BF),
             pltpu.VMEM((64, 8, 256), F32),
+            pltpu.VMEM((3, 4, 64, 512), F32),
+            pltpu.SemaphoreType.DMA((3, 4)),
         ],
         16,
         flops=10_000_000_000,
-        vmem=36,
+        vmem=32,
+        far_out=True,
     )(x, d, z, res, moves, rim_lo, rim_hi, low, packed, prev_pack, next_pack, wg, even, odd, mx, swap)
     return tuple(o[None] for o in outs)
 

time: 91.4 us -> 88 us (0.963)
  blocking collectives: 33.9 us -> 20.4 us
  starting transfers between devices: 21.5 us -> 31.8 us
  local copies, waits for them, and re-layouts: 5.93 us -> 2.85 us
  other arithmetic: 0.05 us -> 1.54 us
  waiting for transfers between devices: 8.95 us -> 10.3 us
    all_to_all x1 -> x0, blocking collectives: 11.4 us -> none  [shards(): res = lax.all_to_all(wide, group, 0, 0, tiled=True)]
    ppermute x4 -> x5, starting transfers between devices: 6.86 us -> 12.6 us  [the longest x3 6 us: shards(): lax.ppermute(mine, 'zh', [(a, a ^ bits) for a in range(4)])]
    all_to_all x0 -> x1, waiting for transfers between devices: none -> 3.87 us  [shards(): res = lax.all_to_all(wide, group, 0, 0, tiled=True)]
    unnamed x26 -> x21, local copies, waits for them, and re-layouts: 5.72 us -> 2.01 us
    all_to_all x0 -> x1, starting transfers between devices: none -> 3.53 us  [shards(): res = lax.all_to_all(wide, group, 0, 0, tiled=True)]
    all_to_all x1, blocking collectives: 22.4 us -> 20.4 us  [shards(): got = lax.all_to_all(part, group, 0, 0, tiled=True)]
    add x2 -> x1, other arithmetic: 0.01 us -> 1.46 us  [base(): return planes - STEP * (HALF * (planes - (denoised - dual))) + dual]
    ppermute x1, waiting for transfers between devices: 1.44 us -> 0.07 us  [shards(): rim_hi = lax.ppermute(rim_up, 'band', up)]
  transfers between devices with their start and end apart: 8 -> 10, of which waited for: 4 -> 5; matrix products, arithmetic and copies ran while one was open for 0% -> 0% of each run, Pallas kernels for 10% -> 9%
where the time goes in v3:
time: 88 us; the launch traced here: 87.6 us
  starting transfers between devices  31.8 us (36%)
  blocking collectives  20.4 us (23%)
  Pallas kernels  19.6 us (22%)
  waiting for transfers between devices  10.3 us (12%)
  local copies, waits for them, and re-layouts  2.85 us (3%)
  other arithmetic  1.54 us (2%)
  between operations  1.06 us (1%)
    all_to_all x1, blocking collectives, shards(): got = lax.all_to_all(part, group, 0, 0, tiled=True)  20.4 us
    pallas_call x1, Pallas kernels, shards(): call(final_kernel, [out((64, 2048), F32)] * 3, [pltpu.VMEM((66, 16, 256),...  9.86 us
    ppermute x1, starting transfers between devices, shards(): rim_lo = lax.ppermute(rim_down, 'band', down)  7.29 us
    ppermute x3, starting transfers between devices, shards(): lax.ppermute(mine, 'zh', [(a, a ^ bits) for a in range(4)])  6 us
    ppermute x1, starting transfers between devices, shards(): prev_pack = lax.ppermute(packed, depth, later)  5.01 us
    ppermute x3, waiting for transfers between devices, shards(): lax.ppermute(mine, 'zh', [(a, a ^ bits) for a in range(4)])  5 us
    ppermute x1, starting transfers between devices, shards(): hi = lax.ppermute(x[0:16].astype(BF), 'band', up)  4.7 us
    all_to_all x1, waiting for transfers between devices, shards(): res = lax.all_to_all(wide, group, 0, 0, tiled=True)  3.87 us
  transfers between devices with their start and end apart: 10, of which 5 were waited for; matrix products, arithmetic and copies ran while one was open for 0% of the time, Pallas kernels for 9%

profile of v3, /device:TPU:1, one launch (start us, length us, event | category | flops | bytes accessed | tf_op | source)
XLA Modules:
  0.0 87.6 jit_solution(14824635155381462793)
XLA Ops:
  0.6 0.0 copy-start.6
  0.6 1.5 %subtract_add_fusion.start = f32[64,2048]{1,0:T(8,128)S(1)} fusion(f32[1,64,2048]{2,1,0:T(8,128)} %param.10, f32[1,64,2048]{2,1,0:T(8,128)} %param.9, f32[1,64,2048]{2,1,0:T(8,128)} %param.8), kind=kLoop, calls=%fused_computation.1 | loop fusion | flops 655360 | bytes 2097152 | tf_op jit(solution)/shard_map/add | solution.py:144
  2.1 0.0 copy-done.6
  2.1 0.6 shard_map.103
  2.7 0.0 copy-start.2
  2.7 0.0 copy-start.5
  2.8 0.7 shard_map.104
  3.5 1.3 %collective-permute-start.3 = (bf16[66,8,256]{2,1,0:T(8,128)(2,1)S(1)}, bf16[66,8,256]{2,1,0:T(8,128)(2,1)S(1)}, u32[]{:S(2)}, u32[]{:S(2)}) collective-permute-start(bf16[66,8,256]{2,1,0:T(8,128)(2,1)S(1)} %get-tuple-element.25.own_pack), channel_id=1, source_target_pairs={{4,0},{8,4},{12,8},{16,12},{20,16},{24,20},{28,24},{32,28},{36,32}... | collective-permute-start | bytes 811016 | tf_op jit(solution)/shard_map/ppermute | solution.py:408
  4.8 5.0 %collective-permute-start.2 = (bf16[66,8,256]{2,1,0:T(8,128)(2,1)S(1)}, bf16[66,8,256]{2,1,0:T(8,128)(2,1)S(1)}, u32[]{:S(2)}, u32[]{:S(2)}) collective-permute-start(bf16[66,8,256]{2,1,0:T(8,128)(2,1)S(1)} %get-tuple-element.25.own_pack), channel_id=1, source_target_pairs={{0,4},{4,8},{8,12},{12,16},{16,20},{20,24},{24,28},{28,32},{32,36}... | collective-permute-start | bytes 811016 | tf_op jit(solution)/shard_map/ppermute | solution.py:407
  9.8 0.0 copy-done.2
  9.8 4.7 %collective-permute-start.1 = (bf16[16,2048]{1,0:T(8,128)(2,1)S(1)}, bf16[16,2048]{1,0:T(8,128)(2,1)S(1)}, u32[]{:S(2)}, u32[]{:S(2)}) collective-permute-start(bf16[16,2048]{1,0:T(8,128)(2,1)S(1)} %get-tuple-element.41), channel_id=1, source_target_pairs={{1,0},{2,1},{3,2},{5,4},{6,5},{7,6},{9,8},{10,9},{11,10},{13,12},{... | collective-permute-start | bytes 196616 | tf_op jit(solution)/shard_map/ppermute | solution.py:390
  14.5 1.9 %collective-permute-start = (bf16[16,2048]{1,0:T(8,128)(2,1)S(1)}, bf16[16,2048]{1,0:T(8,128)(2,1)S(1)}, u32[]{:S(2)}, u32[]{:S(2)}) collective-permute-start(bf16[16,2048]{1,0:T(8,128)(2,1)S(1)} %get-tuple-element.42), channel_id=1, source_target_pairs={{0,1},{1,2},{2,3},{4,5},{5,6},{6,7},{8,9},{9,10},{10,11},{12,13},{... | collective-permute-start | bytes 196616 | tf_op jit(solution)/shard_map/ppermute | solution.py:389
  16.5 0.0 collective-permute-done.1.hi
  16.5 1.3 %collective-permute-done.lo = bf16[16,2048]{1,0:T(8,128)(2,1)S(1)} collective-permute-done((bf16[16,2048]{1,0:T(8,128)(2,1)S(1)}, bf16[16,2048]{1,0:T(8,128)(2,1)S(1)}, u32[]{:S(2)}, u32[]{:S(2)}) %collective-permute-start) | collective-permute-done | bytes 65568 | tf_op jit(solution)/shard_map/ppermute | solution.py:389
  17.8 0.0 copy-done.5
  17.8 2.3 %shard_map.105 = bf16[512,256]{1,0:T(8,128)(2,1)S(1)} custom-call(f32[64,2048]{1,0:T(8,128)S(1)} %bitcast.18, f32[64,2048]{1,0:T(8,128)S(1)} %copy-done.5, bf16[16,2048]{1,0:T(8,128)(2,1)S(1)} %collective-permute-done.lo, bf16[16,2048]{1,0:T(8,128)(2,1)S(1)} %collective-permute-done.1.hi, bf16[2560,256]{1,0:T(8,128)(2,1)S(1)} %get-tuple-element.23.wf, ...), custom_call_target="tpu_custom_call" | custom-call | flops 1000000000 | bytes 4000000 | tf_op jit(solution)/shard_map/pallas_call | solution.py:409
  20.1 0.0 copy-start.9
  20.1 0.0 copy-start.8
  20.2 0.0 collective-permute-done.3.next_pack
  20.2 0.0 collective-permute-done.2.prev_pack
  20.2 20.4 %all_to_all.17 = bf16[16,32,256]{2,1,0:T(8,128)(2,1)S(1)} all-to-all(bf16[16,32,256]{2,1,0:T(8,128)(2,1)S(1)} %bitcast.25), channel_id=1, replica_groups=mesh['xh'=2,'y'=4,'zh'=4,'zl'=2,'band'=4] {'xh','y','zl'}, dimensions={0} | all-to-all | bytes 524288 | tf_op jit(solution)/shard_map/all_to_all | solution.py:421
  40.6 3.8 %collective-permute-start.6 = (f32[32,256]{1,0:T(8,128)S(1)}, f32[32,256]{1,0:T(8,128)S(1)}, u32[]{:S(2)}, u32[]{:S(2)}) collective-permute-start(f32[32,256]{1,0:T(8,128)S(1)} %convert_reduce_fusion), channel_id=1, source_target_pairs={{0,24},{8,16},{16,8},{24,0},{1,25},{9,17},{17,9},{25,1},{2,26},{10... | collective-permute-start | bytes 98312 | tf_op jit(solution)/shard_map/ppermute | solution.py:423
  44.4 0.0 collective-permute-start.5
  44.4 2.2 %collective-permute-start.4 = (f32[32,256]{1,0:T(8,128)S(1)}, f32[32,256]{1,0:T(8,128)S(1)}, u32[]{:S(2)}, u32[]{:S(2)}) collective-permute-start(f32[32,256]{1,0:T(8,128)S(1)} %convert_reduce_fusion), channel_id=1, source_target_pairs={{0,16},{8,24},{16,0},{24,8},{1,17},{9,25},{17,1},{25,9},{2,18},{10... | collective-permute-start | bytes 98312 | tf_op jit(solution)/shard_map/ppermute | solution.py:423
  46.6 0.0 collective-permute-done.6
  46.6 1.5 %collective-permute-done.5 = f32[32,256]{1,0:T(8,128)S(1)} collective-permute-done((f32[32,256]{1,0:T(8,128)S(1)}, f32[32,256]{1,0:T(8,128)S(1)}, u32[]{:S(2)}, u32[]{:S(2)}) %collective-permute-start.5) | collective-permute-done | bytes 32800 | tf_op jit(solution)/shard_map/ppermute | solution.py:423
  48.1 3.5 %collective-permute-done.4 = f32[32,256]{1,0:T(8,128)S(1)} collective-permute-done((f32[32,256]{1,0:T(8,128)S(1)}, f32[32,256]{1,0:T(8,128)S(1)}, u32[]{:S(2)}, u32[]{:S(2)}) %collective-permute-start.4) | collective-permute-done | bytes 32800 | tf_op jit(solution)/shard_map/ppermute | solution.py:423
  51.6 0.7 broadcast_in_dim.15
  52.4 3.5 %all-to-all-start.1 = ((bf16[16,32,256]{2,1,0:T(8,128)(2,1)}), bf16[16,32,256]{2,1,0:T(8,128)(2,1)S(1)}, u32[]{:S(2)}, u32[]{:S(2)}) async-start(bf16[16,32,256]{2,1,0:T(8,128)(2,1)} %broadcast_in_dim.15), calls=%async_computation.1 | async-start | bytes 524288 | tf_op jit(solution)/shard_map/all_to_all | solution.py:440
  55.9 0.0 copy-done.9
  55.9 0.1 copy.13.mix_ref
  56.0 0.0 copy-done.8
  56.0 0.1 copy.12.kernel_ref
  56.1 0.0 copy-start.7
  56.1 1.7 %shard_map.106 = (bf16[2560,768]{1,0:T(8,128)(2,1)S(1)}, bf16[128,256]{1,0:T(8,128)(2,1)S(1)}, bf16[128,256]{1,0:T(8,128)(2,1)S(1)}) custom-call(bf16[66,8,256]{2,1,0:T(8,128)(2,1)S(1)} %collective-permute-done.2.prev_pack, bf16[66,8,256]{2,1,0:T(8,128)(2,1)S(1)} %get-tuple-element.25.own_pack, bf16[66,8,256]{2,1,0:T(8,128)(2,1)S(1)} %collective-permute-done.3.next_pack), custom_call_target="tpu_custom_call" | custom-call | flops 1000000000 | bytes 4000000 | tf_op jit(solution)/shard_map/pallas_call | solution.py:424
  57.8 0.0 copy-start
  57.8 1.9 %copy-done = bf16[2560,768]{1,0:T(8,128)(2,1)} copy-done((bf16[2560,768]{1,0:T(8,128)(2,1)}, bf16[2560,768]{1,0:T(8,128)(2,1)S(1)}, u32[]{:S(2)}) %copy-start) | copy-done | bytes 3932184
  59.7 3.9 %all-to-all-done.1 = bf16[16,32,256]{2,1,0:T(8,128)(2,1)S(1)} async-done(((bf16[16,32,256]{2,1,0:T(8,128)(2,1)}), bf16[16,32,256]{2,1,0:T(8,128)(2,1)S(1)}, u32[]{:S(2)}, u32[]{:S(2)}) %all-to-all-start.1) | async-done | bytes 262176 | tf_op jit(solution)/shard_map/all_to_all | solution.py:440
  63.6 0.0 copy-start.1
  63.6 0.4 shard_map.108
  64.0 7.3 %collective-permute-start.7 = (bf16[256,256]{1,0:T(8,128)(2,1)S(1)}, bf16[256,256]{1,0:T(8,128)(2,1)S(1)}, u32[]{:S(2)}, u32[]{:S(2)}) collective-permute-start(bf16[256,256]{1,0:T(8,128)(2,1)S(1)} %get-tuple-element.32), channel_id=1, source_target_pairs={{0,1},{1,2},{2,3},{4,5},{5,6},{6,7},{8,9},{9,10},{10,11},{12,13},{... | collective-permute-start | bytes 393224 | tf_op jit(solution)/shard_map/ppermute | solution.py:444
  71.2 2.1 %collective-permute-start.8 = (bf16[256,256]{1,0:T(8,128)(2,1)S(1)}, bf16[256,256]{1,0:T(8,128)(2,1)S(1)}, u32[]{:S(2)}, u32[]{:S(2)}) collective-permute-start(bf16[256,256]{1,0:T(8,128)(2,1)S(1)} %get-tuple-element.33), channel_id=1, source_target_pairs={{1,0},{2,1},{3,2},{5,4},{6,5},{7,6},{9,8},{10,9},{11,10},{13,12},{... | collective-permute-start | bytes 393224 | tf_op jit(solution)/shard_map/ppermute | solution.py:445
  73.4 0.0 copy-done.7
  73.4 1.3 %shard_map.109 = (bf16[512,1024]{1,0:T(8,128)(2,1)S(1)}, bf16[512,1024]{1,0:T(8,128)(2,1)S(1)}, bf16[2048,128]{1,0:T(8,128)(2,1)S(1)}) custom-call(bf16[27,16]{1,0:T(8,128)(2,1)S(1)} %copy.12.kernel_ref, f32[1,16]{1,0:T(1,128)S(1)} %bitcast.27, bf16[16,1]{1,0:T(8,128)(2,1)S(1)} %copy.13.mix_ref), custom_call_target="tpu_custom_call" | custom-call | flops 1000000000 | bytes 4000000 | tf_op jit(solution)/shard_map/pallas_call | solution.py:431
  74.7 0.0 copy-done.1
  74.7 0.0 copy-start.3
  74.7 0.0 copy-start.4
  74.7 2.7 %shard_map.107.moves = f32[512,768]{1,0:T(8,128)S(1)} custom-call(bf16[512,256]{1,0:T(8,128)(2,1)S(1)} %bitcast.21, bf16[2560,768]{1,0:T(8,128)(2,1)S(1)} %copy-done.1), custom_call_target="tpu_custom_call" | custom-call | flops 1000000000 | bytes 4000000 | tf_op jit(solution)/shard_map/pallas_call | solution.py:446
  77.5 0.0 collective-permute-done.7.lo
  77.5 0.1 collective-permute-done.8.hi
  77.5 0.0 copy-done.3
  77.5 0.0 copy-done.4
  77.5 9.9 %shard_map.110 = (f32[64,2048]{1,0:T(8,128)}, f32[64,2048]{1,0:T(8,128)}, f32[64,2048]{1,0:T(8,128)}) custom-call(f32[64,2048]{1,0:T(8,128)S(1)} %bitcast.19, f32[64,2048]{1,0:T(8,128)S(1)} %bitcast.23, f32[64,2048]{1,0:T(8,128)S(1)} %bitcast.24, bf16[512,256]{1,0:T(8,128)(2,1)S(1)} %bitcast.22, f32[512,768]{1,0:T(8,128)S(1)} %shard_map.107.moves, ...), custom_call_target="tpu_custom_call" | custom-call | flops 10000000000 | bytes 4000000 | tf_op jit(solution)/shard_map/pallas_call | solution.py:453
  (4 shorter events, 0.1 us)
Async XLA Ops:
  0.6 1.5 %copy-start.6 = (bf16[1,31,31]{2,1,0:T(8,128)(2,1)S(1)}, bf16[1,31,31]{2,1,0:T(8,128)(2,1)}, u32[]{:S(2)}) copy-start(bf16[1,31,31]{2,1,0:T(8,128)(2,1)} %param.12) | copy-start | bytes 5770
  2.7 7.0 %copy-start.2 = (f32[1,64,2048]{2,1,0:T(8,128)S(1)}, f32[1,64,2048]{2,1,0:T(8,128)}, u32[]{:S(2)}) copy-start(f32[1,64,2048]{2,1,0:T(8,128)} %param.8) | copy-start | bytes 1572868
  2.7 15.0 %copy-start.5 = (f32[64,2048]{1,0:T(8,128)S(1)}, f32[64,2048]{1,0:T(8,128)}, u32[]{:S(2)}) copy-start(f32[64,2048]{1,0:T(8,128)} %measured.1) | copy-start | bytes 1572868
  3.5 16.7 %collective-permute-start.3 = (bf16[66,8,256]{2,1,0:T(8,128)(2,1)S(1)}, bf16[66,8,256]{2,1,0:T(8,128)(2,1)S(1)}, u32[]{:S(2)}, u32[]{:S(2)}) collective-permute-start(bf16[66,8,256]{2,1,0:T(8,128)(2,1)S(1)} %get-tuple-element.25.own_pack), channel_id=1, source_target_pairs={{4,0},{8,4},{12,8},{16,12},{20,16},{24,20},{28,24},{32,28},{36,32}... | collective-permute-start | bytes 811016 | tf_op jit(solution)/shard_map/ppermute | solution.py:408
  4.8 15.4 %collective-permute-start.2 = (bf16[66,8,256]{2,1,0:T(8,128)(2,1)S(1)}, bf16[66,8,256]{2,1,0:T(8,128)(2,1)S(1)}, u32[]{:S(2)}, u32[]{:S(2)}) collective-permute-start(bf16[66,8,256]{2,1,0:T(8,128)(2,1)S(1)} %get-tuple-element.25.own_pack), channel_id=1, source_target_pairs={{0,4},{4,8},{8,12},{12,16},{16,20},{20,24},{24,28},{28,32},{32,36}... | collective-permute-start | bytes 811016 | tf_op jit(solution)/shard_map/ppermute | solution.py:407
  9.8 6.6 %collective-permute-start.1 = (bf16[16,2048]{1,0:T(8,128)(2,1)S(1)}, bf16[16,2048]{1,0:T(8,128)(2,1)S(1)}, u32[]{:S(2)}, u32[]{:S(2)}) collective-permute-start(bf16[16,2048]{1,0:T(8,128)(2,1)S(1)} %get-tuple-element.41), channel_id=1, source_target_pairs={{1,0},{2,1},{3,2},{5,4},{6,5},{7,6},{9,8},{10,9},{11,10},{13,12},{... | collective-permute-start | bytes 196616 | tf_op jit(solution)/shard_map/ppermute | solution.py:390
  14.5 3.2 %collective-permute-start = (bf16[16,2048]{1,0:T(8,128)(2,1)S(1)}, bf16[16,2048]{1,0:T(8,128)(2,1)S(1)}, u32[]{:S(2)}, u32[]{:S(2)}) collective-permute-start(bf16[16,2048]{1,0:T(8,128)(2,1)S(1)} %get-tuple-element.42), channel_id=1, source_target_pairs={{0,1},{1,2},{2,3},{4,5},{5,6},{6,7},{8,9},{9,10},{10,11},{12,13},{... | collective-permute-start | bytes 196616 | tf_op jit(solution)/shard_map/ppermute | solution.py:389
  20.1 35.8 %copy-start.9 = (bf16[16]{0:T(256)(128)(2,1)S(1)}, bf16[16]{0:T(256)(128)(2,1)}, u32[]{:S(2)}) copy-start(bf16[16]{0:T(256)(128)(2,1)} %param.15) | copy-start | bytes 100
  20.1 35.9 %copy-start.8 = (bf16[27,16]{0,1:T(8,128)(2,1)S(1)}, bf16[27,16]{0,1:T(8,128)(2,1)}, u32[]{:S(2)}) copy-start(bf16[27,16]{0,1:T(8,128)(2,1)} %param.13) | copy-start | bytes 2596
  40.6 6.0 %collective-permute-start.6 = (f32[32,256]{1,0:T(8,128)S(1)}, f32[32,256]{1,0:T(8,128)S(1)}, u32[]{:S(2)}, u32[]{:S(2)}) collective-permute-start(f32[32,256]{1,0:T(8,128)S(1)} %convert_reduce_fusion), channel_id=1, source_target_pairs={{0,24},{8,16},{16,8},{24,0},{1,25},{9,17},{17,9},{25,1},{2,26},{10... | collective-permute-start | bytes 98312 | tf_op jit(solution)/shard_map/ppermute | solution.py:423
  44.4 3.7 %collective-permute-start.5 = (f32[32,256]{1,0:T(8,128)S(1)}, f32[32,256]{1,0:T(8,128)S(1)}, u32[]{:S(2)}, u32[]{:S(2)}) collective-permute-start(f32[32,256]{1,0:T(8,128)S(1)} %convert_reduce_fusion), channel_id=1, source_target_pairs={{0,8},{8,0},{16,24},{24,16},{1,9},{9,1},{17,25},{25,17},{2,10},{10... | collective-permute-start | bytes 98312 | tf_op jit(solution)/shard_map/ppermute | solution.py:423
  44.4 7.2 %collective-permute-start.4 = (f32[32,256]{1,0:T(8,128)S(1)}, f32[32,256]{1,0:T(8,128)S(1)}, u32[]{:S(2)}, u32[]{:S(2)}) collective-permute-start(f32[32,256]{1,0:T(8,128)S(1)} %convert_reduce_fusion), channel_id=1, source_target_pairs={{0,16},{8,24},{16,0},{24,8},{1,17},{9,25},{17,1},{25,9},{2,18},{10... | collective-permute-start | bytes 98312 | tf_op jit(solution)/shard_map/ppermute | solution.py:423
  52.4 11.2 %all-to-all-start.1 = ((bf16[16,32,256]{2,1,0:T(8,128)(2,1)}), bf16[16,32,256]{2,1,0:T(8,128)(2,1)S(1)}, u32[]{:S(2)}, u32[]{:S(2)}) async-start(bf16[16,32,256]{2,1,0:T(8,128)(2,1)} %broadcast_in_dim.15), calls=%async_computation.1 | async-start | bytes 524288 | tf_op jit(solution)/shard_map/all_to_all | solution.py:440
  56.1 17.3 %copy-start.7 = (f32[16]{0:T(128)S(1)}, f32[16]{0:T(128)}, u32[]{:S(2)}) copy-start(f32[16]{0:T(128)} %param.14) | copy-start | bytes 196
  57.8 1.9 %copy-start = (bf16[2560,768]{1,0:T(8,128)(2,1)}, bf16[2560,768]{1,0:T(8,128)(2,1)S(1)}, u32[]{:S(2)}) copy-start(bf16[2560,768]{1,0:T(8,128)(2,1)S(1)} %get-tuple-element.29.wg) | copy-start | bytes 11796484
  63.6 11.1 %copy-start.1 = (bf16[2560,768]{1,0:T(8,128)(2,1)S(1)}, bf16[2560,768]{1,0:T(8,128)(2,1)}, u32[]{:S(2)}) copy-start(bf16[2560,768]{1,0:T(8,128)(2,1)} %copy-done) | copy-start | bytes 11796484
  64.0 13.5 %collective-permute-start.7 = (bf16[256,256]{1,0:T(8,128)(2,1)S(1)}, bf16[256,256]{1,0:T(8,128)(2,1)S(1)}, u32[]{:S(2)}, u32[]{:S(2)}) collective-permute-start(bf16[256,256]{1,0:T(8,128)(2,1)S(1)} %get-tuple-element.32), channel_id=1, source_target_pairs={{0,1},{1,2},{2,3},{4,5},{5,6},{6,7},{8,9},{9,10},{10,11},{12,13},{... | collective-permute-start | bytes 393224 | tf_op jit(solution)/shard_map/ppermute | solution.py:444
  71.2 6.3 %collective-permute-start.8 = (bf16[256,256]{1,0:T(8,128)(2,1)S(1)}, bf16[256,256]{1,0:T(8,128)(2,1)S(1)}, u32[]{:S(2)}, u32[]{:S(2)}) collective-permute-start(bf16[256,256]{1,0:T(8,128)(2,1)S(1)} %get-tuple-element.33), channel_id=1, source_target_pairs={{1,0},{2,1},{3,2},{5,4},{6,5},{7,6},{9,8},{10,9},{11,10},{13,12},{... | collective-permute-start | bytes 393224 | tf_op jit(solution)/shard_map/ppermute | solution.py:445
  74.7 2.8 %copy-start.3 = (f32[1,64,2048]{2,1,0:T(8,128)S(1)}, f32[1,64,2048]{2,1,0:T(8,128)}, u32[]{:S(2)}) copy-start(f32[1,64,2048]{2,1,0:T(8,128)} %param.9) | copy-start | bytes 1572868
  74.7 2.8 %copy-start.4 = (f32[1,64,2048]{2,1,0:T(8,128)S(1)}, f32[1,64,2048]{2,1,0:T(8,128)}, u32[]{:S(2)}) copy-start(f32[1,64,2048]{2,1,0:T(8,128)} %param.10) | copy-start | bytes 1572868

commit v4 on v3

--- a/solution.py
+++ b/solution.py
@@ -116,9 +116,11 @@
     return jnp.concatenate([ref[64 + g // 2, :, 128 * (g % 2) : 128 * (g % 2) + 128] for g in range(4)], axis=0)
 
 
-def back_weights_kernel(prev_pack, own_pack, next_pack, wg_ref, down_ref, up_ref, strips, wide):
+def back_weights_kernel(prev_pack, own_pack, next_pack, low, wg_ref, starts_ref, down_ref, up_ref, strips, wide):
     down_ref[64:128, 128:256] = jnp.ones((64, 128), BF)
     up_ref[64:128, 128:256] = jnp.ones((64, 128), BF)
+    row = iota((256, 256), 0)
+    col = iota((256, 256), 1)
     for p, pack in enumerate((prev_pack, own_pack, next_pack)):
 
         def put(at, value, p=p):
@@ -126,10 +128,22 @@
 
         toeplitz(unpack_psf(pack), True, strips, put, -STEP, TURN[p])
         wide[...] = pack[0:64].astype(F32)
+        start = wide[...].reshape(512, 256)
+        below = wide[:, 7, 128:256].astype(BF)
+        above = wide[:, 0, 0:128].astype(BF)
+        if p == 1:
+            start = start + low[...].astype(F32).reshape(512, 256)
+        else:
+            same = (col // 32 == row // 32) & (col % 32 == (row % 32 + TURN[p]) % 32)
+            shift = jnp.where(same, 1.0, 0.0).astype(BF)
+            start = jnp.dot(start.astype(BF), shift, preferred_element_type=F32)
+            below = jnp.dot(below, shift[0:128, 0:128], preferred_element_type=F32).astype(BF)
+            above = jnp.dot(above, shift[0:128, 0:128], preferred_element_type=F32).astype(BF)
+        starts_ref[:, 256 * p : 256 * p + 256] = start
         at = slice(64 * (p // 2), 64 * (p // 2) + 64)
         lanes = slice(128 * (p % 2), 128 * (p % 2) + 128)
-        down_ref[at, lanes] = wide[:, 7, 128:256].astype(BF)
-        up_ref[at, lanes] = wide[:, 0, 0:128].astype(BF)
+        down_ref[at, lanes] = below
+        up_ref[at, lanes] = above
 
 
 def gather_rows(main, lhs):
@@ -212,96 +226,90 @@
     up_ref[128:256, :] = edge_up[...]
 
 
-def back_kernel(res, wg, moves_ref, main, lhs):
+def edge_tiles(rows, wg, first, at):
+    tiles = [wg[first : first + 1024, 256 * p + at : 256 * p + at + 128] for p in range(3)]
+    return jnp.concatenate([jnp.dot(rows, tile, preferred_element_type=F32) for tile in tiles], axis=1)
+
+
+def back_kernel(res, wg, starts, noisy_ref, moves_ref, edges_ref, main, lhs):
     main[0] = jnp.zeros((16, 256), F32)
     main[65] = jnp.zeros((16, 256), F32)
     main[1:65, 0:2, :] = jnp.zeros((64, 2, 256), F32)
     main[1:65, 2:10, :] = res[...].astype(F32).reshape(64, 8, 256)
     main[1:65, 10:12, :] = jnp.zeros((64, 2, 256), F32)
     gather_rows(main, lhs)
-    moves_ref[...] = jnp.dot(lhs[...], wg[...], preferred_element_type=F32)
-
-
-def final_kernel(planes, denoised, dual, res, moves, lo, hi, own_low, own_pack, prev_pack, next_pack, wg, even, odd, mx,
-                 swap, np_ref, nd_ref, du_ref, main, lhs, vol, wins, nat, turn, mine, held, sems):
-    main[0] = jnp.zeros((16, 256), F32)
-    main[65] = jnp.zeros((16, 256), F32)
-    main[1:65, 2:10, :] = res[...].astype(F32).reshape(64, 8, 256)
-    for at in range(2):
-        main[1:65, at, :] = lo[64 * at : 64 * at + 64, :].astype(F32)
-        main[1:65, 10 + at, :] = hi[64 * at : 64 * at + 64, :].astype(F32)
+    moves = jnp.dot(lhs[...], wg[...], preferred_element_type=F32)
+    noisy_ref[...] = starts[...] + moves
+    moves_ref[...] = moves[:, 256:512].reshape(64, 8, 256)
     j = iota((64, 256), 1) % 32
 
     def octet(q):
         rim = jnp.where(j < 16, main[2:66, q, :], main[0:64, q, :])
         return [main[1:65, q, :].astype(BF), rim.astype(BF)]
 
-    rows = {q: octet(q) for q in (0, 1, 2, 3, 8, 9, 10, 11)}
-    above = jnp.concatenate(rows[0] + rows[1] + rows[2] + rows[3], axis=1)
-    below = jnp.concatenate(rows[8] + rows[9] + rows[10] + rows[11], axis=1)
+    edges_ref[0] = edge_tiles(jnp.concatenate(octet(2) + octet(3), axis=1), wg, 1536, 128)
+    edges_ref[1] = edge_tiles(jnp.concatenate(octet(8) + octet(9), axis=1), wg, 0, 0)
+
+
+def final_kernel(planes, denoised, dual, noisy, moves, edges, lo, hi, wg, even, odd, mx, swap, np_ref, nd_ref, du_ref,
+                 halo, lhs, vol, nat, turn, mine, held, sems):
+    j = iota((64, 256), 1) % 32
+    rows = []
+    for n, (ref, at) in enumerate(((lo, 0), (lo, 1), (hi, 0), (hi, 1))):
+        halo[n, 0:8] = jnp.zeros((8, 256), F32)
+        halo[n, 72:80] = jnp.zeros((8, 256), F32)
+        halo[n, 8:72] = ref[64 * at : 64 * at + 64, :].astype(F32)
+        rim = jnp.where(j < 16, halo[n, 9:73], halo[n, 7:71])
+        rows.append([ref[64 * at : 64 * at + 64, :], rim.astype(BF)])
     none = [jnp.zeros((64, 512), BF)]
-    first = jnp.concatenate(
-        [jnp.concatenate(rows[0] + rows[1], axis=1), jnp.concatenate(rows[1] + none, axis=1)], axis=0
-    )
-    last = jnp.concatenate(
-        [jnp.concatenate(none + rows[10], axis=1), jnp.concatenate(rows[10] + rows[11], axis=1)], axis=0
-    )
+    above = jnp.concatenate(rows[0] + rows[1], axis=1)
+    below = jnp.concatenate(rows[2] + rows[3], axis=1)
+    first = jnp.concatenate([above, jnp.concatenate(rows[1] + none, axis=1)], axis=0)
+    last = jnp.concatenate([jnp.concatenate(none + rows[2], axis=1), below], axis=0)
     first = jnp.dot(first, wg[0:1024, :], preferred_element_type=F32)
     last = jnp.dot(last, wg[1536:2560, :], preferred_element_type=F32)
+    edge_lo = edges[0] + edge_tiles(above, wg, 512, 128)
+    edge_hi = edges[1] + edge_tiles(below, wg, 1024, 0)
     use_lo = lo[192:256, 128:256] > 0
     use_hi = hi[192:256, 128:256] > 0
-    row = iota((256, 256), 0)
-    col = iota((256, 256), 1)
-    for p, pack in enumerate((prev_pack, own_pack, next_pack)):
-        start = pack[0:64].reshape(512, 256)
+    for p in range(3):
+        cut = slice(256 * p, 256 * p + 256)
+        tile = slice(128 * p, 128 * p + 128)
         at = slice(128 + 64 * (p // 2), 192 + 64 * (p // 2))
         lanes = slice(128 * (p % 2), 128 * (p % 2) + 128)
-        edge_lo = lo[at, lanes]
-        edge_hi = hi[at, lanes]
-        if p == 1:
-            start = start.astype(F32) + own_low[...].astype(F32).reshape(512, 256)
-            edge_lo = edge_lo.astype(F32)
-            edge_hi = edge_hi.astype(F32)
-        else:
-            same = (col // 32 == row // 32) & (col % 32 == (row % 32 + TURN[p]) % 32)
-            shift = jnp.where(same, 1.0, 0.0).astype(BF)
-            start = jnp.dot(start, shift, preferred_element_type=F32)
-            edge_lo = jnp.dot(edge_lo, shift[0:128, 0:128], preferred_element_type=F32)
-            edge_hi = jnp.dot(edge_hi, shift[0:128, 0:128], preferred_element_type=F32)
         vol[p, 0] = jnp.zeros((16, 256), F32)
         vol[p, 65] = jnp.zeros((16, 256), F32)
-        cut = slice(256 * p, 256 * p + 256)
-        vol[p, 1:65, 1:9, :] = (start + moves[:, cut]).reshape(64, 8, 256)
-        for at in range(2):
-            vol[p, 1:65, 1 + at, :] += first[64 * at : 64 * at + 64, cut]
-            vol[p, 1:65, 7 + at, :] += last[64 * at : 64 * at + 64, cut]
-        if p == 1:
-            mine[...] = moves[:, cut].reshape(64, 8, 256)
-            for at in range(2):
-                mine[:, at, :] += first[64 * at : 64 * at + 64, cut]
-                mine[:, 6 + at, :] += last[64 * at : 64 * at + 64, cut]
-        g_lo = jnp.dot(above, wg[512:2560, 256 * p + 128 : 256 * p + 256], preferred_element_type=F32)
-        g_hi = jnp.dot(below, wg[0:2048, 256 * p : 256 * p + 128], preferred_element_type=F32)
-        vol[p, 1:65, 0, 128:256] = jnp.where(use_lo, edge_lo + g_lo, 0.0)
-        vol[p, 1:65, 9, 0:128] = jnp.where(use_hi, edge_hi + g_hi, 0.0)
-        group = iota((66, 8, 128), 2) // 32
-        t0 = vol[p, :, 1:9, 0:128]
-        t1 = vol[p, :, 1:9, 128:256]
-        wins[p, 0] = jnp.where(group == 3, vol[p, :, 0:8, 128:256], t0)
-        wins[p, 1] = jnp.where(group == 0, t1, t0)
-        wins[p, 2] = jnp.where(group == 3, t0, t1)
-        wins[p, 3] = jnp.where(group == 0, vol[p, :, 2:10, 0:128], t1)
-    lane = iota((64, 8, 128), 2)
-    j = lane % 32
-    ones = jnp.where((lane >= 6) & (lane <= 8), 1.0, 0.0)
-    for k in range(4):
-        rim = ones
+        vol[p, 1:65, 1:9, :] = noisy[:, cut].reshape(64, 8, 256)
+        for e in range(2):
+            vol[p, 1:65, 1 + e, :] += first[64 * e : 64 * e + 64, cut]
+            vol[p, 1:65, 7 + e, :] += last[64 * e : 64 * e + 64, cut]
+        vol[p, 1:65, 0, 128:256] = jnp.where(use_lo, lo[at, lanes].astype(F32) + edge_lo[:, tile], 0.0)
+        vol[p, 1:65, 9, 0:128] = jnp.where(use_hi, hi[at, lanes].astype(F32) + edge_hi[:, tile], 0.0)
+    mine[...] = moves[...]
+    for e in range(2):
+        mine[:, e, :] += first[64 * e : 64 * e + 64, 256:512]
+        mine[:, 6 + e, :] += last[64 * e : 64 * e + 64, 256:512]
+    for t in range(2):
+        lanes = slice(128 * t, 128 * t + 128)
+        j = iota((64, 16, 128), 2) % 32
+        rim = jnp.where((j >= 6) & (j <= 8), 1.0, 0.0)
         for p in range(3):
+            rim = jnp.where(j == TURN[p], vol[p, 2:66, :, lanes], rim)
+            rim = jnp.where(j == (31 + TURN[p]) % 32, vol[p, 0:64, :, lanes], rim)
+        vol[3, 1:65, :, lanes] = rim
+    group = iota((64, 8, 128), 2) // 32
+    for p in range(4):
+        t0 = vol[p, 1:65, 1:9, 0:128]
+        t1 = vol[p, 1:65, 1:9, 128:256]
+        windows = (
+            jnp.where(group == 3, vol[p, 1:65, 0:8, 128:256], t0),
+            jnp.where(group == 0, t1, t0),
+            jnp.where(group == 3, t0, t1),
+            jnp.where(group == 0, vol[p, 1:65, 2:10, 0:128], t1),
+        )
+        for k, window in enumerate(windows):
             at = 512 * k + 128 * p
-            lhs[:, at : at + 128] = wins[p, k, 1:65].reshape(512, 128).astype(BF)
-            rim = jnp.where(j == TURN[p], wins[p, k, 2:66], rim)
-            rim = jnp.where(j == (31 + TURN[p]) % 32, wins[p, k, 0:64], rim)
-        lhs[:, 512 * k + 384 : 512 * k + 512] = rim.reshape(512, 128).astype(BF)
+            lhs[:, at : at + 128] = window.reshape(512, 128).astype(BF)
     noise = []
     for half in range(2):
         total = None
@@ -421,13 +429,13 @@
     got = lax.all_to_all(part, group, 0, 0, tiled=True)
     mine = jnp.sum(got.reshape(16, 32, 256).astype(F32), axis=0)
     others = [lax.ppermute(mine, "zh", [(a, a ^ bits) for a in range(4)]) for bits in (2, 1, 3)]
-    wg, edge_down, edge_up = call(
+    wg, starts, edge_down, edge_up = call(
         back_weights_kernel,
-        [out((2560, 768), BF), out((128, 256), BF), out((128, 256), BF)],
+        [out((2560, 768), BF), out((512, 768), F32), out((128, 256), BF), out((128, 256), BF)],
         [strips, pltpu.VMEM((64, 8, 256), F32)],
-        3,
-        vmem=10,
-    )(prev_pack, packed, next_pack)
+        4,
+        vmem=12,
+    )(prev_pack, packed, next_pack, low)
     even, odd, mx = call(
         denoiser_weights_kernel,
         [out((512, 1024), BF), out((512, 1024), BF), out((2048, 128), BF)],
@@ -443,32 +451,31 @@
     )(res, edge_down, edge_up)
     rim_lo = lax.ppermute(rim_down, "band", down)
     rim_hi = lax.ppermute(rim_up, "band", up)
-    (moves,) = call(
+    noisy, moves, edges = call(
         back_kernel,
-        [out((512, 768), F32)],
+        [out((512, 768), F32), out((64, 8, 256), F32), out((2, 64, 384), F32)],
         [pltpu.VMEM((66, 16, 256), F32), pltpu.VMEM((512, 2560), BF)],
-        2,
-        vmem=14,
-    )(res, wg)
+        3,
+        vmem=16,
+    )(res, wg, starts)
     outs = call(
         final_kernel,
         [out((64, 2048), F32)] * 3,
         [
-            pltpu.VMEM((66, 16, 256), F32),
+            pltpu.VMEM((4, 80, 256), F32),
             pltpu.VMEM((512, 2048), BF),
-            pltpu.VMEM((3, 66, 16, 256), F32),
-            pltpu.VMEM((3, 4, 66, 8, 128), F32),
+            pltpu.VMEM((4, 66, 16, 256), F32),
             pltpu.VMEM((2, 16, 64, 128), F32),
             pltpu.VMEM((2, 2, 256, 512), BF),
             pltpu.VMEM((64, 8, 256), F32),
             pltpu.VMEM((3, 4, 64, 512), F32),
             pltpu.SemaphoreType.DMA((3, 4)),
         ],
-        16,
+        13,
         flops=10_000_000_000,
-        vmem=32,
+        vmem=28,
         far_out=True,
-    )(x, d, z, res, moves, rim_lo, rim_hi, low, packed, prev_pack, next_pack, wg, even, odd, mx, swap)
+    )(x, d, z, noisy, moves, edges, rim_lo, rim_hi, wg, even, odd, mx, swap)
     return tuple(o[None] for o in outs)
 
 

time: 88 us -> 84.7 us (0.963)
  starting transfers between devices: 31.8 us -> 27.9 us
  local copies, waits for them, and re-layouts: 2.85 us -> 4.33 us
  waiting for transfers between devices: 10.3 us -> 11.7 us
  blocking collectives: 20.4 us -> 19.2 us
  Pallas kernels: 19.6 us -> 18.6 us
    ppermute x1, waiting for transfers between devices: 0.01 us -> 3.65 us  [shards(): hi = lax.ppermute(x[0:16].astype(BF), 'band', up)]
    ppermute x1, starting transfers between devices: 4.7 us -> 1.92 us  [shards(): hi = lax.ppermute(x[0:16].astype(BF), 'band', up)]
    ppermute x1, starting transfers between devices: 7.29 us -> 4.98 us  [shards(): rim_lo = lax.ppermute(rim_down, 'band', down)]
    ppermute x1, starting transfers between devices: 1.92 us -> 3.96 us  [shards(): lo = lax.ppermute(x[48:64].astype(BF), 'band', down)]
    unnamed x21 -> x29, local copies, waits for them, and re-layouts: 2.01 us -> 3.49 us
    ppermute x1, waiting for transfers between devices: 1.3 us -> 0.01 us  [shards(): lo = lax.ppermute(x[48:64].astype(BF), 'band', down)]
    all_to_all x1, blocking collectives: 20.4 us -> 19.2 us  [shards(): got = lax.all_to_all(part, group, 0, 0, tiled=True)]
    pallas_call x3, Pallas kernels: 14.3 us -> 13.2 us  [the longest x1 8.47 us: shards(): call(final_kernel, [out((64, 2048), F32)] * 3, [pltpu.VMEM((4, 80, 256),...]
  transfers between devices with their start and end apart: 10 -> 10, of which waited for: 5 -> 5; matrix products, arithmetic and copies ran while one was open for 0% -> 0% of each run, Pallas kernels for 9% -> 10%
where the time goes in v4:
time: 84.7 us; the launch traced here: 84.3 us
  starting transfers between devices  27.9 us (33%)
  blocking collectives  19.2 us (23%)
  Pallas kernels  18.6 us (22%)
  waiting for transfers between devices  11.7 us (14%)
  local copies, waits for them, and re-layouts  4.33 us (5%)
  other arithmetic  1.54 us (2%)
  between operations  1.1 us (1%)
    all_to_all x1, blocking collectives, shards(): got = lax.all_to_all(part, group, 0, 0, tiled=True)  19.2 us
    pallas_call x1, Pallas kernels, shards(): call(final_kernel, [out((64, 2048), F32)] * 3, [pltpu.VMEM((4, 80, 256),...  8.47 us
    ppermute x3, starting transfers between devices, shards(): lax.ppermute(mine, 'zh', [(a, a ^ bits) for a in range(4)])  5.74 us
    ppermute x1, starting transfers between devices, shards(): rim_lo = lax.ppermute(rim_down, 'band', down)  4.98 us
    ppermute x3, waiting for transfers between devices, shards(): lax.ppermute(mine, 'zh', [(a, a ^ bits) for a in range(4)])  4.9 us
    ppermute x1, starting transfers between devices, shards(): prev_pack = lax.ppermute(packed, depth, later)  4.39 us
    ppermute x1, starting transfers between devices, shards(): lo = lax.ppermute(x[48:64].astype(BF), 'band', down)  3.96 us
    ppermute x1, waiting for transfers between devices, shards(): hi = lax.ppermute(x[0:16].astype(BF), 'band', up)  3.65 us
  transfers between devices with their start and end apart: 10, of which 5 were waited for; matrix products, arithmetic and copies ran while one was open for 0% of the time, Pallas kernels for 10%

profile of v4, /device:TPU:1, one launch (start us, length us, event | category | flops | bytes accessed | tf_op | source)
XLA Modules:
  0.0 84.3 jit_solution(17294206398801991022)
XLA Ops:
  0.6 0.0 copy-start.6
  0.6 1.5 %subtract_add_fusion.start = f32[64,2048]{1,0:T(8,128)S(1)} fusion(f32[1,64,2048]{2,1,0:T(8,128)} %param.10, f32[1,64,2048]{2,1,0:T(8,128)} %param.9, f32[1,64,2048]{2,1,0:T(8,128)} %param.8), kind=kLoop, calls=%fused_computation.1 | loop fusion | flops 655360 | bytes 2097152 | tf_op jit(solution)/shard_map/add | solution.py:158
  2.1 0.0 copy-done.6
  2.1 0.6 shard_map.103
  2.7 0.0 copy-start.8
  2.7 0.0 copy-start.2
  2.8 0.0 copy-start.5
  2.8 0.7 shard_map.104
  3.5 4.4 %collective-permute-start.2 = (bf16[66,8,256]{2,1,0:T(8,128)(2,1)S(1)}, bf16[66,8,256]{2,1,0:T(8,128)(2,1)S(1)}, u32[]{:S(2)}, u32[]{:S(2)}) collective-permute-start(bf16[66,8,256]{2,1,0:T(8,128)(2,1)S(1)} %get-tuple-element.29.own_pack), channel_id=1, source_target_pairs={{0,4},{4,8},{8,12},{12,16},{16,20},{20,24},{24,28},{28,32},{32,36}... | collective-permute-start | bytes 811016 | tf_op jit(solution)/shard_map/ppermute | solution.py:415
  7.9 1.3 %collective-permute-start.3 = (bf16[66,8,256]{2,1,0:T(8,128)(2,1)S(1)}, bf16[66,8,256]{2,1,0:T(8,128)(2,1)S(1)}, u32[]{:S(2)}, u32[]{:S(2)}) collective-permute-start(bf16[66,8,256]{2,1,0:T(8,128)(2,1)S(1)} %get-tuple-element.29.own_pack), channel_id=1, source_target_pairs={{4,0},{8,4},{12,8},{16,12},{20,16},{24,20},{28,24},{32,28},{36,32}... | collective-permute-start | bytes 811016 | tf_op jit(solution)/shard_map/ppermute | solution.py:416
  9.2 0.0 copy-done.2
  9.2 4.0 %collective-permute-start = (bf16[16,2048]{1,0:T(8,128)(2,1)S(1)}, bf16[16,2048]{1,0:T(8,128)(2,1)S(1)}, u32[]{:S(2)}, u32[]{:S(2)}) collective-permute-start(bf16[16,2048]{1,0:T(8,128)(2,1)S(1)} %get-tuple-element.50), channel_id=1, source_target_pairs={{0,1},{1,2},{2,3},{4,5},{5,6},{6,7},{8,9},{9,10},{10,11},{12,13},{... | collective-permute-start | bytes 196616 | tf_op jit(solution)/shard_map/ppermute | solution.py:397
  13.2 1.9 %collective-permute-start.1 = (bf16[16,2048]{1,0:T(8,128)(2,1)S(1)}, bf16[16,2048]{1,0:T(8,128)(2,1)S(1)}, u32[]{:S(2)}, u32[]{:S(2)}) collective-permute-start(bf16[16,2048]{1,0:T(8,128)(2,1)S(1)} %get-tuple-element.49), channel_id=1, source_target_pairs={{1,0},{2,1},{3,2},{5,4},{6,5},{7,6},{9,8},{10,9},{11,10},{13,12},{... | collective-permute-start | bytes 196616 | tf_op jit(solution)/shard_map/ppermute | solution.py:398
  15.1 0.0 collective-permute-done.lo
  15.1 3.6 %collective-permute-done.1.hi = bf16[16,2048]{1,0:T(8,128)(2,1)S(1)} collective-permute-done((bf16[16,2048]{1,0:T(8,128)(2,1)S(1)}, bf16[16,2048]{1,0:T(8,128)(2,1)S(1)}, u32[]{:S(2)}, u32[]{:S(2)}) %collective-permute-start.1) | collective-permute-done | bytes 65568 | tf_op jit(solution)/shard_map/ppermute | solution.py:398
  18.8 0.0 copy-done.8
  18.8 0.0 copy-done.5
  18.8 2.3 %shard_map.105 = bf16[512,256]{1,0:T(8,128)(2,1)S(1)} custom-call(f32[64,2048]{1,0:T(8,128)S(1)} %bitcast.18, f32[64,2048]{1,0:T(8,128)S(1)} %copy-done.5, bf16[16,2048]{1,0:T(8,128)(2,1)S(1)} %collective-permute-done.lo, bf16[16,2048]{1,0:T(8,128)(2,1)S(1)} %collective-permute-done.1.hi, bf16[2560,256]{1,0:T(8,128)(2,1)S(1)} %get-tuple-element.27.wf, ...), custom_call_target="tpu_custom_call" | custom-call | flops 1000000000 | bytes 4000000 | tf_op jit(solution)/shard_map/pallas_call | solution.py:417
  21.1 0.0 copy-start.12
  21.1 0.0 copy-start.13
  21.2 0.0 collective-permute-done.2.prev_pack
  21.2 0.0 collective-permute-done.3.next_pack
  21.2 19.2 %all_to_all.17 = bf16[16,32,256]{2,1,0:T(8,128)(2,1)S(1)} all-to-all(bf16[16,32,256]{2,1,0:T(8,128)(2,1)S(1)} %bitcast.24), channel_id=1, replica_groups=mesh['xh'=2,'y'=4,'zh'=4,'zl'=2,'band'=4] {'xh','y','zl'}, dimensions={0} | all-to-all | bytes 524288 | tf_op jit(solution)/shard_map/all_to_all | solution.py:429
  40.4 3.7 %collective-permute-start.4 = (f32[32,256]{1,0:T(8,128)S(1)}, f32[32,256]{1,0:T(8,128)S(1)}, u32[]{:S(2)}, u32[]{:S(2)}) collective-permute-start(f32[32,256]{1,0:T(8,128)S(1)} %convert_reduce_fusion), channel_id=1, source_target_pairs={{0,16},{8,24},{16,0},{24,8},{1,17},{9,25},{17,1},{25,9},{2,18},{10... | collective-permute-start | bytes 98312 | tf_op jit(solution)/shard_map/ppermute | solution.py:431
  44.1 1.1 %collective-permute-start.5 = (f32[32,256]{1,0:T(8,128)S(1)}, f32[32,256]{1,0:T(8,128)S(1)}, u32[]{:S(2)}, u32[]{:S(2)}) collective-permute-start(f32[32,256]{1,0:T(8,128)S(1)} %convert_reduce_fusion), channel_id=1, source_target_pairs={{0,8},{8,0},{16,24},{24,16},{1,9},{9,1},{17,25},{25,17},{2,10},{10... | collective-permute-start | bytes 98312 | tf_op jit(solution)/shard_map/ppermute | solution.py:431
  45.2 0.9 %collective-permute-start.6 = (f32[32,256]{1,0:T(8,128)S(1)}, f32[32,256]{1,0:T(8,128)S(1)}, u32[]{:S(2)}, u32[]{:S(2)}) collective-permute-start(f32[32,256]{1,0:T(8,128)S(1)} %convert_reduce_fusion), channel_id=1, source_target_pairs={{0,24},{8,16},{16,8},{24,0},{1,25},{9,17},{17,9},{25,1},{2,26},{10... | collective-permute-start | bytes 98312 | tf_op jit(solution)/shard_map/ppermute | solution.py:431
  46.1 1.1 %collective-permute-done.4 = f32[32,256]{1,0:T(8,128)S(1)} collective-permute-done((f32[32,256]{1,0:T(8,128)S(1)}, f32[32,256]{1,0:T(8,128)S(1)}, u32[]{:S(2)}, u32[]{:S(2)}) %collective-permute-start.4) | collective-permute-done | bytes 32800 | tf_op jit(solution)/shard_map/ppermute | solution.py:431
  47.2 2.9 %collective-permute-done.5 = f32[32,256]{1,0:T(8,128)S(1)} collective-permute-done((f32[32,256]{1,0:T(8,128)S(1)}, f32[32,256]{1,0:T(8,128)S(1)}, u32[]{:S(2)}, u32[]{:S(2)}) %collective-permute-start.5) | collective-permute-done | bytes 32800 | tf_op jit(solution)/shard_map/ppermute | solution.py:431
  50.1 1.0 %collective-permute-done.6 = f32[32,256]{1,0:T(8,128)S(1)} collective-permute-done((f32[32,256]{1,0:T(8,128)S(1)}, f32[32,256]{1,0:T(8,128)S(1)}, u32[]{:S(2)}, u32[]{:S(2)}) %collective-permute-start.6) | collective-permute-done | bytes 32800 | tf_op jit(solution)/shard_map/ppermute | solution.py:431
  51.0 0.7 broadcast_in_dim.15
  51.8 3.5 %all-to-all-start.1 = ((bf16[16,32,256]{2,1,0:T(8,128)(2,1)}), bf16[16,32,256]{2,1,0:T(8,128)(2,1)S(1)}, u32[]{:S(2)}, u32[]{:S(2)}) async-start(bf16[16,32,256]{2,1,0:T(8,128)(2,1)} %broadcast_in_dim.15), calls=%async_computation.1 | async-start | bytes 524288 | tf_op jit(solution)/shard_map/all_to_all | solution.py:448
  55.3 0.0 copy-done.12
  55.3 0.1 copy.12.kernel_ref
  55.4 0.0 copy-done.13
  55.4 0.1 copy.13.mix_ref
  55.5 0.0 copy-start.7
  55.5 1.9 %shard_map.106 = (bf16[2560,768]{1,0:T(8,128)(2,1)S(1)}, f32[512,768]{1,0:T(8,128)S(1)}, bf16[128,256]{1,0:T(8,128)(2,1)S(1)}, bf16[128,256]{1,0:T(8,128)(2,1)S(1)}) custom-call(bf16[66,8,256]{2,1,0:T(8,128)(2,1)S(1)} %collective-permute-done.2.prev_pack, bf16[66,8,256]{2,1,0:T(8,128)(2,1)S(1)} %get-tuple-element.29.own_pack, ...), custom_call_target="tpu_custom_call" | custom-call | flops 1000000000 | bytes 4000000 | tf_op jit(solution)/shard_map/pallas_call | solution.py:432
  57.4 0.0 copy-start
  57.4 1.9 %copy-done = bf16[2560,768]{1,0:T(8,128)(2,1)} copy-done((bf16[2560,768]{1,0:T(8,128)(2,1)}, bf16[2560,768]{1,0:T(8,128)(2,1)S(1)}, u32[]{:S(2)}) %copy-start) | copy-done | bytes 3932184
  59.3 0.0 copy-start.10
  59.3 0.6 copy-done.10
  59.9 3.1 %all-to-all-done.1 = bf16[16,32,256]{2,1,0:T(8,128)(2,1)S(1)} async-done(((bf16[16,32,256]{2,1,0:T(8,128)(2,1)}), bf16[16,32,256]{2,1,0:T(8,128)(2,1)S(1)}, u32[]{:S(2)}, u32[]{:S(2)}) %all-to-all-start.1) | async-done | bytes 262176 | tf_op jit(solution)/shard_map/all_to_all | solution.py:448
  63.0 0.0 copy-start.11
  63.0 0.8 copy-done.11
  63.9 0.0 copy-start.1
  63.9 0.4 shard_map.108
  64.3 5.0 %collective-permute-start.7 = (bf16[256,256]{1,0:T(8,128)(2,1)S(1)}, bf16[256,256]{1,0:T(8,128)(2,1)S(1)}, u32[]{:S(2)}, u32[]{:S(2)}) collective-permute-start(bf16[256,256]{1,0:T(8,128)(2,1)S(1)} %get-tuple-element.41), channel_id=1, source_target_pairs={{0,1},{1,2},{2,3},{4,5},{5,6},{6,7},{8,9},{9,10},{10,11},{12,13},{... | collective-permute-start | bytes 393224 | tf_op jit(solution)/shard_map/ppermute | solution.py:452
  69.2 2.1 %collective-permute-start.8 = (bf16[256,256]{1,0:T(8,128)(2,1)S(1)}, bf16[256,256]{1,0:T(8,128)(2,1)S(1)}, u32[]{:S(2)}, u32[]{:S(2)}) collective-permute-start(bf16[256,256]{1,0:T(8,128)(2,1)S(1)} %get-tuple-element.42), channel_id=1, source_target_pairs={{1,0},{2,1},{3,2},{5,4},{6,5},{7,6},{9,8},{10,9},{11,10},{13,12},{... | collective-permute-start | bytes 393224 | tf_op jit(solution)/shard_map/ppermute | solution.py:453
  71.3 0.0 copy-done.7
  71.4 1.3 %shard_map.109 = (bf16[512,1024]{1,0:T(8,128)(2,1)S(1)}, bf16[512,1024]{1,0:T(8,128)(2,1)S(1)}, bf16[2048,128]{1,0:T(8,128)(2,1)S(1)}) custom-call(bf16[27,16]{1,0:T(8,128)(2,1)S(1)} %copy.12.kernel_ref, f32[1,16]{1,0:T(1,128)S(1)} %bitcast.26, bf16[16,1]{1,0:T(8,128)(2,1)S(1)} %copy.13.mix_ref), custom_call_target="tpu_custom_call" | custom-call | flops 1000000000 | bytes 4000000 | tf_op jit(solution)/shard_map/pallas_call | solution.py:439
  72.7 0.0 copy-done.1
  72.7 0.0 copy-start.3
  72.7 0.0 copy-start.4
  72.7 0.0 copy-start.9
  72.7 2.8 %shard_map.107 = (f32[512,768]{1,0:T(8,128)S(1)}, f32[64,8,256]{2,1,0:T(8,128)S(1)}, f32[2,64,384]{2,1,0:T(8,128)S(1)}) custom-call(bf16[512,256]{1,0:T(8,128)(2,1)S(1)} %bitcast.21, bf16[2560,768]{1,0:T(8,128)(2,1)S(1)} %copy-done.1, f32[512,768]{1,0:T(8,128)S(1)} %get-tuple-element.35.starts), custom_call_target="tpu_custom_call" | custom-call | flops 1000000000 | bytes 4000000 | tf_op jit(solution)/shard_map/pallas_call | solution.py:454
  75.6 0.0 collective-permute-done.7.lo
  75.6 0.0 collective-permute-done.8.hi
  75.6 0.0 copy-done.3
  75.6 0.0 copy-done.4
  75.6 0.0 copy-done.9
  75.6 8.5 %shard_map.110 = (f32[64,2048]{1,0:T(8,128)}, f32[64,2048]{1,0:T(8,128)}, f32[64,2048]{1,0:T(8,128)}) custom-call(f32[64,2048]{1,0:T(8,128)S(1)} %bitcast.19, f32[64,2048]{1,0:T(8,128)S(1)} %bitcast.22, f32[64,2048]{1,0:T(8,128)S(1)} %bitcast.23, f32[512,768]{1,0:T(8,128)S(1)} %get-tuple-element.36.noisy, f32[64,8,256]{2,1,0:T(8,128)S(1)} %get-tuple-element.37.moves, ...), custom_call_target="tpu_custom_call" | custom-call | flops 10000000000 | bytes 4000000 | tf_op jit(solution)/shard_map/pallas_call | solution.py:461
  (4 shorter events, 0.1 us)
Async XLA Ops:
  0.6 1.5 %copy-start.6 = (bf16[1,31,31]{2,1,0:T(8,128)(2,1)S(1)}, bf16[1,31,31]{2,1,0:T(8,128)(2,1)}, u32[]{:S(2)}) copy-start(bf16[1,31,31]{2,1,0:T(8,128)(2,1)} %param.12) | copy-start | bytes 5770
  2.7 16.0 %copy-start.8 = (bf16[512,512]{1,0:T(8,128)(2,1)}, bf16[512,512]{1,0:T(8,128)(2,1)S(1)}, u32[]{:S(2)}) copy-start(bf16[512,512]{1,0:T(8,128)(2,1)S(1)} %get-tuple-element.28.swap) | copy-start | bytes 1572868
  2.7 6.4 %copy-start.2 = (f32[1,64,2048]{2,1,0:T(8,128)S(1)}, f32[1,64,2048]{2,1,0:T(8,128)}, u32[]{:S(2)}) copy-start(f32[1,64,2048]{2,1,0:T(8,128)} %param.8) | copy-start | bytes 1572868
  2.8 16.0 %copy-start.5 = (f32[64,2048]{1,0:T(8,128)S(1)}, f32[64,2048]{1,0:T(8,128)}, u32[]{:S(2)}) copy-start(f32[64,2048]{1,0:T(8,128)} %measured.1) | copy-start | bytes 1572868
  3.5 17.7 %collective-permute-start.2 = (bf16[66,8,256]{2,1,0:T(8,128)(2,1)S(1)}, bf16[66,8,256]{2,1,0:T(8,128)(2,1)S(1)}, u32[]{:S(2)}, u32[]{:S(2)}) collective-permute-start(bf16[66,8,256]{2,1,0:T(8,128)(2,1)S(1)} %get-tuple-element.29.own_pack), channel_id=1, source_target_pairs={{0,4},{4,8},{8,12},{12,16},{16,20},{20,24},{24,28},{28,32},{32,36}... | collective-permute-start | bytes 811016 | tf_op jit(solution)/shard_map/ppermute | solution.py:415
  7.9 13.3 %collective-permute-start.3 = (bf16[66,8,256]{2,1,0:T(8,128)(2,1)S(1)}, bf16[66,8,256]{2,1,0:T(8,128)(2,1)S(1)}, u32[]{:S(2)}, u32[]{:S(2)}) collective-permute-start(bf16[66,8,256]{2,1,0:T(8,128)(2,1)S(1)} %get-tuple-element.29.own_pack), channel_id=1, source_target_pairs={{4,0},{8,4},{12,8},{16,12},{20,16},{24,20},{28,24},{32,28},{36,32}... | collective-permute-start | bytes 811016 | tf_op jit(solution)/shard_map/ppermute | solution.py:416
  9.2 5.9 %collective-permute-start = (bf16[16,2048]{1,0:T(8,128)(2,1)S(1)}, bf16[16,2048]{1,0:T(8,128)(2,1)S(1)}, u32[]{:S(2)}, u32[]{:S(2)}) collective-permute-start(bf16[16,2048]{1,0:T(8,128)(2,1)S(1)} %get-tuple-element.50), channel_id=1, source_target_pairs={{0,1},{1,2},{2,3},{4,5},{5,6},{6,7},{8,9},{9,10},{10,11},{12,13},{... | collective-permute-start | bytes 196616 | tf_op jit(solution)/shard_map/ppermute | solution.py:397
  13.2 5.6 %collective-permute-start.1 = (bf16[16,2048]{1,0:T(8,128)(2,1)S(1)}, bf16[16,2048]{1,0:T(8,128)(2,1)S(1)}, u32[]{:S(2)}, u32[]{:S(2)}) collective-permute-start(bf16[16,2048]{1,0:T(8,128)(2,1)S(1)} %get-tuple-element.49), channel_id=1, source_target_pairs={{1,0},{2,1},{3,2},{5,4},{6,5},{7,6},{9,8},{10,9},{11,10},{13,12},{... | collective-permute-start | bytes 196616 | tf_op jit(solution)/shard_map/ppermute | solution.py:398
  21.1 34.2 %copy-start.12 = (bf16[27,16]{0,1:T(8,128)(2,1)S(1)}, bf16[27,16]{0,1:T(8,128)(2,1)}, u32[]{:S(2)}) copy-start(bf16[27,16]{0,1:T(8,128)(2,1)} %param.13) | copy-start | bytes 2596
  21.1 34.3 %copy-start.13 = (bf16[16]{0:T(256)(128)(2,1)S(1)}, bf16[16]{0:T(256)(128)(2,1)}, u32[]{:S(2)}) copy-start(bf16[16]{0:T(256)(128)(2,1)} %param.15) | copy-start | bytes 100
  40.4 6.8 %collective-permute-start.4 = (f32[32,256]{1,0:T(8,128)S(1)}, f32[32,256]{1,0:T(8,128)S(1)}, u32[]{:S(2)}, u32[]{:S(2)}) collective-permute-start(f32[32,256]{1,0:T(8,128)S(1)} %convert_reduce_fusion), channel_id=1, source_target_pairs={{0,16},{8,24},{16,0},{24,8},{1,17},{9,25},{17,1},{25,9},{2,18},{10... | collective-permute-start | bytes 98312 | tf_op jit(solution)/shard_map/ppermute | solution.py:431
  44.1 6.0 %collective-permute-start.5 = (f32[32,256]{1,0:T(8,128)S(1)}, f32[32,256]{1,0:T(8,128)S(1)}, u32[]{:S(2)}, u32[]{:S(2)}) collective-permute-start(f32[32,256]{1,0:T(8,128)S(1)} %convert_reduce_fusion), channel_id=1, source_target_pairs={{0,8},{8,0},{16,24},{24,16},{1,9},{9,1},{17,25},{25,17},{2,10},{10... | collective-permute-start | bytes 98312 | tf_op jit(solution)/shard_map/ppermute | solution.py:431
  45.2 5.8 %collective-permute-start.6 = (f32[32,256]{1,0:T(8,128)S(1)}, f32[32,256]{1,0:T(8,128)S(1)}, u32[]{:S(2)}, u32[]{:S(2)}) collective-permute-start(f32[32,256]{1,0:T(8,128)S(1)} %convert_reduce_fusion), channel_id=1, source_target_pairs={{0,24},{8,16},{16,8},{24,0},{1,25},{9,17},{17,9},{25,1},{2,26},{10... | collective-permute-start | bytes 98312 | tf_op jit(solution)/shard_map/ppermute | solution.py:431
  51.8 11.3 %all-to-all-start.1 = ((bf16[16,32,256]{2,1,0:T(8,128)(2,1)}), bf16[16,32,256]{2,1,0:T(8,128)(2,1)S(1)}, u32[]{:S(2)}, u32[]{:S(2)}) async-start(bf16[16,32,256]{2,1,0:T(8,128)(2,1)} %broadcast_in_dim.15), calls=%async_computation.1 | async-start | bytes 524288 | tf_op jit(solution)/shard_map/all_to_all | solution.py:448
  55.5 15.8 %copy-start.7 = (f32[16]{0:T(128)S(1)}, f32[16]{0:T(128)}, u32[]{:S(2)}) copy-start(f32[16]{0:T(128)} %param.14) | copy-start | bytes 196
  57.4 1.9 %copy-start = (bf16[2560,768]{1,0:T(8,128)(2,1)}, bf16[2560,768]{1,0:T(8,128)(2,1)S(1)}, u32[]{:S(2)}) copy-start(bf16[2560,768]{1,0:T(8,128)(2,1)S(1)} %get-tuple-element.34.wg) | copy-start | bytes 11796484
  59.3 0.6 copy-start.10
  63.0 0.8 copy-start.11
  63.9 8.8 %copy-start.1 = (bf16[2560,768]{1,0:T(8,128)(2,1)S(1)}, bf16[2560,768]{1,0:T(8,128)(2,1)}, u32[]{:S(2)}) copy-start(bf16[2560,768]{1,0:T(8,128)(2,1)} %copy-done) | copy-start | bytes 11796484
  64.3 11.3 %collective-permute-start.7 = (bf16[256,256]{1,0:T(8,128)(2,1)S(1)}, bf16[256,256]{1,0:T(8,128)(2,1)S(1)}, u32[]{:S(2)}, u32[]{:S(2)}) collective-permute-start(bf16[256,256]{1,0:T(8,128)(2,1)S(1)} %get-tuple-element.41), channel_id=1, source_target_pairs={{0,1},{1,2},{2,3},{4,5},{5,6},{6,7},{8,9},{9,10},{10,11},{12,13},{... | collective-permute-start | bytes 393224 | tf_op jit(solution)/shard_map/ppermute | solution.py:452
  69.2 6.4 %collective-permute-start.8 = (bf16[256,256]{1,0:T(8,128)(2,1)S(1)}, bf16[256,256]{1,0:T(8,128)(2,1)S(1)}, u32[]{:S(2)}, u32[]{:S(2)}) collective-permute-start(bf16[256,256]{1,0:T(8,128)(2,1)S(1)} %get-tuple-element.42), channel_id=1, source_target_pairs={{1,0},{2,1},{3,2},{5,4},{6,5},{7,6},{9,8},{10,9},{11,10},{13,12},{... | collective-permute-start | bytes 393224 | tf_op jit(solution)/shard_map/ppermute | solution.py:453
  72.7 2.9 %copy-start.3 = (f32[1,64,2048]{2,1,0:T(8,128)S(1)}, f32[1,64,2048]{2,1,0:T(8,128)}, u32[]{:S(2)}) copy-start(f32[1,64,2048]{2,1,0:T(8,128)} %param.9) | copy-start | bytes 1572868
  72.7 2.9 %copy-start.4 = (f32[1,64,2048]{2,1,0:T(8,128)S(1)}, f32[1,64,2048]{2,1,0:T(8,128)}, u32[]{:S(2)}) copy-start(f32[1,64,2048]{2,1,0:T(8,128)} %param.10) | copy-start | bytes 1572868
  72.7 2.9 %copy-start.9 = (bf16[512,512]{1,0:T(8,128)(2,1)S(1)}, bf16[512,512]{1,0:T(8,128)(2,1)}, u32[]{:S(2)}) copy-start(bf16[512,512]{1,0:T(8,128)(2,1)} %copy-done.8) | copy-start | bytes 1572868

commit v5 on v4

--- a/solution.py
+++ b/solution.py
@@ -55,7 +55,7 @@
 TURN = (2, 0, 4)
 
 
-def forward_weights_kernel(psf_ref, wf_ref, same_ref, strips):
+def forward_weights_kernel(psf_ref, wf_ref, strips):
     def put(at, value):
         wf_ref[at : at + value.shape[0], :] = value
 
@@ -366,7 +366,7 @@
         copy.wait()
 
 
-def call(body, outs, scratch, n_in, flops=1_000_000_000, vmem=20, far_out=False, aliases=None):
+def call(body, outs, scratch, n_in, flops=1_000_000_000, vmem=20, far_out=False):
     whole = pl.BlockSpec(memory_space=pltpu.VMEM)
     distant = pl.BlockSpec(memory_space=pltpu.HBM)
     return pl.pallas_call(
@@ -375,7 +375,6 @@
         in_specs=[whole] * n_in,
         out_specs=[distant if far_out else whole] * len(outs),
         scratch_shapes=scratch,
-        input_output_aliases=aliases or {},
         compiler_params=pltpu.CompilerParams(vmem_limit_bytes=vmem * MIB),
         cost_estimate=pl.CostEstimate(flops=flops, bytes_accessed=4_000_000, transcendentals=0),
     )
@@ -404,14 +403,7 @@
         vmem=12,
     )(base(x, d, z), psf[0])
     strips = pltpu.VMEM((4, 64, 1536), BF)
-    wf, packed = call(
-        forward_weights_kernel,
-        [out((2560, 256), BF), out((66, 8, 256), BF)],
-        [strips],
-        1,
-        vmem=8,
-        aliases={0: 1},
-    )(packed)
+    (wf,) = call(forward_weights_kernel, [out((2560, 256), BF)], [strips], 1, vmem=8)(packed)
     prev_pack = lax.ppermute(packed, depth, later)
     next_pack = lax.ppermute(packed, depth, earlier)
     (part,) = call(

time: 84.7 us -> 84 us (level)
  waiting for transfers between devices: 11.7 us -> 10.8 us
  transfers between devices with their start and end apart: 10 -> 10, of which waited for: 5 -> 5; matrix products, arithmetic and copies ran while one was open for 0% -> 0% of each run, Pallas kernels for 10% -> 11%
where the time goes in v5:
time: 84 us; the launch traced here: 83.6 us
  starting transfers between devices  28.1 us (33%)
  blocking collectives  19.2 us (23%)
  Pallas kernels  18.6 us (22%)
  waiting for transfers between devices  10.8 us (13%)
  local copies, waits for them, and re-layouts  4.32 us (5%)
  other arithmetic  1.54 us (2%)
  between operations  1.1 us (1%)
    all_to_all x1, blocking collectives, shards(): got = lax.all_to_all(part, group, 0, 0, tiled=True)  19.2 us
    pallas_call x1, Pallas kernels, shards(): call(final_kernel, [out((64, 2048), F32)] * 3, [pltpu.VMEM((4, 80, 256),...  8.47 us
    ppermute x3, starting transfers between devices, shards(): lax.ppermute(mine, 'zh', [(a, a ^ bits) for a in range(4)])  5.74 us
    ppermute x1, starting transfers between devices, shards(): rim_lo = lax.ppermute(rim_down, 'band', down)  5 us
    ppermute x3, waiting for transfers between devices, shards(): lax.ppermute(mine, 'zh', [(a, a ^ bits) for a in range(4)])  4.74 us
    ppermute x1, starting transfers between devices, shards(): prev_pack = lax.ppermute(packed, depth, later)  4.39 us
    ppermute x1, starting transfers between devices, shards(): lo = lax.ppermute(x[48:64].astype(BF), 'band', down)  3.96 us
    all_to_all x1, starting transfers between devices, shards(): res = lax.all_to_all(wide, group, 0, 0, tiled=True)  3.53 us
  transfers between devices with their start and end apart: 10, of which 5 were waited for; matrix products, arithmetic and copies ran while one was open for 0% of the time, Pallas kernels for 11%

profile of v5, /device:TPU:1, one launch (start us, length us, event | category | flops | bytes accessed | tf_op | source)
XLA Modules:
  0.0 83.6 jit_solution(12682864001078144270)
XLA Ops:
  0.6 0.0 copy-start.6
  0.6 1.5 %subtract_add_fusion.start = f32[64,2048]{1,0:T(8,128)S(1)} fusion(f32[1,64,2048]{2,1,0:T(8,128)} %param.10, f32[1,64,2048]{2,1,0:T(8,128)} %param.9, f32[1,64,2048]{2,1,0:T(8,128)} %param.8), kind=kLoop, calls=%fused_computation.1 | loop fusion | flops 655360 | bytes 2097152 | tf_op jit(solution)/shard_map/add | solution.py:158
  2.1 0.0 copy-done.6
  2.1 0.0 copy-start.2
  2.1 0.6 shard_map.103
  2.7 0.0 copy-start.8
  2.8 4.4 %collective-permute-start.2 = (bf16[66,8,256]{2,1,0:T(8,128)(2,1)S(1)}, bf16[66,8,256]{2,1,0:T(8,128)(2,1)S(1)}, u32[]{:S(2)}, u32[]{:S(2)}) collective-permute-start(bf16[66,8,256]{2,1,0:T(8,128)(2,1)S(1)} %get-tuple-element.24.psf_ref.own_pack), channel_id=1, source_target_pairs={{0,4},{4,8},{8,12},{12,16},{16,20},{20,24},{24,28},{28,32},{32,36}... | collective-permute-start | bytes 811016 | tf_op jit(solution)/shard_map/ppermute | solution.py:407
  7.2 1.3 %collective-permute-start.3 = (bf16[66,8,256]{2,1,0:T(8,128)(2,1)S(1)}, bf16[66,8,256]{2,1,0:T(8,128)(2,1)S(1)}, u32[]{:S(2)}, u32[]{:S(2)}) collective-permute-start(bf16[66,8,256]{2,1,0:T(8,128)(2,1)S(1)} %get-tuple-element.24.psf_ref.own_pack), channel_id=1, source_target_pairs={{4,0},{8,4},{12,8},{16,12},{20,16},{24,20},{28,24},{32,28},{36,32}... | collective-permute-start | bytes 811016 | tf_op jit(solution)/shard_map/ppermute | solution.py:408
  8.5 0.0 copy-done.2
  8.5 4.0 %collective-permute-start = (bf16[16,2048]{1,0:T(8,128)(2,1)S(1)}, bf16[16,2048]{1,0:T(8,128)(2,1)S(1)}, u32[]{:S(2)}, u32[]{:S(2)}) collective-permute-start(bf16[16,2048]{1,0:T(8,128)(2,1)S(1)} %get-tuple-element.46), channel_id=1, source_target_pairs={{0,1},{1,2},{2,3},{4,5},{5,6},{6,7},{8,9},{9,10},{10,11},{12,13},{... | collective-permute-start | bytes 196616 | tf_op jit(solution)/shard_map/ppermute | solution.py:396
  12.5 0.0 copy-start.5
  12.5 2.1 %collective-permute-start.1 = (bf16[16,2048]{1,0:T(8,128)(2,1)S(1)}, bf16[16,2048]{1,0:T(8,128)(2,1)S(1)}, u32[]{:S(2)}, u32[]{:S(2)}) collective-permute-start(bf16[16,2048]{1,0:T(8,128)(2,1)S(1)} %get-tuple-element.45), channel_id=1, source_target_pairs={{1,0},{2,1},{3,2},{5,4},{6,5},{7,6},{9,8},{10,9},{11,10},{13,12},{... | collective-permute-start | bytes 196616 | tf_op jit(solution)/shard_map/ppermute | solution.py:397
  14.6 0.7 shard_map.104.wf
  15.3 0.0 collective-permute-done.lo
  15.3 2.9 %collective-permute-done.1.hi = bf16[16,2048]{1,0:T(8,128)(2,1)S(1)} collective-permute-done((bf16[16,2048]{1,0:T(8,128)(2,1)S(1)}, bf16[16,2048]{1,0:T(8,128)(2,1)S(1)}, u32[]{:S(2)}, u32[]{:S(2)}) %collective-permute-start.1) | collective-permute-done | bytes 65568 | tf_op jit(solution)/shard_map/ppermute | solution.py:397
  18.2 0.0 copy-done.8
  18.2 0.0 copy-done.5
  18.2 2.3 %shard_map.105 = bf16[512,256]{1,0:T(8,128)(2,1)S(1)} custom-call(f32[64,2048]{1,0:T(8,128)S(1)} %bitcast.18, f32[64,2048]{1,0:T(8,128)S(1)} %copy-done.5, bf16[16,2048]{1,0:T(8,128)(2,1)S(1)} %collective-permute-done.lo, bf16[16,2048]{1,0:T(8,128)(2,1)S(1)} %collective-permute-done.1.hi, bf16[2560,256]{1,0:T(8,128)(2,1)S(1)} %shard_map.104.wf, ...), custom_call_target="tpu_custom_call" | custom-call | flops 1000000000 | bytes 4000000 | tf_op jit(solution)/shard_map/pallas_call | solution.py:409
  20.6 0.0 copy-start.12
  20.6 0.0 copy-start.13
  20.6 0.0 collective-permute-done.2.prev_pack
  20.6 0.0 collective-permute-done.3.next_pack
  20.6 19.2 %all_to_all.17 = bf16[16,32,256]{2,1,0:T(8,128)(2,1)S(1)} all-to-all(bf16[16,32,256]{2,1,0:T(8,128)(2,1)S(1)} %bitcast.24), channel_id=1, replica_groups=mesh['xh'=2,'y'=4,'zh'=4,'zl'=2,'band'=4] {'xh','y','zl'}, dimensions={0} | all-to-all | bytes 524288 | tf_op jit(solution)/shard_map/all_to_all | solution.py:421
  39.8 3.7 %collective-permute-start.4 = (f32[32,256]{1,0:T(8,128)S(1)}, f32[32,256]{1,0:T(8,128)S(1)}, u32[]{:S(2)}, u32[]{:S(2)}) collective-permute-start(f32[32,256]{1,0:T(8,128)S(1)} %convert_reduce_fusion), channel_id=1, source_target_pairs={{0,16},{8,24},{16,0},{24,8},{1,17},{9,25},{17,1},{25,9},{2,18},{10... | collective-permute-start | bytes 98312 | tf_op jit(solution)/shard_map/ppermute | solution.py:423
  43.5 1.0 %collective-permute-start.5 = (f32[32,256]{1,0:T(8,128)S(1)}, f32[32,256]{1,0:T(8,128)S(1)}, u32[]{:S(2)}, u32[]{:S(2)}) collective-permute-start(f32[32,256]{1,0:T(8,128)S(1)} %convert_reduce_fusion), channel_id=1, source_target_pairs={{0,8},{8,0},{16,24},{24,16},{1,9},{9,1},{17,25},{25,17},{2,10},{10... | collective-permute-start | bytes 98312 | tf_op jit(solution)/shard_map/ppermute | solution.py:423
  44.5 1.1 %collective-permute-start.6 = (f32[32,256]{1,0:T(8,128)S(1)}, f32[32,256]{1,0:T(8,128)S(1)}, u32[]{:S(2)}, u32[]{:S(2)}) collective-permute-start(f32[32,256]{1,0:T(8,128)S(1)} %convert_reduce_fusion), channel_id=1, source_target_pairs={{0,24},{8,16},{16,8},{24,0},{1,25},{9,17},{17,9},{25,1},{2,26},{10... | collective-permute-start | bytes 98312 | tf_op jit(solution)/shard_map/ppermute | solution.py:423
  45.6 1.0 %collective-permute-done.4 = f32[32,256]{1,0:T(8,128)S(1)} collective-permute-done((f32[32,256]{1,0:T(8,128)S(1)}, f32[32,256]{1,0:T(8,128)S(1)}, u32[]{:S(2)}, u32[]{:S(2)}) %collective-permute-start.4) | collective-permute-done | bytes 32800 | tf_op jit(solution)/shard_map/ppermute | solution.py:423
  46.6 2.8 %collective-permute-done.5 = f32[32,256]{1,0:T(8,128)S(1)} collective-permute-done((f32[32,256]{1,0:T(8,128)S(1)}, f32[32,256]{1,0:T(8,128)S(1)}, u32[]{:S(2)}, u32[]{:S(2)}) %collective-permute-start.5) | collective-permute-done | bytes 32800 | tf_op jit(solution)/shard_map/ppermute | solution.py:423
  49.4 1.0 %collective-permute-done.6 = f32[32,256]{1,0:T(8,128)S(1)} collective-permute-done((f32[32,256]{1,0:T(8,128)S(1)}, f32[32,256]{1,0:T(8,128)S(1)}, u32[]{:S(2)}, u32[]{:S(2)}) %collective-permute-start.6) | collective-permute-done | bytes 32800 | tf_op jit(solution)/shard_map/ppermute | solution.py:423
  50.3 0.7 broadcast_in_dim.15
  51.1 3.5 %all-to-all-start.1 = ((bf16[16,32,256]{2,1,0:T(8,128)(2,1)}), bf16[16,32,256]{2,1,0:T(8,128)(2,1)S(1)}, u32[]{:S(2)}, u32[]{:S(2)}) async-start(bf16[16,32,256]{2,1,0:T(8,128)(2,1)} %broadcast_in_dim.15), calls=%async_computation.1 | async-start | bytes 524288 | tf_op jit(solution)/shard_map/all_to_all | solution.py:440
  54.6 0.0 copy-done.12
  54.6 0.1 copy.11.kernel_ref
  54.7 0.0 copy-done.13
  54.7 0.1 copy.12.mix_ref
  54.8 0.0 copy-start.7
  54.8 1.9 %shard_map.106 = (bf16[2560,768]{1,0:T(8,128)(2,1)S(1)}, f32[512,768]{1,0:T(8,128)S(1)}, bf16[128,256]{1,0:T(8,128)(2,1)S(1)}, bf16[128,256]{1,0:T(8,128)(2,1)S(1)}) custom-call(bf16[66,8,256]{2,1,0:T(8,128)(2,1)S(1)} %collective-permute-done.2.prev_pack, bf16[66,8,256]{2,1,0:T(8,128)(2,1)S(1)} %get-tuple-element.24.psf_ref.own_pack, ...), custom_call_target="tpu_custom_call" | custom-call | flops 1000000000 | bytes 4000000 | tf_op jit(solution)/shard_map/pallas_call | solution.py:424
  56.7 0.0 copy-start
  56.7 1.9 %copy-done = bf16[2560,768]{1,0:T(8,128)(2,1)} copy-done((bf16[2560,768]{1,0:T(8,128)(2,1)}, bf16[2560,768]{1,0:T(8,128)(2,1)S(1)}, u32[]{:S(2)}) %copy-start) | copy-done | bytes 3932184
  58.6 0.0 copy-start.10
  58.6 0.6 copy-done.10
  59.2 3.1 %all-to-all-done.1 = bf16[16,32,256]{2,1,0:T(8,128)(2,1)S(1)} async-done(((bf16[16,32,256]{2,1,0:T(8,128)(2,1)}), bf16[16,32,256]{2,1,0:T(8,128)(2,1)S(1)}, u32[]{:S(2)}, u32[]{:S(2)}) %all-to-all-start.1) | async-done | bytes 262176 | tf_op jit(solution)/shard_map/all_to_all | solution.py:440
  62.3 0.0 copy-start.11
  62.3 0.8 %copy-done.11 = bf16[128,256]{1,0:T(8,128)(2,1)S(1)} copy-done((bf16[128,256]{1,0:T(8,128)(2,1)S(1)}, bf16[128,256]{1,0:T(8,128)(2,1)}, u32[]{:S(2)}) %copy-start.11) | copy-done | bytes 65560
  63.1 0.0 copy-start.1
  63.1 0.4 shard_map.108
  63.5 5.0 %collective-permute-start.7 = (bf16[256,256]{1,0:T(8,128)(2,1)S(1)}, bf16[256,256]{1,0:T(8,128)(2,1)S(1)}, u32[]{:S(2)}, u32[]{:S(2)}) collective-permute-start(bf16[256,256]{1,0:T(8,128)(2,1)S(1)} %get-tuple-element.37), channel_id=1, source_target_pairs={{0,1},{1,2},{2,3},{4,5},{5,6},{6,7},{8,9},{9,10},{10,11},{12,13},{... | collective-permute-start | bytes 393224 | tf_op jit(solution)/shard_map/ppermute | solution.py:444
  68.5 2.1 %collective-permute-start.8 = (bf16[256,256]{1,0:T(8,128)(2,1)S(1)}, bf16[256,256]{1,0:T(8,128)(2,1)S(1)}, u32[]{:S(2)}, u32[]{:S(2)}) collective-permute-start(bf16[256,256]{1,0:T(8,128)(2,1)S(1)} %get-tuple-element.38), channel_id=1, source_target_pairs={{1,0},{2,1},{3,2},{5,4},{6,5},{7,6},{9,8},{10,9},{11,10},{13,12},{... | collective-permute-start | bytes 393224 | tf_op jit(solution)/shard_map/ppermute | solution.py:445
  70.6 0.0 copy-done.7
  70.7 1.3 %shard_map.109 = (bf16[512,1024]{1,0:T(8,128)(2,1)S(1)}, bf16[512,1024]{1,0:T(8,128)(2,1)S(1)}, bf16[2048,128]{1,0:T(8,128)(2,1)S(1)}) custom-call(bf16[27,16]{1,0:T(8,128)(2,1)S(1)} %copy.11.kernel_ref, f32[1,16]{1,0:T(1,128)S(1)} %bitcast.26, bf16[16,1]{1,0:T(8,128)(2,1)S(1)} %copy.12.mix_ref), custom_call_target="tpu_custom_call" | custom-call | flops 1000000000 | bytes 4000000 | tf_op jit(solution)/shard_map/pallas_call | solution.py:431
  72.0 0.0 copy-done.1
  72.0 0.0 copy-start.3
  72.0 0.0 copy-start.4
  72.0 0.0 copy-start.9
  72.0 2.8 %shard_map.107 = (f32[512,768]{1,0:T(8,128)S(1)}, f32[64,8,256]{2,1,0:T(8,128)S(1)}, f32[2,64,384]{2,1,0:T(8,128)S(1)}) custom-call(bf16[512,256]{1,0:T(8,128)(2,1)S(1)} %bitcast.21, bf16[2560,768]{1,0:T(8,128)(2,1)S(1)} %copy-done.1, f32[512,768]{1,0:T(8,128)S(1)} %get-tuple-element.31.starts), custom_call_target="tpu_custom_call" | custom-call | flops 1000000000 | bytes 4000000 | tf_op jit(solution)/shard_map/pallas_call | solution.py:446
  74.9 0.0 collective-permute-done.7.lo
  74.9 0.0 collective-permute-done.8.hi
  74.9 0.0 copy-done.3
  74.9 0.0 copy-done.4
  74.9 0.0 copy-done.9
  74.9 8.5 %shard_map.110 = (f32[64,2048]{1,0:T(8,128)}, f32[64,2048]{1,0:T(8,128)}, f32[64,2048]{1,0:T(8,128)}) custom-call(f32[64,2048]{1,0:T(8,128)S(1)} %bitcast.19, f32[64,2048]{1,0:T(8,128)S(1)} %bitcast.22, f32[64,2048]{1,0:T(8,128)S(1)} %bitcast.23, f32[512,768]{1,0:T(8,128)S(1)} %get-tuple-element.32.noisy, f32[64,8,256]{2,1,0:T(8,128)S(1)} %get-tuple-element.33.moves, ...), custom_call_target="tpu_custom_call" | custom-call | flops 10000000000 | bytes 4000000 | tf_op jit(solution)/shard_map/pallas_call | solution.py:453
  (4 shorter events, 0.1 us)
Async XLA Ops:
  0.6 1.5 %copy-start.6 = (bf16[1,31,31]{2,1,0:T(8,128)(2,1)S(1)}, bf16[1,31,31]{2,1,0:T(8,128)(2,1)}, u32[]{:S(2)}) copy-start(bf16[1,31,31]{2,1,0:T(8,128)(2,1)} %param.12) | copy-start | bytes 5770
  2.1 6.3 %copy-start.2 = (f32[1,64,2048]{2,1,0:T(8,128)S(1)}, f32[1,64,2048]{2,1,0:T(8,128)}, u32[]{:S(2)}) copy-start(f32[1,64,2048]{2,1,0:T(8,128)} %param.8) | copy-start | bytes 1572868
  2.7 15.5 %copy-start.8 = (bf16[512,512]{1,0:T(8,128)(2,1)}, bf16[512,512]{1,0:T(8,128)(2,1)S(1)}, u32[]{:S(2)}) copy-start(bf16[512,512]{1,0:T(8,128)(2,1)S(1)} %get-tuple-element.25.swap) | copy-start | bytes 1572868
  2.8 17.8 %collective-permute-start.2 = (bf16[66,8,256]{2,1,0:T(8,128)(2,1)S(1)}, bf16[66,8,256]{2,1,0:T(8,128)(2,1)S(1)}, u32[]{:S(2)}, u32[]{:S(2)}) collective-permute-start(bf16[66,8,256]{2,1,0:T(8,128)(2,1)S(1)} %get-tuple-element.24.psf_ref.own_pack), channel_id=1, source_target_pairs={{0,4},{4,8},{8,12},{12,16},{16,20},{20,24},{24,28},{28,32},{32,36}... | collective-permute-start | bytes 811016 | tf_op jit(solution)/shard_map/ppermute | solution.py:407
  7.2 13.4 %collective-permute-start.3 = (bf16[66,8,256]{2,1,0:T(8,128)(2,1)S(1)}, bf16[66,8,256]{2,1,0:T(8,128)(2,1)S(1)}, u32[]{:S(2)}, u32[]{:S(2)}) collective-permute-start(bf16[66,8,256]{2,1,0:T(8,128)(2,1)S(1)} %get-tuple-element.24.psf_ref.own_pack), channel_id=1, source_target_pairs={{4,0},{8,4},{12,8},{16,12},{20,16},{24,20},{28,24},{32,28},{36,32}... | collective-permute-start | bytes 811016 | tf_op jit(solution)/shard_map/ppermute | solution.py:408
  8.5 6.7 %collective-permute-start = (bf16[16,2048]{1,0:T(8,128)(2,1)S(1)}, bf16[16,2048]{1,0:T(8,128)(2,1)S(1)}, u32[]{:S(2)}, u32[]{:S(2)}) collective-permute-start(bf16[16,2048]{1,0:T(8,128)(2,1)S(1)} %get-tuple-element.46), channel_id=1, source_target_pairs={{0,1},{1,2},{2,3},{4,5},{5,6},{6,7},{8,9},{9,10},{10,11},{12,13},{... | collective-permute-start | bytes 196616 | tf_op jit(solution)/shard_map/ppermute | solution.py:396
  12.5 5.7 %copy-start.5 = (f32[64,2048]{1,0:T(8,128)S(1)}, f32[64,2048]{1,0:T(8,128)}, u32[]{:S(2)}) copy-start(f32[64,2048]{1,0:T(8,128)} %measured.1) | copy-start | bytes 1572868
  12.5 5.7 %collective-permute-start.1 = (bf16[16,2048]{1,0:T(8,128)(2,1)S(1)}, bf16[16,2048]{1,0:T(8,128)(2,1)S(1)}, u32[]{:S(2)}, u32[]{:S(2)}) collective-permute-start(bf16[16,2048]{1,0:T(8,128)(2,1)S(1)} %get-tuple-element.45), channel_id=1, source_target_pairs={{1,0},{2,1},{3,2},{5,4},{6,5},{7,6},{9,8},{10,9},{11,10},{13,12},{... | collective-permute-start | bytes 196616 | tf_op jit(solution)/shard_map/ppermute | solution.py:397
  20.6 34.0 %copy-start.12 = (bf16[27,16]{0,1:T(8,128)(2,1)S(1)}, bf16[27,16]{0,1:T(8,128)(2,1)}, u32[]{:S(2)}) copy-start(bf16[27,16]{0,1:T(8,128)(2,1)} %param.13) | copy-start | bytes 2596
  20.6 34.1 %copy-start.13 = (bf16[16]{0:T(256)(128)(2,1)S(1)}, bf16[16]{0:T(256)(128)(2,1)}, u32[]{:S(2)}) copy-start(bf16[16]{0:T(256)(128)(2,1)} %param.15) | copy-start | bytes 100
  39.8 6.8 %collective-permute-start.4 = (f32[32,256]{1,0:T(8,128)S(1)}, f32[32,256]{1,0:T(8,128)S(1)}, u32[]{:S(2)}, u32[]{:S(2)}) collective-permute-start(f32[32,256]{1,0:T(8,128)S(1)} %convert_reduce_fusion), channel_id=1, source_target_pairs={{0,16},{8,24},{16,0},{24,8},{1,17},{9,25},{17,1},{25,9},{2,18},{10... | collective-permute-start | bytes 98312 | tf_op jit(solution)/shard_map/ppermute | solution.py:423
  43.5 5.8 %collective-permute-start.5 = (f32[32,256]{1,0:T(8,128)S(1)}, f32[32,256]{1,0:T(8,128)S(1)}, u32[]{:S(2)}, u32[]{:S(2)}) collective-permute-start(f32[32,256]{1,0:T(8,128)S(1)} %convert_reduce_fusion), channel_id=1, source_target_pairs={{0,8},{8,0},{16,24},{24,16},{1,9},{9,1},{17,25},{25,17},{2,10},{10... | collective-permute-start | bytes 98312 | tf_op jit(solution)/shard_map/ppermute | solution.py:423
  44.5 5.8 %collective-permute-start.6 = (f32[32,256]{1,0:T(8,128)S(1)}, f32[32,256]{1,0:T(8,128)S(1)}, u32[]{:S(2)}, u32[]{:S(2)}) collective-permute-start(f32[32,256]{1,0:T(8,128)S(1)} %convert_reduce_fusion), channel_id=1, source_target_pairs={{0,24},{8,16},{16,8},{24,0},{1,25},{9,17},{17,9},{25,1},{2,26},{10... | collective-permute-start | bytes 98312 | tf_op jit(solution)/shard_map/ppermute | solution.py:423
  51.1 11.2 %all-to-all-start.1 = ((bf16[16,32,256]{2,1,0:T(8,128)(2,1)}), bf16[16,32,256]{2,1,0:T(8,128)(2,1)S(1)}, u32[]{:S(2)}, u32[]{:S(2)}) async-start(bf16[16,32,256]{2,1,0:T(8,128)(2,1)} %broadcast_in_dim.15), calls=%async_computation.1 | async-start | bytes 524288 | tf_op jit(solution)/shard_map/all_to_all | solution.py:440
  54.8 15.8 %copy-start.7 = (f32[16]{0:T(128)S(1)}, f32[16]{0:T(128)}, u32[]{:S(2)}) copy-start(f32[16]{0:T(128)} %param.14) | copy-start | bytes 196
  56.7 1.9 %copy-start = (bf16[2560,768]{1,0:T(8,128)(2,1)}, bf16[2560,768]{1,0:T(8,128)(2,1)S(1)}, u32[]{:S(2)}) copy-start(bf16[2560,768]{1,0:T(8,128)(2,1)S(1)} %get-tuple-element.30.wg) | copy-start | bytes 11796484
  58.6 0.6 copy-start.10
  62.3 0.8 %copy-start.11 = (bf16[128,256]{1,0:T(8,128)(2,1)S(1)}, bf16[128,256]{1,0:T(8,128)(2,1)}, u32[]{:S(2)}) copy-start(bf16[128,256]{1,0:T(8,128)(2,1)} %copy-done.10) | copy-start | bytes 196612
  63.1 8.8 %copy-start.1 = (bf16[2560,768]{1,0:T(8,128)(2,1)S(1)}, bf16[2560,768]{1,0:T(8,128)(2,1)}, u32[]{:S(2)}) copy-start(bf16[2560,768]{1,0:T(8,128)(2,1)} %copy-done) | copy-start | bytes 11796484
  63.5 11.4 %collective-permute-start.7 = (bf16[256,256]{1,0:T(8,128)(2,1)S(1)}, bf16[256,256]{1,0:T(8,128)(2,1)S(1)}, u32[]{:S(2)}, u32[]{:S(2)}) collective-permute-start(bf16[256,256]{1,0:T(8,128)(2,1)S(1)} %get-tuple-element.37), channel_id=1, source_target_pairs={{0,1},{1,2},{2,3},{4,5},{5,6},{6,7},{8,9},{9,10},{10,11},{12,13},{... | collective-permute-start | bytes 393224 | tf_op jit(solution)/shard_map/ppermute | solution.py:444
  68.5 6.4 %collective-permute-start.8 = (bf16[256,256]{1,0:T(8,128)(2,1)S(1)}, bf16[256,256]{1,0:T(8,128)(2,1)S(1)}, u32[]{:S(2)}, u32[]{:S(2)}) collective-permute-start(bf16[256,256]{1,0:T(8,128)(2,1)S(1)} %get-tuple-element.38), channel_id=1, source_target_pairs={{1,0},{2,1},{3,2},{5,4},{6,5},{7,6},{9,8},{10,9},{11,10},{13,12},{... | collective-permute-start | bytes 393224 | tf_op jit(solution)/shard_map/ppermute | solution.py:445
  72.0 2.9 %copy-start.3 = (f32[1,64,2048]{2,1,0:T(8,128)S(1)}, f32[1,64,2048]{2,1,0:T(8,128)}, u32[]{:S(2)}) copy-start(f32[1,64,2048]{2,1,0:T(8,128)} %param.9) | copy-start | bytes 1572868
  72.0 2.9 %copy-start.4 = (f32[1,64,2048]{2,1,0:T(8,128)S(1)}, f32[1,64,2048]{2,1,0:T(8,128)}, u32[]{:S(2)}) copy-start(f32[1,64,2048]{2,1,0:T(8,128)} %param.10) | copy-start | bytes 1572868
  72.0 2.9 %copy-start.9 = (bf16[512,512]{1,0:T(8,128)(2,1)S(1)}, bf16[512,512]{1,0:T(8,128)(2,1)}, u32[]{:S(2)}) copy-start(bf16[512,512]{1,0:T(8,128)(2,1)} %copy-done.8) | copy-start | bytes 1572868
